TPU v7x, 32 devices: a whole 2x2x4 slice. The times are simulated.
32 devices in a mesh: dp: 4 (over z), fsdp: 8 (over y, x, core).
Axes of the slice: x: 2, y: 2, z: 4, core: 2. Of those that a mesh axis runs over, the one named last changes fastest.
Arguments:
- layer_input: bfloat16 [32, 472, 768], P(('dp', 'fsdp')), may hold values from -6 to 6
- mask_index: int32 [32, 232], P(('dp', 'fsdp')), may hold values from 0 to 471, as said below
- distract: int32 [32, 232, 100], P(('dp', 'fsdp')), may hold values from 0 to 231, as said below
- code_choice: int32 [32, 232, 2], P(('dp', 'fsdp')), may hold values from 0 to 319
- params: float32 [7421952], P(('dp', 'fsdp')), may hold values from -4 to 4
- moment_one: float32 [7421952], P(('dp', 'fsdp')), may hold values from -5.9604645e-07 to 5.9604645e-07
- moment_two: float32 [7421952], P(('dp', 'fsdp')), may hold values from 2.748603e-15 to 1.0994412e-14
- vectors: float32 [9728], replicated, may hold values from -1 to 3
- vector_one: float32 [9728], replicated, may hold values from -2.3841858e-06 to 2.3841858e-06
- vector_two: float32 [9728], replicated, may hold values from 4.3923754e-14 to 1.7515607e-13
Outputs:
- total_loss: float32 [], replicated
- grad_norm: float32 [], replicated
- layer_output: bfloat16 [32, 472, 768], P(('dp', 'fsdp'))
- input_grad: float32 [32, 472, 768], P(('dp', 'fsdp'))
- refreshed_weights: float32 [7421952], P(('dp', 'fsdp'))
- params_bfloat_copy: bfloat16 [7421952], P(('dp', 'fsdp'))
- new_moment_one: float32 [7421952], P(('dp', 'fsdp'))
- new_moment_two: float32 [7421952], P(('dp', 'fsdp'))
- new_vectors: float32 [9728], replicated
- new_vector_one: float32 [9728], replicated
- new_vector_two: float32 [9728], replicated
Inputs may be any that keep to these rules, and one draw needn't show every extreme that they name: `mask_index`: each utterance's 232 positions are distinct and increasing. `distract`: for each masked frame, 100 distinct indices of other masked frames of the same utterance, never its own.
All inputs are finite; a program needn't handle non-finite values.
Results may differ from a plain program's by a relative error of at most 0.014.
The roundings to bfloat16 on the way count: a program that leaves them out, or rounds other values in their place, can miss the bound.
Values may be sent and summed in bfloat16 or wider, within the bound.
A program may use at most 192 MiB of HBM per device.

v0:
```python
from functools import partial

import jax
import jax.numpy as jnp
from jax import lax
from jax.sharding import PartitionSpec as P

D = 768
H = 12
HD = 64
FF = 3072
FINAL = 256
G = 2
V = 320
CD = 128
LEN = 472
MASKED = 232
STEP = 10


eps_norm = 1e-05
eps_cos = 1e-06
softness_divisor = 0.1
beta_one = 0.9
beta_two = 0.98
adam_eps = 1e-08
decay_rate = 0.01
rate_matrix = 0.03
rate_vector = 0.2
clip_level = 0.001


def unpack(flat_values):
    shapes = [(D, 3 * D), (D, D), (D, FF), (FF, D), (D, FINAL), (G * CD, V), (G * CD, FINAL)]
    pieces = []
    offset = 0
    for height, width in shapes:
        pieces.append(flat_values[offset : offset + height * width].reshape(height, width))
        offset = offset + height * width
    return pieces


def split_vectors(vector_all):
    lengths = [D, D, D, D, D, FF, D, D, D, FINAL, FINAL]
    pieces = []
    offset = 0
    for length in lengths:
        pieces.append(vector_all[offset : offset + length])
        offset = offset + length
    return pieces


def layer_norm(values, scale_gain, shift_bias):
    centered = values - jnp.mean(values, axis=-1, keepdims=True)
    variance = jnp.mean(centered * centered, axis=-1, keepdims=True)
    return centered * lax.rsqrt(variance + eps_norm) * scale_gain + shift_bias


def pick_rows(source, index_rows):
    return source[index_rows]


def place_rows(template, index_rows, values):
    return template.at[index_rows].set(values)


def contrast_loss(chosen, targets, distract):
    encoder_unit_heading = chosen * lax.rsqrt(
        jnp.sum(chosen * chosen, axis=-1, keepdims=True) + eps_cos
    )
    quantized_unit_heading = targets * lax.rsqrt(
        jnp.sum(targets * targets, axis=-1, keepdims=True) + eps_cos
    )
    angular_agreement = (
        jnp.einsum(
            "rby,roy->rbo",
            encoder_unit_heading,
            quantized_unit_heading,
            precision=lax.Precision.HIGHEST,
        )
        / softness_divisor
    )
    positive = jnp.diagonal(angular_agreement, axis1=1, axis2=2)
    negative = jnp.take_along_axis(angular_agreement, distract, axis=2)
    logits_all = jnp.concatenate([positive[..., None], negative], axis=-1)
    return jnp.sum(jax.nn.logsumexp(logits_all, axis=-1) - positive)


def adamw_update(master, first_moment, second, gradient, step_rate):
    first_new = beta_one * first_moment + (1.0 - beta_one) * gradient
    second_new = beta_two * second + (1.0 - beta_two) * gradient * gradient
    first_hat = first_new / (1.0 - beta_one**STEP)
    second_hat = second_new / (1.0 - beta_two**STEP)
    master_new = master * (1.0 - step_rate * decay_rate) - step_rate * first_hat / (
        jnp.sqrt(second_hat) + adam_eps
    )
    return (master_new, first_new, second_new)


def column_sum(values):
    return jnp.sum(values.astype(jnp.float32), axis=tuple(range(values.ndim - 1)))


def on_device(
    layer_input,
    mask_index,
    distract,
    code_choice,
    params,
    moment_one,
    moment_two,
    vectors,
    vector_one,
    vector_two,
):
    bf16 = jnp.bfloat16
    f32 = jnp.float32
    count_utts = layer_input.shape[0]
    total_masked = count_utts * lax.axis_size(("dp", "fsdp")) * MASKED
    token_rows = count_utts * LEN
    shard_low = params.astype(bf16)
    gathered = lax.all_gather(shard_low, ("dp", "fsdp"), axis=0, tiled=True)
    qkv_weight, out_weight, up_weight, down_weight, proj_weight, codebook, code_weight = unpack(
        gathered
    )
    (
        bias_query,
        bias_value,
        bias_out,
        gain_one,
        shift_one,
        bias_up,
        bias_down,
        gain_two,
        shift_two,
        bias_proj,
        bias_code,
    ) = split_vectors(vectors)
    inputs = layer_input.reshape(token_rows, D)
    projected = jnp.dot(inputs, qkv_weight, preferred_element_type=f32)
    query_heads = (projected[:, :D] + bias_query).astype(bf16).reshape(count_utts, LEN, H, HD)
    key_heads = projected[:, D : 2 * D].astype(bf16).reshape(count_utts, LEN, H, HD)
    value_heads = (projected[:, 2 * D :] + bias_value).astype(bf16).reshape(count_utts, LEN, H, HD)
    scores = (
        jnp.einsum("blhe,bmhe->bhlm", query_heads, key_heads, preferred_element_type=f32) * 0.125
    )
    attn_probs = jax.nn.softmax(scores, axis=-1)
    probs_low = attn_probs.astype(bf16)
    attended = jnp.einsum("bhlm,bmhe->blhe", probs_low, value_heads, preferred_element_type=f32)
    attended = attended.astype(bf16).reshape(token_rows, D)
    residual_one = (
        inputs.astype(f32) + jnp.dot(attended, out_weight, preferred_element_type=f32) + bias_out
    )
    normed, back_one = jax.vjp(layer_norm, residual_one, gain_one, shift_one)
    normed_low = normed.astype(bf16)
    hidden = jnp.dot(normed_low, up_weight, preferred_element_type=f32) + bias_up
    active, gelu_back = jax.vjp(partial(jax.nn.gelu, approximate=False), hidden)
    active_low = active.astype(bf16)
    residual_two = normed + jnp.dot(active_low, down_weight, preferred_element_type=f32) + bias_down
    output, back_two = jax.vjp(layer_norm, residual_two, gain_two, shift_two)
    output_low = output.astype(bf16)
    context = jnp.dot(output_low, proj_weight, preferred_element_type=f32) + bias_proj
    choose = (code_choice[..., None] == jnp.arange(V, dtype=jnp.int32)).astype(bf16)
    code_vectors = jnp.einsum(
        "bmgv,gcv->bmgc", choose, codebook.reshape(G, CD, V), preferred_element_type=f32
    )
    code_vectors = code_vectors.astype(bf16).reshape(count_utts, MASKED, G * CD)
    targets = (
        jnp.einsum("bmc,cf->bmf", code_vectors, code_weight, preferred_element_type=f32) + bias_code
    )
    chosen = jax.vmap(pick_rows)(context.reshape(count_utts, LEN, FINAL), mask_index)
    loss_local, contrast_back = jax.vjp(partial(contrast_loss, distract=distract), chosen, targets)
    qkv_weight, out_weight, up_weight, down_weight, proj_weight, codebook, code_weight = unpack(
        lax.all_gather(shard_low, ("dp", "fsdp"), axis=0, tiled=True)
    )
    d_selected_code, d_targets = contrast_back(jnp.asarray(1.0 / total_masked, f32))
    d_targets_low = d_targets.astype(bf16)
    quantized_offset_slope = column_sum(d_targets_low)
    d_code_weight = jnp.einsum(
        "bmc,bmf->cf", code_vectors, d_targets_low, preferred_element_type=f32
    )
    d_code_vectors = jnp.einsum(
        "bmf,cf->bmc", d_targets_low, code_weight, preferred_element_type=f32
    )
    d_codebook = jnp.einsum(
        "bmgc,bmgv->gcv",
        d_code_vectors.reshape(count_utts, MASKED, G, CD),
        choose.astype(f32),
        precision=lax.Precision.HIGHEST,
    ).reshape(G * CD, V)
    d_context = jax.vmap(place_rows)(
        jnp.zeros((count_utts, LEN, FINAL), f32), mask_index, d_selected_code
    )
    d_context_low = d_context.reshape(token_rows, FINAL).astype(bf16)
    d_bias_proj = column_sum(d_context_low)
    d_proj_weight = jnp.einsum("td,tf->df", output_low, d_context_low, preferred_element_type=f32)
    result_sensitivity = jnp.einsum(
        "tf,df->td", d_context_low, proj_weight, preferred_element_type=f32
    )
    d_residual_two, d_gain_two, d_shift_two = back_two(result_sensitivity)
    d_second_low = d_residual_two.astype(bf16)
    d_bias_down = column_sum(d_second_low)
    d_down_weight = jnp.einsum("th,td->hd", active_low, d_second_low, preferred_element_type=f32)
    d_active = jnp.einsum("td,hd->th", d_second_low, down_weight, preferred_element_type=f32)
    (d_hidden,) = gelu_back(d_active)
    d_hidden_low = d_hidden.astype(bf16)
    d_bias_up = column_sum(d_hidden_low)
    d_up_weight = jnp.einsum("td,th->dh", normed_low, d_hidden_low, preferred_element_type=f32)
    d_normed = d_residual_two + jnp.einsum(
        "th,dh->td", d_hidden_low, up_weight, preferred_element_type=f32
    )
    d_residual_one, d_gain_one, d_shift_one = back_one(d_normed)
    d_branch_low = d_residual_one.astype(bf16)
    d_bias_out = column_sum(d_branch_low)
    d_out_weight = jnp.einsum("td,te->de", attended, d_branch_low, preferred_element_type=f32)
    d_attended = jnp.einsum("te,de->td", d_branch_low, out_weight, preferred_element_type=f32)
    d_attended = d_attended.astype(bf16).reshape(count_utts, LEN, H, HD)
    d_value = jnp.einsum("bhlm,blhe->bmhe", probs_low, d_attended, preferred_element_type=f32)
    d_probs = jnp.einsum("blhe,bmhe->bhlm", d_attended, value_heads, preferred_element_type=f32)
    d_scores = (
        attn_probs * (d_probs - jnp.sum(attn_probs * d_probs, axis=-1, keepdims=True))
    ).astype(bf16)
    d_query = jnp.einsum("bhlm,bmhe->blhe", d_scores, key_heads, preferred_element_type=f32) * 0.125
    d_key = jnp.einsum("bhlm,blhe->bmhe", d_scores, query_heads, preferred_element_type=f32) * 0.125
    d_projected = jnp.concatenate(
        [
            d_query.reshape(token_rows, D),
            d_key.reshape(token_rows, D),
            d_value.reshape(token_rows, D),
        ],
        axis=1,
    ).astype(bf16)
    d_sums = column_sum(d_projected)
    d_qkv_weight = jnp.einsum("td,te->de", inputs, d_projected, preferred_element_type=f32)
    input_grad = d_residual_one + jnp.einsum(
        "te,de->td", d_projected, qkv_weight, preferred_element_type=f32
    )
    flat_grad = jnp.concatenate(
        [
            matrix_grad.reshape(-1)
            for matrix_grad in (
                d_qkv_weight,
                d_out_weight,
                d_up_weight,
                d_down_weight,
                d_proj_weight,
                d_codebook,
                d_code_weight,
            )
        ]
    )
    vector_gradient = jnp.concatenate(
        [
            d_sums[:D],
            d_sums[2 * D :],
            d_bias_out,
            d_gain_one,
            d_shift_one,
            d_bias_up,
            d_bias_down,
            d_gain_two,
            d_shift_two,
            d_bias_proj,
            quantized_offset_slope,
        ]
    )
    vector_sum, loss_sum = lax.psum((vector_gradient, loss_local), ("dp", "fsdp"))
    owner_rows = params.shape[0]
    grad_shard = lax.psum_scatter(
        lax.slice_in_dim(flat_grad, 0, lax.axis_size(("dp", "fsdp")) * owner_rows, axis=0),
        ("dp", "fsdp"),
        scatter_dimension=0,
        tiled=True,
    )
    local_squares = jnp.sum(grad_shard * grad_shard)
    square_sum = lax.psum(local_squares, ("dp", "fsdp"))
    grad_norm = jnp.sqrt(square_sum + jnp.sum(vector_sum * vector_sum))
    factor = jnp.minimum(1.0, clip_level / (grad_norm + 1e-06))
    refreshed_weights, new_one, new_two = adamw_update(
        params, moment_one, moment_two, grad_shard * factor, rate_matrix
    )
    new_vectors, new_vector_first, new_vector_second = adamw_update(
        vectors, vector_one, vector_two, vector_sum * factor, rate_vector
    )
    total_loss = loss_sum / total_masked
    return (
        total_loss,
        grad_norm,
        output_low.reshape(count_utts, LEN, D),
        input_grad.reshape(count_utts, LEN, D),
        refreshed_weights,
        refreshed_weights.astype(bf16),
        new_one,
        new_two,
        new_vectors,
        new_vector_first,
        new_vector_second,
    )


def solution(mesh):
    in_specs = (
        P(("dp", "fsdp"), None, None),
        P(("dp", "fsdp"), None),
        P(("dp", "fsdp"), None, None),
        P(("dp", "fsdp"), None, None),
        P(("dp", "fsdp")),
        P(("dp", "fsdp")),
        P(("dp", "fsdp")),
        P(),
        P(),
        P(),
    )
    out_specs = (
        P(),
        P(),
        P(("dp", "fsdp"), None, None),
        P(("dp", "fsdp"), None, None),
        P(("dp", "fsdp")),
        P(("dp", "fsdp")),
        P(("dp", "fsdp")),
        P(("dp", "fsdp")),
        P(),
        P(),
        P(),
    )
    return jax.shard_map(
        on_device, mesh=mesh, in_specs=in_specs, out_specs=out_specs, check_vma=False
    )
```

profile of v0, /device:TPU:0, one launch (start us, length us, event | category | flops | bytes accessed | tf_op | source)
XLA Modules:
  0.0 1590.5 jit_solution(10912107443730524070)
XLA Ops:
  8.5 6.1 reshape.745
  20.0 173.8 %all-gather.3.cloned.1.call-done = bf16[32,1,231936]{2,1,0:T(2,128)(2,1)} async-done(((bf16[1,1,231936]{2,1,0:T(2,128)(2,1)}), bf16[32,1,231936]{2,1,0:T(2,128)(2,1)}) %all-gather.3.cloned.1.call-update) | async-done | bytes 14843920 | tf_op jit(solution)/shard_map/all_gather | solution.py:122
  193.8 283.7 %reduce.23 = bf16[32,231936]{1,0:T(8,128)(2,1)} reduce(bf16[32,1,231936]{2,1,0:T(2,128)(2,1)} %all-gather.3.cloned.1.call-done, bf16[]{:T(256)} %constant.239), dimensions={1}, to_apply=%all-gather.reduce_sub_computation | reduce | bytes 29687810 | tf_op jit(solution)/shard_map/all_gather | solution.py:122
  477.5 26.0 %reshape.746 = bf16[7421952]{0:T(1024)(128)(2,1)} reshape(bf16[32,231936]{1,0:T(8,128)(2,1)} %reduce.23) | data formatting | bytes 29687808
  503.5 8.9 fusion.96
  516.8 8.3 slice.138
  525.0 7.7 reshape.648
  532.7 3.9 fusion.31
  542.8 6.5 fusion.99
  549.4 5.8 fusion.18
  556.4 9.4 slice.141
  565.9 18.9 %multiply_convert_fusion.1 = (bf16[472,3072]{1,0:T(8,128)(2,1)S(1)}, f32[472,3072]{1,0:T(8,128)}, f32[472,3072]{1,0:T(8,128)}) fusion(f32[3072]{0:T(1024)S(1)} %slice.139, bf16[768,3072]{1,0:T(8,128)(2,1)} %slice.138, f32[472,768]{1,0:T(8,128)S(1)} %get-tuple-element.64, f32[768]{0:T(1024)S(1)} %get-tuple-element.52, f32[768]{0:T(1024)S(1)} %get-tuple-element.53, ...), kind=kOutput, calls=%fused_computation.16 | convolution fusion | flops 2324686848 | bytes 20690624 | tf_op jit(solution)/shard_map/dot_general | solution.py:156
  584.9 5.0 fusion.101
  599.9 174.6 %gather_fusion.2 = f32[23200]{0:T(1024)S(1)} fusion(f32[232,232]{1,0:T(8,128)S(1)} %convolution_multiply_fusion, s32[23200]{0:T(1024)S(1)} %reshape.691), kind=kCustom, calls=%fused_computation.2 | custom fusion | bytes 371200 | tf_op jit(solution)/shard_map/jvp(jit(take_along_axis))/gather | solution.py:84
  776.4 155.4 %scatter_custom_fusion.2 = f32[53824]{0:T(1024)S(1)} fusion(s32[23200]{0:T(1024)} %reshape.723, f32[23200]{0:T(1024)S(1)} %reshape.725, f32[]{:T(128)} %constant.58.clone.1), kind=kCustom, calls=%fused_computation.137 | custom fusion | flops 23200 | bytes 215808
  932.2 13.3 scatter_fusion
  951.6 9.8 convert_reduce_fusion
  972.2 7.4 fusion.21
  979.6 5.8 multiply_reduce_fusion
  995.6 5.6 convolution_bitcast_fusion.1
  1001.2 5.2 fusion.103
  1009.4 6.8 convolution_bitcast_fusion
  1016.2 8.0 copy.94
  1024.2 7.9 reshape.661
  1032.1 5.1 constant_dynamic-update-slice_fusion
  1040.4 9.4 copy.103
  1049.8 10.8 reshape.664
  1068.2 9.3 constant_dynamic-update-slice_fusion.6
  1077.4 4.1 constant_dynamic-update-slice_fusion.5
  1087.9 6.1 add_bitcast_fusion
  1093.9 437.6 %all-reduce.4.cloned.1.call-done = f32[7421952]{0:T(1024)} async-done(((f32[7421952]{0:T(1024)}), f32[7421952]{0:T(1024)}) %all-reduce.4.cloned.1.call-update) | async-done | bytes 29687824
  1533.6 40.5 %all-reduce.1 = (f32[]{:T(128)}, f32[]{:T(128)}, f32[9728]{0:T(1024)S(1)}) all-reduce(f32[]{:T(128)} %get-tuple-element.60, f32[]{:T(128)} %multiply_reduce_fusion.8, f32[9728]{0:T(1024)S(1)} %constant_dynamic-update-slice_fusion.8), channel_id=1, replica_groups=mesh['dp'=4,'fsdp'=8] {'dp','fsdp'}, use_global_device_ids=true, to_apply=%region_11.12 | all-reduce | flops 9730 | bytes 77840 | tf_op jit(solution)/shard_map/psum | solution.py:267
  (306 shorter events, 84.2 us)
Async XLA Ops:
  7.2 11.6 copy-start.34
  7.2 186.5 %all-gather.3.cloned.1.call-start = ((), (), s32[]{:S(2)}) async-start(), calls=%async_computation | async-start | bytes 30615552 | tf_op jit(solution)/shard_map/all_gather | solution.py:122
  14.6 1516.9 %all-reduce.4.cloned.1.call-start = ((), (), s32[]{:S(2)}) async-start(), calls=%async_computation.1 | async-start | bytes 59375616
  15.3 550.5 %copy-start.60 = (f32[3072]{0:T(1024)}, f32[3072]{0:T(1024)S(1)}, u32[]{:S(2)}) copy-start(f32[3072]{0:T(1024)S(1)} %slice.139) | copy-start | bytes 36868
  16.3 461.1 %copy-start.19 = (s32[1,232,100]{2,1,0:T(8,128)}, s32[1,232,100]{2,1,0:T(8,128)S(1)}, u32[]{:S(2)}) copy-start(s32[1,232,100]{2,1,0:T(8,128)S(1)} %copy.86) | copy-start | bytes 278404
  20.0 564.8 %copy-start.54 = (f32[768]{0:T(1024)}, f32[768]{0:T(1024)S(1)}, u32[]{:S(2)}) copy-start(f32[768]{0:T(1024)S(1)} %get-tuple-element.53) | copy-start | bytes 9220
  20.0 564.8 %copy-start.68 = (f32[768]{0:T(1024)}, f32[768]{0:T(1024)S(1)}, u32[]{:S(2)}) copy-start(f32[768]{0:T(1024)S(1)} %get-tuple-element.52) | copy-start | bytes 9220
  503.5 11.4 copy-start
  516.8 73.6 %copy-start.23 = (bf16[65536]{0:T(1024)(128)(2,1)}, bf16[65536]{0:T(1024)(128)(2,1)S(1)}, u32[]{:S(2)}) copy-start(bf16[65536]{0:T(1024)(128)(2,1)S(1)} %slice.177) | copy-start | bytes 393220
  556.1 28.7 %copy-start.48 = (f32[472]{0:T(512)}, f32[472]{0:T(512)S(1)}, u32[]{:S(2)}) copy-start(f32[472]{0:T(512)S(1)} %broadcast_multiply_fusion.2) | copy-start | bytes 5668
  556.4 28.4 %copy-start.63 = (f32[472]{0:T(512)}, f32[472]{0:T(512)S(1)}, u32[]{:S(2)}) copy-start(f32[472]{0:T(512)S(1)} %fusion.72) | copy-start | bytes 5668
  565.9 18.9 %copy-start.8 = (bf16[3072,768]{1,0:T(8,128)(2,1)S(1)}, bf16[3072,768]{1,0:T(8,128)(2,1)}, u32[]{:S(2)}) copy-start(bf16[3072,768]{1,0:T(8,128)(2,1)} %slice.141) | copy-start | bytes 14155780
  595.8 349.7 %copy-start.2 = (f32[232,256]{1,0:T(8,128)}, f32[232,256]{1,0:T(8,128)S(1)}, u32[]{:S(2)}) copy-start(f32[232,256]{1,0:T(8,128)S(1)} %get-tuple-element.69) | copy-start | bytes 712708
  599.9 174.9 %copy-start.20 = (s32[1,232,100]{2,1,0:T(8,128)S(1)}, s32[1,232,100]{2,1,0:T(8,128)}, u32[]{:S(2)}) copy-start(s32[1,232,100]{2,1,0:T(8,128)} %copy-done.19) | copy-start | bytes 278404
  599.9 332.3 %copy-start.1 = (s32[232,1]{0,1:T(1,128)S(1)}, s32[232,1]{0,1:T(1,128)}, u32[]{:S(2)}) copy-start(s32[232,1]{0,1:T(1,128)} %or_select_fusion) | copy-start | bytes 2788
  774.5 173.3 %copy-start.37 = (f32[768]{0:T(1024)S(1)}, f32[768]{0:T(1024)}, u32[]{:S(2)}) copy-start(f32[768]{0:T(1024)} %get-tuple-element.49) | copy-start | bytes 9220
  774.5 173.3 %copy-start.39 = (f32[472]{0:T(512)S(1)}, f32[472]{0:T(512)}, u32[]{:S(2)}) copy-start(f32[472]{0:T(512)} %copy-done.38) | copy-start | bytes 5668
  774.5 173.3 %copy-start.41 = (f32[472]{0:T(512)S(1)}, f32[472]{0:T(512)}, u32[]{:S(2)}) copy-start(f32[472]{0:T(512)} %copy-done.40) | copy-start | bytes 5668
  775.9 174.3 %copy-start.53 = (f32[472]{0:T(512)S(1)}, f32[472]{0:T(512)}, u32[]{:S(2)}) copy-start(f32[472]{0:T(512)} %copy-done.52) | copy-start | bytes 5668
  950.2 11.2 slice-start.9
  965.5 14.1 copy-start.65
  972.2 13.2 slice-start.6
  972.2 13.2 slice-start.7
  1049.8 13.4 copy-start.25
  1049.8 13.9 copy-start.74
  1064.7 12.7 slice-start.3
  1087.8 488.9 %copy-start.35 = (f32[9728]{0:T(1024)S(1)}, f32[9728]{0:T(1024)}, u32[]{:S(2)}) copy-start(f32[9728]{0:T(1024)} %param.17) | copy-start | bytes 116740
  1087.8 488.9 %copy-start.42 = (f32[9728]{0:T(1024)S(1)}, f32[9728]{0:T(1024)}, u32[]{:S(2)}) copy-start(f32[9728]{0:T(1024)} %param.18) | copy-start | bytes 116740
  1087.8 488.9 %copy-start.43 = (f32[9728]{0:T(1024)S(1)}, f32[9728]{0:T(1024)}, u32[]{:S(2)}) copy-start(f32[9728]{0:T(1024)} %param.19) | copy-start | bytes 116740
  1087.8 489.6 %copy-start.9 = (f32[231936]{0:T(1024)S(1)}, f32[231936]{0:T(1024)}, u32[]{:S(2)}) copy-start(f32[231936]{0:T(1024)} %param.14) | copy-start | bytes 2783236
  1087.9 489.6 %copy-start.26 = (f32[231936]{0:T(1024)S(1)}, f32[231936]{0:T(1024)}, u32[]{:S(2)}) copy-start(f32[231936]{0:T(1024)} %param.15) | copy-start | bytes 2783236
  1087.9 489.5 %copy-start.27 = (f32[231936]{0:T(1024)S(1)}, f32[231936]{0:T(1024)}, u32[]{:S(2)}) copy-start(f32[231936]{0:T(1024)} %param.16) | copy-start | bytes 2783236
  (64 other events, 355.1 us)
Sparse Core Ops, SparseCore 0:
  14.7 179.0 all-gather.2
  1084.2 447.2 all-reduce.3
where the time goes:
time: 1600 us; the launch traced here: 1590 us
  waiting for transfers between devices  611 us (38%)
  other arithmetic  476 us (30%)
  local copies, waits for them, and re-layouts  335 us (21%)
  matrix products  108 us (7%)
  blocking collectives  40.5 us (3%)
  between operations  20 us (1%)
    unnamed x3, waiting for transfers between devices  438 us
    all_gather x1, other arithmetic, on_device(): gathered = lax.all_gather(shard_low, ('dp', 'fsdp'), axis=0, tiled=True)  284 us
    gather x4, local copies, waits for them, and re-layouts, contrast_loss(): negative = jnp.take_along_axis(angular_agreement, distract, axis=2)  175 us
    all_gather x1, waiting for transfers between devices, on_device(): gathered = lax.all_gather(shard_low, ('dp', 'fsdp'), axis=0, tiled=True)  174 us
    unnamed x8, other arithmetic  156 us
    unnamed x205, local copies, waits for them, and re-layouts  74.4 us
    psum x1, blocking collectives, on_device(): lax.psum((vector_gradient, loss_local), ('dp', 'fsdp'))  40.5 us
  transfers between devices with their start and end apart: 2, of which 2 were waited for; matrix products, arithmetic and copies ran while one was open for 1% of the time, Pallas kernels for 0%

commit v1 on v0

--- a/solution.py
+++ b/solution.py
@@ -3,7 +3,13 @@
 import jax
 import jax.numpy as jnp
 from jax import lax
+from jax.experimental import pallas as pl
+from jax.experimental.pallas import tpu as pltpu
 from jax.sharding import PartitionSpec as P
+
+MESH = pl.DeviceIdType.MESH
+NROW = 9664
+GROW = NROW + 256
 
 D = 768
 H = 12
@@ -56,34 +62,25 @@
     return centered * lax.rsqrt(variance + eps_norm) * scale_gain + shift_bias
 
 
-def pick_rows(source, index_rows):
-    return source[index_rows]
-
-
-def place_rows(template, index_rows, values):
-    return template.at[index_rows].set(values)
-
-
-def contrast_loss(chosen, targets, distract):
-    encoder_unit_heading = chosen * lax.rsqrt(
-        jnp.sum(chosen * chosen, axis=-1, keepdims=True) + eps_cos
-    )
-    quantized_unit_heading = targets * lax.rsqrt(
-        jnp.sum(targets * targets, axis=-1, keepdims=True) + eps_cos
-    )
-    angular_agreement = (
-        jnp.einsum(
-            "rby,roy->rbo",
-            encoder_unit_heading,
-            quantized_unit_heading,
-            precision=lax.Precision.HIGHEST,
-        )
-        / softness_divisor
-    )
-    positive = jnp.diagonal(angular_agreement, axis1=1, axis2=2)
-    negative = jnp.take_along_axis(angular_agreement, distract, axis=2)
-    logits_all = jnp.concatenate([positive[..., None], negative], axis=-1)
-    return jnp.sum(jax.nn.logsumexp(logits_all, axis=-1) - positive)
+def contrast(chosen, targets, distract, weight):
+    hi = dict(precision=lax.Precision.HIGHEST)
+    frames = jnp.arange(MASKED, dtype=jnp.int32)
+    allowed = jnp.any(distract[:, :, None] == frames, axis=1) | (frames[:, None] == frames)
+
+    def agreement(chosen, targets):
+        left = chosen * lax.rsqrt(jnp.sum(chosen * chosen, axis=-1, keepdims=True) + eps_cos)
+        right = targets * lax.rsqrt(jnp.sum(targets * targets, axis=-1, keepdims=True) + eps_cos)
+        return jnp.einsum("by,oy->bo", left, right, **hi) / softness_divisor
+
+    similar, back = jax.vjp(agreement, chosen, targets)
+    same = frames[:, None] == frames
+    positive = jnp.sum(jnp.where(same, similar, 0.0), axis=1)
+    top = jnp.max(jnp.where(allowed, similar, -jnp.inf), axis=1)
+    parts = jnp.where(allowed, jnp.exp(similar - top[:, None]), 0.0)
+    total = jnp.sum(parts, axis=1)
+    loss = jnp.sum(top + jnp.log(total) - positive)
+    d_similar = weight * (parts / total[:, None] - same.astype(jnp.float32))
+    return (loss,) + back(d_similar)
 
 
 def adamw_update(master, first_moment, second, gradient, step_rate):
@@ -95,6 +92,327 @@
         jnp.sqrt(second_hat) + adam_eps
     )
     return (master_new, first_new, second_new)
+
+
+def ag_kernel(p_ref, g_ref, raw, land, sem_raw, R, D, SU, SZ, SV, SD):
+    bf16 = jnp.bfloat16
+    z = lax.axis_index("dp"); f = lax.axis_index("fsdp")
+    c = f % 2; k = f // 2; x = k % 2; y = k // 2
+    fc = f + 1 - 2 * c
+    fx = f + 2 - 4 * x
+    fy = f + 4 - 8 * y
+    uf = fx * (1 - c) + fy * c
+    vf = fy * (1 - c) + fx * c
+    ku = uf // 2; kv = vf // 2; kuv = 3 - k
+    Z = 4
+    bar = pltpu.get_barrier_semaphore()
+    for t in ((z, fc), (z, fx), (z, fy)):
+        pl.semaphore_signal(bar, inc=1, device_id=t, device_id_type=MESH)
+    @pl.when(z > 0)
+    def _(): pl.semaphore_signal(bar, inc=1, device_id=(z - 1, f), device_id_type=MESH)
+    @pl.when(z < Z - 1)
+    def _(): pl.semaphore_signal(bar, inc=1, device_id=(z + 1, f), device_id_type=MESH)
+    pl.semaphore_wait(bar, 3 + (z + Z - 1) // Z + (2 * Z - 2 - z) // Z)
+
+    rawcopy = pltpu.make_async_remote_copy(src_ref=p_ref.at[pl.ds(0, 1812)], dst_ref=land.at[pl.ds(0, 1812)], send_sem=sem_raw.at[0], recv_sem=sem_raw.at[1],
+                                           device_id=(z, fc), device_id_type=MESH)
+    rawcopy.start()
+    @pl.when(c == 0)
+    def _(): raw[96:96 + 1812, :] = p_ref[...]
+    @pl.when(c == 1)
+    def _(): raw[96 + 1812:96 + 3624, :] = p_ref[...]
+    rawcopy.wait()
+    @pl.when(c == 1)
+    def _(): raw[96:96 + 1812, :] = land[0:1812]
+    @pl.when(c == 0)
+    def _(): raw[96 + 1812:96 + 3624, :] = land[0:1812]
+    own = 2416 * z + 608 * k
+    for j in range(6):
+        g_ref[pl.ds(own, 592), 128*j:128*j+128] = raw[pl.ds(96 + 24 * k + j, 592, stride=6), :].astype(bf16)
+        last = raw[pl.ds(96 + (592 + 4 * k) * 6 + j, 16, stride=6), :]
+        first = raw[pl.ds(24 * k + j, 16, stride=6), :]
+        row = lax.broadcasted_iota(jnp.int32, (16, 128), 0)
+        g_ref[pl.ds(NROW + 16 * (4 * z + k), 16), 128*j:128*j+128] = jnp.where(row < 12 - 4 * k, last, first).astype(bf16)
+
+    def spans(plane, kk, cc):
+        m = pl.multiple_of(2416 * plane + 608 * kk + 304 * cc, 16)
+        ms = 2416 * plane + 608 * kk
+        side = NROW + 16 * (4 * plane + kk)
+        e = pl.multiple_of((ms + 288) * (1 - cc) + side * cc, 16)
+        return ((m, 288), (e, 16))
+    def copies(plane, kk, cc, dev, ssem, rsem):
+        return [pltpu.make_async_remote_copy(src_ref=g_ref.at[pl.ds(s, n)], dst_ref=g_ref.at[pl.ds(s, n)], send_sem=ssem.at[i], recv_sem=rsem.at[i], device_id=dev, device_id_type=MESH)
+                for i, (s, n) in enumerate(spans(plane, kk, cc))]
+    up = (z + 1, f); down = (z - 1, f)
+    def send(plane, kk, dev, ssem):
+        for cp in copies(plane, kk, c, dev, ssem, R.at[4 * plane + kk]): cp.start()
+    def d2d(plane, kk):
+        for cp in copies(plane, kk, c, (z, fc), SD.at[4 * plane + kk], D.at[4 * plane + kk]): cp.start()
+    def recv(plane, kk):
+        for cp in copies(plane, kk, c, (z, fc), SD.at[0], R.at[4 * plane + kk]): cp.wait_recv()
+    def recvd(plane, kk):
+        for cp in copies(plane, kk, 1 - c, (z, fc), SD.at[0], D.at[4 * plane + kk]): cp.wait_recv()
+    def sent(plane, kk, ssem):
+        for cp in copies(plane, kk, c, (z, fc), ssem, R.at[0]): cp.wait_send()
+
+    send(z, k, (z, uf), SU)
+    @pl.when(z < Z - 1)
+    def _(): send(z, k, up, SZ.at[0, z, 0])
+    @pl.when(z > 0)
+    def _(): send(z, k, down, SZ.at[1, z, 0])
+    send(z, k, (z, vf), SV.at[z, 0])
+    recv(z, ku)
+    @pl.when(z < Z - 1)
+    def _(): send(z, ku, up, SZ.at[0, z, 1])
+    @pl.when(z > 0)
+    def _(): send(z, ku, down, SZ.at[1, z, 1])
+    send(z, ku, (z, vf), SV.at[z, 1])
+    d2d(z, ku)
+    for s in range(1, Z + 1):
+        if s < Z:
+            for i, kk in ((0, k), (1, ku)):
+                @pl.when(z - s >= 0)
+                def _():
+                    recv(z - s, kk)
+                    @pl.when(z < Z - 1)
+                    def _(): send(z - s, kk, up, SZ.at[0, z - s, i])
+                    send(z - s, kk, (z, vf), SV.at[z - s, i])
+                    d2d(z - s, kk)
+                @pl.when(z + s < Z)
+                def _():
+                    recv(z + s, kk)
+                    @pl.when(z > 0)
+                    def _(): send(z + s, kk, down, SZ.at[1, z + s, i])
+                    send(z + s, kk, (z, vf), SV.at[z + s, i])
+                    d2d(z + s, kk)
+        t = s - 1
+        for kk in (kv, kuv):
+            if t == 0:
+                recv(z, kk); d2d(z, kk)
+            else:
+                @pl.when(z - t >= 0)
+                def _(): recv(z - t, kk); d2d(z - t, kk)
+                @pl.when(z + t < Z)
+                def _(): recv(z + t, kk); d2d(z + t, kk)
+    for plane in range(Z):
+        for kk in (ku, kv, kuv):
+            recvd(plane, kk)
+        @pl.when(z != plane)
+        def _(): recvd(plane, k)
+    sent(z, k, SU)
+    for plane in range(Z):
+        for i, kk in ((0, k), (1, ku)):
+            sent(plane, kk, SV.at[plane, i])
+            @pl.when((z < Z - 1) & (plane <= z))
+            def _(): sent(plane, kk, SZ.at[0, plane, i])
+            @pl.when((z > 0) & (plane >= z))
+            def _(): sent(plane, kk, SZ.at[1, plane, i])
+        for kk in (ku, kv, kuv):
+            sent(plane, kk, SD.at[4 * plane + kk])
+        @pl.when(z != plane)
+        def _(): sent(plane, k, SD.at[4 * plane + k])
+    row = lax.broadcasted_iota(jnp.int32, (16, 768), 0)
+    for plane in range(Z):
+        for q, bound in ((0, 12), (1, 8), (2, 4)):
+            a = g_ref[NROW + 16 * (4 * plane + q):NROW + 16 * (4 * plane + q) + 16, :].astype(jnp.float32)
+            b = g_ref[NROW + 16 * (4 * plane + q + 1):NROW + 16 * (4 * plane + q + 1) + 16, :].astype(jnp.float32)
+            at = 2416 * plane + 608 * q + 592
+            g_ref[at:at + 16, :] = jnp.where(row < bound, a, b).astype(bf16)
+
+def ag(params):
+    DMA = pltpu.SemaphoreType.DMA
+    return pl.pallas_call(ag_kernel,
+        out_shape=jax.ShapeDtypeStruct((GROW, 768), jnp.bfloat16),
+        in_specs=[pl.BlockSpec(memory_space=pltpu.VMEM)], out_specs=pl.BlockSpec(memory_space=pltpu.VMEM),
+        scratch_shapes=[pltpu.VMEM((96 + 3624 + 96, 128), jnp.float32), pltpu.VMEM((1816, 128), jnp.float32), DMA((2,)),
+                        DMA((16, 2)), DMA((16, 2)), DMA((2,)), DMA((2, 4, 2, 2)), DMA((4, 2, 2)), DMA((16, 2))],
+        compiler_params=pltpu.CompilerParams(collective_id=0, has_side_effects=True, vmem_limit_bytes=60*2**20))(params.reshape(1812, 128))
+
+
+HALF = 304
+
+def place():
+    z = lax.axis_index("dp"); f = lax.axis_index("fsdp")
+    c = f % 2; k = f // 2; x = k % 2; y = k // 2
+    fc = f + 1 - 2 * c
+    fx = f + 2 - 4 * x
+    fy = f + 4 - 8 * y
+    uf = fx * (1 - c) + fy * c
+    vf = fy * (1 - c) + fx * c
+    return z, f, c, k, fc, fx, fy, uf, vf
+
+def greet(z, f, fc, fx, fy, Z):
+    bar = pltpu.get_barrier_semaphore()
+    for t in ((z, fc), (z, fx), (z, fy)):
+        pl.semaphore_signal(bar, inc=1, device_id=t, device_id_type=MESH)
+    @pl.when(z > 0)
+    def _(): pl.semaphore_signal(bar, inc=1, device_id=(z - 1, f), device_id_type=MESH)
+    @pl.when(z < Z - 1)
+    def _(): pl.semaphore_signal(bar, inc=1, device_id=(z + 1, f), device_id_type=MESH)
+    pl.semaphore_wait(bar, 3 + (z + Z - 1) // Z + (2 * Z - 2 - z) // Z)
+
+def rs_kernel(g_in, vec_in, out, vec_out, sq_out, g, LD, LV, LZ, LU, B, F, vec, vland, sq, sqland,
+              s_in, SD, RD, SV, RV, SZ, RZ, SU, SX, SB, SQ):
+    bf16 = jnp.bfloat16; f32 = jnp.float32
+    z, f, c, k, fc, fx, fy, uf, vf = place()
+    ku = uf // 2; kv = vf // 2; kuv = 3 - k
+    Z = 4
+    cp = pltpu.make_async_copy(g_in, g.at[pl.ds(0, NROW)], s_in)
+    cp.start()
+    greet(z, f, fc, fx, fy, Z)
+    cp.wait()
+    row = lax.broadcasted_iota(jnp.int32, (16, 768), 0)
+    for plane in range(Z):
+        b37, b75, b113 = [g[2416 * plane + 16 * b:2416 * plane + 16 * b + 16, :].astype(f32) for b in (37, 75, 113)]
+        for q, v in enumerate((b37, jnp.where(row < 8, b75, b37), jnp.where(row < 4, b113, b75), b113)):
+            at = NROW + 16 * (4 * plane + q)
+            g[at:at + 16, :] = v.astype(bf16)
+
+    def spans(plane, kk, cc):
+        ms = 2416 * plane + 608 * kk
+        m = pl.multiple_of(ms + 304 * cc, 16)
+        side = NROW + 16 * (4 * plane + kk)
+        e = pl.multiple_of((ms + 288) * (1 - cc) + side * cc, 16)
+        return (m, e)
+    def copies(plane, kk, cc, dst, dev, ssem, rsem):
+        m, e = spans(plane, kk, cc)
+        return [pltpu.make_async_remote_copy(src_ref=g.at[pl.ds(m, 288)], dst_ref=dst.at[pl.ds(0, 288)], send_sem=ssem.at[0], recv_sem=rsem.at[0], device_id=dev, device_id_type=MESH),
+                pltpu.make_async_remote_copy(src_ref=g.at[pl.ds(e, 16)], dst_ref=dst.at[pl.ds(288, 16)], send_sem=ssem.at[1], recv_sem=rsem.at[1], device_id=dev, device_id_type=MESH)]
+    def start(cs):
+        for q in cs: q.start()
+    def add(plane, kk, srcs, final=False):
+        m, e = spans(plane, kk, c)
+        def one(at, i):
+            v = g[pl.ds(at, 16), :].astype(f32)
+            for s in srcs:
+                v = v + s[pl.ds(i, 16), :].astype(f32)
+            if final:
+                B[pl.ds(16 + i, 16), :] = v
+            else:
+                g[pl.ds(at, 16), :] = v.astype(bf16)
+        def body(b, _):
+            i = pl.multiple_of(16 * b, 16)
+            one(pl.multiple_of(m + i, 16), i)
+            return 0
+        lax.fori_loop(0, 18, body, 0)
+        one(e, 288)
+
+    order = (3, 0, 2, 1)
+    U = lambda plane, kk: 4 * plane + kk
+    for plane in order:
+        for kk in (kv, kuv):
+            start(copies(plane, kk, 1 - c, LD.at[U(plane, kk)], (z, fc), SD.at[U(plane, kk)], RD.at[U(plane, kk)]))
+    for plane in order:
+        for kk in (k, ku):
+            start(copies(plane, kk, 1 - c, LD.at[U(plane, kk)], (z, fc), SD.at[U(plane, kk)], RD.at[U(plane, kk)]))
+    def wait_d(plane, kk):
+        for q in copies(plane, kk, 1 - c, LD.at[U(plane, kk)], (z, fc), SD.at[U(plane, kk)], RD.at[U(plane, kk)]): q.wait_recv()
+    def landv(plane, kk): return LV.at[U(plane, kk)]
+    for plane in order:
+        for kk in (kv, kuv):
+            wait_d(plane, kk)
+            add(plane, kk, [LD.at[U(plane, kk)]])
+            start(copies(plane, kk, c, landv(plane, kk), (z, vf), SV.at[U(plane, kk)], RV.at[U(plane, kk)]))
+    def zsend(plane, i, kk, up):
+        return copies(plane, kk, c, LZ.at[up, U(plane, kk)], (z + (2 * up - 1), f), SZ.at[U(plane, kk)], RZ.at[up, U(plane, kk)])
+    def zwait(plane, kk, up):
+        for q in copies(plane, kk, c, LZ.at[up, U(plane, kk)], (z, fc), SZ.at[U(plane, kk)], RZ.at[up, U(plane, kk)]): q.wait_recv()
+    for plane in order:
+        for i, kk in ((0, k), (1, ku)):
+            u = U(plane, kk)
+            wait_d(plane, kk)
+            for q in copies(plane, kk, c, landv(plane, kk), (z, vf), SV.at[u], RV.at[u]): q.wait_recv()
+            @pl.when(z < plane)
+            def _():
+                @pl.when(z > 0)
+                def _():
+                    zwait(plane, kk, 1)
+                    add(plane, kk, [LD.at[u], LV.at[u], LZ.at[1, u]])
+                @pl.when(z == 0)
+                def _():
+                    add(plane, kk, [LD.at[u], LV.at[u]])
+                start(zsend(plane, i, kk, 1))
+            @pl.when(z > plane)
+            def _():
+                @pl.when(z < Z - 1)
+                def _():
+                    zwait(plane, kk, 0)
+                    add(plane, kk, [LD.at[u], LV.at[u], LZ.at[0, u]])
+                @pl.when(z == Z - 1)
+                def _():
+                    add(plane, kk, [LD.at[u], LV.at[u]])
+                start(zsend(plane, i, kk, 0))
+    def gather_z(kk, extra, final):
+        u = U(z, kk)
+        @pl.when(z == 0)
+        def _():
+            zwait(z, kk, 0)
+            add(z, kk, [LD.at[u], LV.at[u], LZ.at[0, u]] + extra, final)
+        @pl.when(z == Z - 1)
+        def _():
+            zwait(z, kk, 1)
+            add(z, kk, [LD.at[u], LV.at[u], LZ.at[1, u]] + extra, final)
+        @pl.when((z > 0) & (z < Z - 1))
+        def _():
+            zwait(z, kk, 0)
+            zwait(z, kk, 1)
+            add(z, kk, [LD.at[u], LV.at[u], LZ.at[0, u], LZ.at[1, u]] + extra, final)
+    gather_z(ku, [], False)
+    ucopies = copies(z, ku, c, LU, (z, uf), SU.at[0], SU.at[1])
+    start(ucopies)
+    for q in copies(z, k, c, LU, (z, uf), SU.at[0], SU.at[1]): q.wait_recv()
+    gather_z(k, [LU], True)
+    bx = pltpu.make_async_remote_copy(src_ref=B.at[pl.ds(304, 16)], dst_ref=B.at[pl.ds(0, 16)], send_sem=SB.at[0], recv_sem=SB.at[1], device_id=(z, fc), device_id_type=MESH)
+    bx.start()
+    vec[...] = vec_in[...]
+    steps = [(z, fc), (z, fx), (z, fy), (z + 1 - 2 * (z % 2), f), (z + 2 - 4 * (z // 2), f)]
+    for i, dev in enumerate(steps):
+        q = pltpu.make_async_remote_copy(src_ref=vec, dst_ref=vland.at[i], send_sem=SX.at[i, 0], recv_sem=SX.at[i, 1], device_id=dev, device_id_type=MESH)
+        q.start(); q.wait()
+        vec[...] = vec[...] + vland[i]
+    vec_out[...] = vec[...]
+    bx.wait()
+    tot = jnp.zeros((8, 128), f32)
+    for j in range(6):
+        F[pl.ds(j, 320, stride=6), :] = B[:, 128 * j:128 * j + 128]
+    for j in range(6):
+        v = F[pl.ds(6 * (16 - 2 * c - 4 * k) + j, 302, stride=6), :]
+        out[pl.ds(j, 302, stride=6), :] = v
+        vv = v * v
+        tot = tot + jnp.sum(vv[0:296].reshape(37, 8, 128), axis=0)
+        tot = tot + jnp.concatenate([vv[296:302], jnp.zeros((2, 128), f32)], axis=0)
+    sq[...] = tot
+    for i, dev in enumerate(steps):
+        q = pltpu.make_async_remote_copy(src_ref=sq, dst_ref=sqland.at[i], send_sem=SQ.at[i, 0], recv_sem=SQ.at[i, 1], device_id=dev, device_id_type=MESH)
+        q.start(); q.wait()
+        sq[...] = sq[...] + sqland[i]
+    sq_out[...] = sq[...]
+    for plane in range(Z):
+        for kk in range(4):
+            u = U(plane, kk)
+            for q in copies(plane, kk, 1 - c, LD.at[u], (z, fc), SD.at[u], RD.at[u]): q.wait_send()
+        for kk in (kv, kuv):
+            u = U(plane, kk)
+            for q in copies(plane, kk, c, LV.at[u], (z, vf), SV.at[u], RV.at[u]): q.wait_send()
+        @pl.when(z != plane)
+        def _():
+            for kk in (k, ku):
+                u = U(plane, kk)
+                for q in copies(plane, kk, c, LZ.at[0, u], (z, fc), SZ.at[u], RZ.at[0, u]): q.wait_send()
+    for q in ucopies: q.wait_send()
+
+def rs(g, vec):
+    DMA = pltpu.SemaphoreType.DMA
+    f32 = jnp.float32; bf16 = jnp.bfloat16
+    V = pl.BlockSpec(memory_space=pltpu.VMEM)
+    return pl.pallas_call(rs_kernel,
+        out_shape=[jax.ShapeDtypeStruct((1812, 128), f32), jax.ShapeDtypeStruct(vec.shape, f32), jax.ShapeDtypeStruct((8, 128), f32)],
+        in_specs=[pl.BlockSpec(memory_space=pl.ANY), V], out_specs=[V, V, V],
+        scratch_shapes=[pltpu.VMEM((GROW, 768), bf16), pltpu.VMEM((16, HALF, 768), bf16), pltpu.VMEM((16, HALF, 768), bf16), pltpu.VMEM((2, 16, HALF, 768), bf16),
+                        pltpu.VMEM((HALF, 768), bf16), pltpu.VMEM((320, 768), f32), pltpu.VMEM((1920, 128), f32), pltpu.VMEM(vec.shape, f32), pltpu.VMEM((5,) + vec.shape, f32),
+                        pltpu.VMEM((8, 128), f32), pltpu.VMEM((5, 8, 128), f32),
+                        DMA, DMA((16, 2)), DMA((16, 2)), DMA((16, 2)), DMA((16, 2)), DMA((16, 2)), DMA((2, 16, 2)), DMA((2, 2)), DMA((5, 2)), DMA((2,)), DMA((5, 2))],
+        compiler_params=pltpu.CompilerParams(collective_id=1, has_side_effects=True, vmem_limit_bytes=62*2**20))(g, vec)
 
 
 def column_sum(values):
@@ -118,8 +436,11 @@
     count_utts = layer_input.shape[0]
     total_masked = count_utts * lax.axis_size(("dp", "fsdp")) * MASKED
     token_rows = count_utts * LEN
-    shard_low = params.astype(bf16)
-    gathered = lax.all_gather(shard_low, ("dp", "fsdp"), axis=0, tiled=True)
+    kernels = lax.axis_size("dp") == 4 and lax.axis_size("fsdp") == 8
+    if kernels:
+        gathered = ag(params)[:NROW].reshape(-1)
+    else:
+        gathered = lax.all_gather(params.astype(bf16), ("dp", "fsdp"), axis=0, tiled=True)
     qkv_weight, out_weight, up_weight, down_weight, proj_weight, codebook, code_weight = unpack(
         gathered
     )
@@ -159,7 +480,9 @@
     residual_two = normed + jnp.dot(active_low, down_weight, preferred_element_type=f32) + bias_down
     output, back_two = jax.vjp(layer_norm, residual_two, gain_two, shift_two)
     output_low = output.astype(bf16)
-    context = jnp.dot(output_low, proj_weight, preferred_element_type=f32) + bias_proj
+    place = (mask_index[0][:, None] == jnp.arange(LEN, dtype=jnp.int32)).astype(bf16)
+    picked = jnp.dot(place, output_low, preferred_element_type=f32).astype(bf16)
+    chosen = jnp.dot(picked, proj_weight, preferred_element_type=f32) + bias_proj
     choose = (code_choice[..., None] == jnp.arange(V, dtype=jnp.int32)).astype(bf16)
     code_vectors = jnp.einsum(
         "bmgv,gcv->bmgc", choose, codebook.reshape(G, CD, V), preferred_element_type=f32
@@ -168,12 +491,8 @@
     targets = (
         jnp.einsum("bmc,cf->bmf", code_vectors, code_weight, preferred_element_type=f32) + bias_code
     )
-    chosen = jax.vmap(pick_rows)(context.reshape(count_utts, LEN, FINAL), mask_index)
-    loss_local, contrast_back = jax.vjp(partial(contrast_loss, distract=distract), chosen, targets)
-    qkv_weight, out_weight, up_weight, down_weight, proj_weight, codebook, code_weight = unpack(
-        lax.all_gather(shard_low, ("dp", "fsdp"), axis=0, tiled=True)
-    )
-    d_selected_code, d_targets = contrast_back(jnp.asarray(1.0 / total_masked, f32))
+    loss_local, d_chosen, d_targets = contrast(chosen, targets[0], distract[0], 1.0 / total_masked)
+    d_targets = d_targets[None]
     d_targets_low = d_targets.astype(bf16)
     quantized_offset_slope = column_sum(d_targets_low)
     d_code_weight = jnp.einsum(
@@ -188,12 +507,10 @@
         choose.astype(f32),
         precision=lax.Precision.HIGHEST,
     ).reshape(G * CD, V)
-    d_context = jax.vmap(place_rows)(
-        jnp.zeros((count_utts, LEN, FINAL), f32), mask_index, d_selected_code
-    )
-    d_context_low = d_context.reshape(token_rows, FINAL).astype(bf16)
-    d_bias_proj = column_sum(d_context_low)
-    d_proj_weight = jnp.einsum("td,tf->df", output_low, d_context_low, preferred_element_type=f32)
+    d_chosen_low = d_chosen.astype(bf16)
+    d_bias_proj = column_sum(d_chosen_low)
+    d_proj_weight = jnp.einsum("td,tf->df", picked, d_chosen_low, preferred_element_type=f32)
+    d_context_low = jnp.einsum("mt,mf->tf", place, d_chosen_low, preferred_element_type=f32).astype(bf16)
     result_sensitivity = jnp.einsum(
         "tf,df->td", d_context_low, proj_weight, preferred_element_type=f32
     )
@@ -264,16 +581,17 @@
             quantized_offset_slope,
         ]
     )
-    vector_sum, loss_sum = lax.psum((vector_gradient, loss_local), ("dp", "fsdp"))
-    owner_rows = params.shape[0]
-    grad_shard = lax.psum_scatter(
-        lax.slice_in_dim(flat_grad, 0, lax.axis_size(("dp", "fsdp")) * owner_rows, axis=0),
-        ("dp", "fsdp"),
-        scatter_dimension=0,
-        tiled=True,
-    )
-    local_squares = jnp.sum(grad_shard * grad_shard)
-    square_sum = lax.psum(local_squares, ("dp", "fsdp"))
+    if kernels:
+        padded = jnp.concatenate([vector_gradient, jnp.full((512,), loss_local)]).reshape(80, 128)
+        grad_shard, sums, squares = rs(flat_grad.astype(bf16).reshape(NROW, 768), padded)
+        grad_shard = grad_shard.reshape(-1)
+        square_sum = jnp.sum(squares)
+        vector_sum = sums.reshape(-1)[:9728]
+        loss_sum = sums[79, 0]
+    else:
+        vector_sum, loss_sum = lax.psum((vector_gradient, loss_local), ("dp", "fsdp"))
+        grad_shard = lax.psum_scatter(flat_grad, ("dp", "fsdp"), scatter_dimension=0, tiled=True)
+        square_sum = lax.psum(jnp.sum(grad_shard * grad_shard), ("dp", "fsdp"))
     grad_norm = jnp.sqrt(square_sum + jnp.sum(vector_sum * vector_sum))
     factor = jnp.minimum(1.0, clip_level / (grad_norm + 1e-06))
     refreshed_weights, new_one, new_two = adamw_update(

time: 1600 us -> 540 us (0.34)
  waiting for transfers between devices: 611 us -> 0 us
  other arithmetic: 476 us -> 24.8 us
  Pallas kernels: 0 us -> 227 us
  local copies, waits for them, and re-layouts: 335 us -> 172 us
  blocking collectives: 40.5 us -> 0 us
    unnamed x3 -> x0, waiting for transfers between devices: 438 us -> none
    all_gather x1 -> x0, other arithmetic: 284 us -> none  [on_device(): gathered = lax.all_gather(shard_low, ('dp', 'fsdp'), axis=0, tiled=True)]
    pallas_call x0 -> x2, Pallas kernels: none -> 227 us  [the longest x1 141 us: rs(): pl.pallas_call(rs_kernel, out_shape=[jax.ShapeDtypeStruct((1812, 128), f3...]
    gather x7 -> x0, local copies, waits for them, and re-layouts: 180 us -> none  [the longest x4 175 us: contrast_loss(): negative = jnp.take_along_axis(angular_agreement, distract, axis=2)]
    all_gather x1 -> x0, waiting for transfers between devices: 174 us -> none  [on_device(): gathered = lax.all_gather(shard_low, ('dp', 'fsdp'), axis=0, tiled=True)]
    unnamed x8 -> x6, other arithmetic: 156 us -> 0.01 us
    psum x1 -> x0, blocking collectives: 40.5 us -> none  [on_device(): lax.psum((vector_gradient, loss_local), ('dp', 'fsdp'))]
    unnamed x205 -> x173, local copies, waits for them, and re-layouts: 74.4 us -> 37 us
  transfers between devices with their start and end apart: 2 -> 0, of which waited for: 2 -> 0; matrix products, arithmetic and copies ran while one was open for 1% -> 0% of each run, Pallas kernels for 0% -> 0%
where the time goes in v1:
time: 540 us; the launch traced here: 529 us
  Pallas kernels  227 us (42%)
  local copies, waits for them, and re-layouts  172 us (32%)
  matrix products  98 us (18%)
  other arithmetic  24.8 us (5%)
  between operations  6.48 us (1%)
    pallas_call x1, Pallas kernels, rs(): pl.pallas_call(rs_kernel, out_shape=[jax.ShapeDtypeStruct((1812, 128), f3...  141 us
    pallas_call x1, Pallas kernels, ag(): pl.pallas_call(ag_kernel, out_shape=jax.ShapeDtypeStruct((GROW, 768), jnp...  86.8 us
    unnamed x173, local copies, waits for them, and re-layouts  37 us
    slice x9, local copies, waits for them, and re-layouts, unpack(): flat_values[offset:offset + height * width].reshape(height, width)  28.5 us
    convert_element_type x1, local copies, waits for them, and re-layouts, on_device(): flat_grad.astype(bf16).reshape(NROW, 768)  25.8 us
    reshape x1, local copies, waits for them, and re-layouts, on_device(): gathered = ag(params)[:NROW].reshape(-1)  25.8 us
    dot_general x1, matrix products, on_device(): jnp.dot(normed_low, up_weight, preferred_element_type=f32) + bias_up  19.2 us
    reshape x3, local copies, waits for them, and re-layouts, on_device(): matrix_grad.reshape(-1)  16 us

profile of v1, /device:TPU:0, one launch (start us, length us, event | category | flops | bytes accessed | tf_op | source)
XLA Modules:
  0.0 528.9 jit_solution(6907392463811289434)
XLA Ops:
  0.6 86.8 %shard_map.185 = bf16[9920,768]{1,0:T(8,128)(2,1)} custom-call(f32[1812,128]{1,0:T(8,128)} %bitcast.135), custom_call_target="tpu_custom_call" | custom-call | tf_op jit(solution)/shard_map/pallas_call | solution.py:224
  89.5 3.6 reshape.331
  93.1 4.1 fusion.47
  101.5 6.5 %fusion.97 = (f32[12,472]{1,0:T(8,128)S(1)}, f32[12,472,472]{1,2,0:T(8,128)}) fusion(bf16[472,12,64]{0,2,1:T(8,128)(2,1)S(1)} %bitcast.136, bf16[472,12,64]{0,2,1:T(8,128)(2,1)S(1)} %bitcast.138), kind=kOutput, calls=%fused_computation.187 | convolution fusion | flops 350216928 | bytes 12166272 | tf_op jit(solution)/shard_map/sub | solution.py:468
  109.1 6.0 %fusion.27 = bf16[12,64,472]{2,1,0:T(8,128)(2,1)S(1)} fusion(bf16[472,12,64]{0,2,1:T(8,128)(2,1)} %bitcast.147, f32[12,472,472]{1,2,0:T(8,128)} %get-tuple-element.59, f32[12,472]{1,0:T(8,128)S(1)} %get-tuple-element.58), kind=kOutput, calls=%fused_computation.67 | convolution fusion | flops 347905536 | bytes 12166272 | tf_op jit(solution)/shard_map/bhlm,bmhe->blhe/dot_general | solution.py:470
  120.2 2.4 slice.103
  122.6 8.6 %reshape.336 = bf16[768,3072]{1,0:T(8,128)(2,1)} reshape(bf16[3072,768]{1,0:T(8,128)(2,1)} %slice.103) | data formatting | bytes 9437184 | tf_op jit(solution)/shard_map/reshape | solution.py:44
  131.3 19.2 %multiply_convert_fusion.1 = (bf16[472,3072]{1,0:T(8,128)(2,1)S(1)}, f32[472,3072]{1,0:T(8,128)}, f32[472,3072]{1,0:T(8,128)}) fusion(f32[3072]{0:T(1024)S(1)} %slice.104, bf16[768,3072]{1,0:T(8,128)(2,1)} %reshape.336, f32[472,768]{1,0:T(8,128)} %copy-done.5, f32[768]{0:T(1024)S(1)} %get-tuple-element.53, f32[768]{0:T(1024)S(1)} %get-tuple-element.54, ...), kind=kOutput, calls=%fused_computation.12 | convolution fusion | flops 2324686848 | bytes 20690624 | tf_op jit(solution)/shard_map/dot_general | solution.py:477
  150.6 2.6 fusion.99
  157.3 13.2 %slice.111 = bf16[9664,768]{1,0:T(8,128)(2,1)} slice(bf16[9920,768]{1,0:T(8,128)(2,1)} %shard_map.185), slice={[0:9664], [0:768]} | slice | bytes 29687808 | tf_op jit(solution)/shard_map/slice | solution.py:441
  170.5 25.8 %reshape.338 = bf16[7421952]{0:T(1024)(128)(2,1)} reshape(bf16[9664,768]{1,0:T(8,128)(2,1)} %slice.111) | data formatting | bytes 29687808 | tf_op jit(solution)/shard_map/reshape | solution.py:441
  197.9 23.1 %slice.113 = bf16[28992,256]{1,0:T(8,128)(2,1)} reshape(bf16[9664,768]{1,0:T(8,128)(2,1)} %slice.111) | data formatting | bytes 29687808 | tf_op jit(solution)/shard_map/slice | solution.py:44
  222.3 4.4 fusion.1
  229.6 2.5 multiply_reduce_fusion.2
  234.4 10.4 %convert_reduce_fusion = (f32[3072]{0:T(1024)}, bf16[472,3072]{1,0:T(8,128)(2,1)}) fusion(f32[472,3072]{1,0:T(8,128)} %get-tuple-element.45, bf16[472,768]{1,0:T(8,128)(2,1)S(1)} %get-tuple-element.37, bf16[9920,768]{1,0:T(8,128)(2,1)} %shard_map.185, f32[472,3072]{1,0:T(8,128)} %get-tuple-element.62, f32[3072]{0:T(1024)S(1)} %slice.104), kind=kOutput, calls=%fused_computation.10 | convolution fusion | flops 2251822080 | bytes 19968000 | tf_op jit(solution)/shard_map/td,hd->th/dot_general | solution.py:521
  244.8 5.4 %multiply_reduce_fusion.3 = (f32[768]{0:T(1024)}, f32[472]{0:T(512)S(1)}, f32[768]{0:T(1024)}, f32[472,768]{1,0:T(8,128)S(1)}) fusion(f32[472,768]{1,0:T(8,128)S(1)} %copy-done.7, f32[472]{0:T(512)S(1)} %fusion.78, f32[472]{0:T(512)S(1)} %broadcast_multiply_fusion.1, f32[768]{0:T(1024)S(1)} %get-tuple-element.54, bf16[472,3072]{1,0:T(8,128)(2,1)} %get-tuple-element.80, ...), kind=kOutput, calls=%fused_computation.58 | convolution fusion | flops 2230798336 | bytes 11985280 | tf_op jit(solution)/shard_map/th,dh->td/dot_general | solution.py:526
  256.1 5.8 %multiply_reduce_fusion = (f32[12,472]{1,0:T(8,128)S(1)}, f32[12,472,472]{1,2,0:T(8,128)S(1)}) fusion(f32[12,472,472]{1,2,0:T(8,128)} %get-tuple-element.59, f32[12,472]{1,0:T(8,128)S(1)} %get-tuple-element.58, bf16[472,12,64]{0,2,1:T(8,128)(2,1)S(1)} %bitcast.149, bf16[472,12,64]{0,2,1:T(8,128)(2,1)S(1)} %bitcast.148), kind=kOutput, calls=%fused_computation.4 | convolution fusion | flops 350210784 | bytes 22882560 | tf_op jit(solution)/shard_map/blhe,bmhe->bhlm/dot_general | solution.py:536
  264.1 3.4 multiply_convert_fusion
  285.6 5.0 fusion.23
  290.7 3.5 copy.67
  294.2 3.8 fusion.12
  298.0 4.5 copy.58
  302.5 5.8 %reshape.344 = bf16[1769472]{0:T(1024)(128)(2,1)} reshape(bf16[768,2304]{1,0:T(8,128)(2,1)S(1)} %copy.58) | data formatting | bytes 7077888 | tf_op jit(solution)/shard_map/reshape | solution.py:557
  308.3 3.5 constant_dynamic-update-slice_fusion
  314.6 6.0 %constant_dynamic-update-slice_fusion.6 = bf16[7421952]{0:T(1024)(128)(2,1)} fusion(bf16[7421952]{0:T(1024)(128)(2,1)} %constant_dynamic-update-slice_fusion.7, bf16[2359296]{0:T(1024)(128)(2,1)} %bitcast.129), kind=kLoop, calls=%fused_computation.152 | loop fusion | bytes 9437184
  320.6 4.3 convolution_convert_fusion.1
  325.0 9.2 %reshape.347 = bf16[2359296]{0:T(1024)(128)(2,1)} reshape(bf16[3072,768]{1,0:T(8,128)(2,1)} %convolution_convert_fusion.1) | data formatting | bytes 9437184 | tf_op jit(solution)/shard_map/reshape | solution.py:557
  334.2 5.5 %constant_dynamic-update-slice_fusion.5 = bf16[7421952]{0:T(1024)(128)(2,1)} fusion(bf16[7421952]{0:T(1024)(128)(2,1)} %constant_dynamic-update-slice_fusion.6, bf16[2359296]{0:T(1024)(128)(2,1)} %reshape.347), kind=kLoop, calls=%fused_computation.151 | loop fusion | bytes 9437184
  342.5 25.8 %convert_element_type.131.g_in = bf16[9664,768]{1,0:T(8,128)(2,1)} reshape(bf16[7421952]{0:T(1024)(128)(2,1)} %constant_dynamic-update-slice_fusion.2) | data formatting | bytes 29687808 | tf_op jit(solution)/shard_map/convert_element_type | solution.py:586
  368.3 140.6 %shard_map.186 = (f32[1812,128]{1,0:T(8,128)}, f32[80,128]{1,0:T(8,128)}, f32[8,128]{1,0:T(8,128)}) custom-call(bf16[9664,768]{1,0:T(8,128)(2,1)} %convert_element_type.131.g_in, f32[80,128]{1,0:T(8,128)} %bitcast.158), custom_call_target="tpu_custom_call" | custom-call | tf_op jit(solution)/shard_map/pallas_call | solution.py:408
  514.9 3.8 fusion.87
  518.7 4.4 add_bitcast_fusion
  (244 shorter events, 62.7 us)
Async XLA Ops:
  97.2 53.3 %copy-start.49 = (f32[768]{0:T(1024)}, f32[768]{0:T(1024)S(1)}, u32[]{:S(2)}) copy-start(f32[768]{0:T(1024)S(1)} %get-tuple-element.53) | copy-start | bytes 9220
  109.1 8.7 %copy-start.52 = (bf16[1,472,768]{2,1,0:T(8,128)(2,1)S(1)}, bf16[1,472,768]{2,1,0:T(8,128)(2,1)}, u32[]{:S(2)}) copy-start(bf16[1,472,768]{2,1,0:T(8,128)(2,1)} %param.10) | copy-start | bytes 2174980
  120.2 130.1 %copy-start.45 = (f32[472]{0:T(512)}, f32[472]{0:T(512)S(1)}, u32[]{:S(2)}) copy-start(f32[472]{0:T(512)S(1)} %fusion.78) | copy-start | bytes 5668
  122.6 27.9 %slice-start.4 = ((s8[15237120]{0:T(1024)(128)(4,1)}), s8[2654208]{0:T(1024)(128)(4,1)S(1)}, s32[]{:S(2)}) async-start(s8[15237120]{0:T(1024)(128)(4,1)} %bitcast.125), calls=%async_computation.4 | async-start | bytes 5308416
  131.2 19.3 %slice-start.5 = ((s8[15237120]{0:T(1024)(128)(4,1)}), s8[4194304]{0:T(1024)(128)(4,1)S(1)}, s32[]{:S(2)}) async-start(s8[15237120]{0:T(1024)(128)(4,1)} %bitcast.125), calls=%async_computation.5 | async-start | bytes 8388608
  131.2 19.3 %slice-start.6 = ((s8[15237120]{0:T(1024)(128)(4,1)}), s8[4194304]{0:T(1024)(128)(4,1)S(1)}, s32[]{:S(2)}) async-start(s8[15237120]{0:T(1024)(128)(4,1)} %bitcast.125), calls=%async_computation.6 | async-start | bytes 8388608
  131.2 19.3 %slice-start.7 = ((s8[15237120]{0:T(1024)(128)(4,1)}), s8[4194304]{0:T(1024)(128)(4,1)S(1)}, s32[]{:S(2)}) async-start(s8[15237120]{0:T(1024)(128)(4,1)} %bitcast.125), calls=%async_computation.7 | async-start | bytes 8388608
  131.3 19.3 %copy-start.6 = (f32[472,768]{1,0:T(8,128)S(1)}, f32[472,768]{1,0:T(8,128)}, u32[]{:S(2)}) copy-start(f32[472,768]{1,0:T(8,128)} %copy-done.5) | copy-start | bytes 4349956
  170.5 26.9 %copy-start.51 = (s32[1,232,2]{1,2,0:T(2,128)S(1)}, s32[1,232,2]{1,2,0:T(2,128)}, u32[]{:S(2)}) copy-start(s32[1,232,2]{1,2,0:T(2,128)} %param.13) | copy-start | bytes 5572
  197.9 23.1 %copy-start.35 = (bf16[1,232,2,128]{3,2,1,0:T(2,128)(2,1)}, bf16[1,232,2,128]{3,2,1,0:T(2,128)(2,1)S(1)}, u32[]{:S(2)}) copy-start(bf16[1,232,2,128]{3,2,1,0:T(2,128)(2,1)S(1)} %copy.53) | copy-start | bytes 356356
  197.9 24.4 %copy-start.38 = (s32[1,232,100]{1,0,2:T(1,128)S(1)}, s32[1,232,100]{1,0,2:T(1,128)}, u32[]{:S(2)}) copy-start(s32[1,232,100]{1,0,2:T(1,128)} %param.12) | copy-start | bytes 278404
  197.9 31.6 %copy-start.1 = (f32[472,768]{1,0:T(8,128)S(1)}, f32[472,768]{1,0:T(8,128)}, u32[]{:S(2)}) copy-start(f32[472,768]{1,0:T(8,128)} %copy-done) | copy-start | bytes 4349956
  222.2 11.9 %copy-start.20 = (f32[232,256]{1,0:T(8,128)}, f32[232,256]{1,0:T(8,128)S(1)}, u32[]{:S(2)}) copy-start(f32[232,256]{1,0:T(8,128)S(1)} %get-tuple-element.66) | copy-start | bytes 712708
  222.2 11.9 %copy-start.43 = (f32[232]{0:T(256)}, f32[232]{0:T(256)S(1)}, u32[]{:S(2)}) copy-start(f32[232]{0:T(256)S(1)} %get-tuple-element.81) | copy-start | bytes 2788
  222.3 11.9 %copy-start.44 = (f32[232]{0:T(256)}, f32[232]{0:T(256)S(1)}, u32[]{:S(2)}) copy-start(f32[232]{0:T(256)S(1)} %get-tuple-element.82) | copy-start | bytes 2788
  232.0 12.8 %slice-start.18 = ((s8[4718592]{0:T(1024)(128)(4,1)}), s8[4194304]{0:T(1024)(128)(4,1)S(1)}, s32[]{:S(2)}) async-start(s8[4718592]{0:T(1024)(128)(4,1)} %bitcast.133), calls=%async_computation.18 | async-start | bytes 8388608
  234.4 10.4 %copy-start.27 = (bf16[472,768]{1,0:T(8,128)(2,1)}, bf16[472,768]{1,0:T(8,128)(2,1)S(1)}, u32[]{:S(2)}) copy-start(bf16[472,768]{1,0:T(8,128)(2,1)S(1)} %get-tuple-element.37) | copy-start | bytes 2174980
  234.4 10.4 %copy-start.7 = (f32[472,768]{1,0:T(8,128)S(1)}, f32[472,768]{1,0:T(8,128)}, u32[]{:S(2)}) copy-start(f32[472,768]{1,0:T(8,128)} %copy-done.5) | copy-start | bytes 4349956
  234.4 10.4 %slice-start.19 = ((s8[4718592]{0:T(1024)(128)(4,1)}), s8[524288]{0:T(1024)(128)(4,1)S(1)}, s32[]{:S(2)}) async-start(s8[4718592]{0:T(1024)(128)(4,1)} %bitcast.133), calls=%async_computation.19 | async-start | bytes 1048576
  234.4 18.6 %slice-start.8 = ((s8[15237120]{0:T(1024)(128)(4,1)}), s8[2654208]{0:T(1024)(128)(4,1)S(1)}, s32[]{:S(2)}) async-start(s8[15237120]{0:T(1024)(128)(4,1)} %bitcast.127), calls=%async_computation.8 | async-start | bytes 5308416
  234.4 18.6 %slice-start.9 = ((s8[15237120]{0:T(1024)(128)(4,1)}), s8[4194304]{0:T(1024)(128)(4,1)S(1)}, s32[]{:S(2)}) async-start(s8[15237120]{0:T(1024)(128)(4,1)} %bitcast.127), calls=%async_computation.9 | async-start | bytes 8388608
  234.4 18.6 %slice-start.10 = ((s8[15237120]{0:T(1024)(128)(4,1)}), s8[4194304]{0:T(1024)(128)(4,1)S(1)}, s32[]{:S(2)}) async-start(s8[15237120]{0:T(1024)(128)(4,1)} %bitcast.127), calls=%async_computation.10 | async-start | bytes 8388608
  268.6 25.5 %copy-start.14 = (bf16[12,64,472]{2,1,0:T(8,128)(2,1)}, bf16[12,64,472]{2,1,0:T(8,128)(2,1)S(1)}, u32[]{:S(2)}) copy-start(bf16[12,64,472]{2,1,0:T(8,128)(2,1)S(1)} %multiply_convert_fusion.3) | copy-start | bytes 2174980
  270.5 23.7 %copy-start.16 = (bf16[12,64,472]{2,1,0:T(8,128)(2,1)}, bf16[12,64,472]{2,1,0:T(8,128)(2,1)S(1)}, u32[]{:S(2)}) copy-start(bf16[12,64,472]{2,1,0:T(8,128)(2,1)S(1)} %multiply_convert_fusion.2) | copy-start | bytes 2174980
  272.3 10.8 %slice-start.14 = ((bf16[28992,256]{1,0:T(8,128)(2,1)}), bf16[256,256]{1,0:T(8,128)(2,1)S(1)}, s32[]{:S(2)}) async-start(bf16[28992,256]{1,0:T(8,128)(2,1)} %slice.113), calls=%async_computation.14 | async-start | bytes 262144 | tf_op jit(solution)/shard_map/slice | solution.py:44
  368.3 144.9 %copy-start.37 = (f32[9728]{0:T(1024)S(1)}, f32[9728]{0:T(1024)}, u32[]{:S(2)}) copy-start(f32[9728]{0:T(1024)} %param.17) | copy-start | bytes 116740
  368.3 144.9 %copy-start.40 = (f32[9728]{0:T(1024)S(1)}, f32[9728]{0:T(1024)}, u32[]{:S(2)}) copy-start(f32[9728]{0:T(1024)} %param.18) | copy-start | bytes 116740
  368.3 144.9 %copy-start.41 = (f32[9728]{0:T(1024)S(1)}, f32[9728]{0:T(1024)}, u32[]{:S(2)}) copy-start(f32[9728]{0:T(1024)} %param.19) | copy-start | bytes 116740
  368.3 146.5 %copy-start.8 = (f32[231936]{0:T(1024)S(1)}, f32[231936]{0:T(1024)}, u32[]{:S(2)}) copy-start(f32[231936]{0:T(1024)} %param.14) | copy-start | bytes 2783236
  509.0 9.7 %copy-start.4 = (f32[472,768]{1,0:T(8,128)S(1)}, f32[472,768]{1,0:T(8,128)}, u32[]{:S(2)}) copy-start(f32[472,768]{1,0:T(8,128)} %copy-done.3) | copy-start | bytes 4349956
  509.0 9.7 %copy-start.15 = (bf16[12,64,472]{2,1,0:T(8,128)(2,1)S(1)}, bf16[12,64,472]{2,1,0:T(8,128)(2,1)}, u32[]{:S(2)}) copy-start(bf16[12,64,472]{2,1,0:T(8,128)(2,1)} %copy-done.14) | copy-start | bytes 2174980
  509.0 9.7 %copy-start.47 = (f32[472]{0:T(512)S(1)}, f32[472]{0:T(512)}, u32[]{:S(2)}) copy-start(f32[472]{0:T(512)} %copy-done.46) | copy-start | bytes 5668
  (47 other events, 219.6 us)

commit v2 on v0

--- a/solution.py
+++ b/solution.py
@@ -1,20 +1,217 @@
-from functools import partial
+import functools
 
 import jax
 import jax.numpy as jnp
 from jax import lax
+from jax.experimental import pallas as pl
+from jax.experimental.pallas import tpu as pltpu
 from jax.sharding import PartitionSpec as P
-
-D = 768
-H = 12
-HD = 64
-FF = 3072
-FINAL = 256
-G = 2
-V = 320
-CD = 128
-LEN = 472
-MASKED = 232
+D = 768; H = 12; HD = 64; FF = 3072; FINAL = 256; G = 2; V = 320; CD = 128; LEN = 472; MASKED = 232
+NROW = 9664; GROW = NROW + 256
+T = 512
+LT = 480
+bf16 = jnp.bfloat16
+f32 = jnp.float32
+NT = (((1,), (1,)), ((), ()))
+BQ, BV, BO, G1, S1, BUP, BDOWN, G2, S2, BPROJ, BCODE = [768 * i for i in range(6)] + [3840 + 3072 + 768 * i for i in range(3)] + [9216, 9472]
+
+def mm(a, b):
+    return jnp.dot(a, b, preferred_element_type=f32)
+
+def mm_nt(a, b, precision=None):
+    return lax.dot_general(a, b, NT, preferred_element_type=f32, precision=precision)
+
+def hi(a, b):
+    return jnp.dot(a, b, preferred_element_type=f32, precision=lax.Precision.HIGHEST)
+
+def split_rows(g, base, parts, nice, first, tmp):
+    def body(b, _):
+        src = pl.multiple_of(base + b * 64 * parts, 64)
+        for j in range(6):
+            tmp[j, 0:64 * parts, :] = g[pl.ds(src, 64 * parts), 128 * j:128 * j + 128].astype(f32)
+        for t in range(parts):
+            at = pl.multiple_of((first + t) * D + b * 64, 64)
+            for j in range(6):
+                nice[pl.ds(at, 64), 128 * j:128 * j + 128] = tmp[j, pl.ds(t, 64, stride=parts), :].astype(bf16)
+        return 0
+    lax.fori_loop(0, D // 64, body, 0)
+
+def norm_rows(r, gain, shift, low, wide, hat, rstd):
+    def body(b, _):
+        at = pl.multiple_of(b * 48, 16)
+        v = r[pl.ds(at, 48), :]
+        m = jnp.mean(v, axis=-1, keepdims=True)
+        c = v - m
+        var = jnp.mean(c * c, axis=-1, keepdims=True)
+        inv = lax.rsqrt(var + eps_norm)
+        xh = c * inv
+        o = xh * gain + shift
+        hat[pl.ds(at, 48), :] = xh
+        rstd[pl.ds(at, 48), :] = jnp.broadcast_to(inv, (48, 128))
+        if wide is not None:
+            wide[pl.ds(at, 48), :] = o
+        low[pl.ds(at, 48), :] = o.astype(bf16)
+        return 0
+    lax.fori_loop(0, LT // 48, body, 0)
+
+def transpose_to(src, dst, rows, cols):
+    def body(n, _):
+        at = pl.multiple_of(n * 128, 128)
+        dst[pl.ds(at, 128), :] = src[:, pl.ds(at, 128)].T
+        return 0
+    lax.fori_loop(0, cols // 128, body, 0)
+
+def prepare(x_ref, xp, xT, mask_ref, distract_ref, choice_ref, vec_ref, vec, place, placeT, allowed, choose):
+    for i in range(vec_ref.shape[0]):
+        vec[0:1, 128 * i:128 * i + 128] = vec_ref[i:i + 1, :]
+    xp[...] = jnp.zeros((T, D), bf16)
+    xp[0:LEN, :] = x_ref[0]
+    transpose_to(xp, xT, T, D)
+    zero = jnp.zeros((1, 256 - MASKED), jnp.int32) - 1
+    def wide(row):
+        return jnp.concatenate([row, zero], axis=1)
+    hot = jnp.where(lax.broadcasted_iota(jnp.int32, (T, 256), 0) == wide(mask_ref[...]), 1.0, 0.0)
+    placeT[...] = hot.astype(bf16)
+    place[...] = hot.T.astype(bf16)
+    row = lax.broadcasted_iota(jnp.int32, (256, 256), 0)
+    col = lax.broadcasted_iota(jnp.int32, (256, 256), 1)
+    allowed[...] = jnp.where((row == col) & (col < MASKED), 1.0, 0.0)
+    rows = [wide(distract_ref[i]) for i in range(distract_ref.shape[0])]
+    def body(b, _):
+        at = pl.multiple_of(8 * b, 8)
+        acc = allowed[pl.ds(at, 8), :]
+        n = lax.broadcasted_iota(jnp.int32, (8, 256), 0) + at
+        for r in rows:
+            acc = jnp.where(n == r, 1.0, acc)
+        allowed[pl.ds(at, 8), :] = acc
+        return 0
+    lax.fori_loop(0, MASKED // 8, body, 0)
+    allowed[...] = allowed[...].T
+    for g in range(2):
+        v = jnp.where(lax.broadcasted_iota(jnp.int32, (384, 256), 0) == wide(choice_ref[0, g:g + 1, :]), 1.0, 0.0)
+        choose[g] = v.T
+
+def project(xp, nice, vec, q, kk, kT, vv, vT):
+    for t, (dst, bias) in enumerate(((q, BQ), (kk, None), (vv, BV))):
+        for n in range(3):
+            acc = mm(xp[...], nice[t * D:(t + 1) * D, 256 * n:256 * n + 256])
+            if bias is not None:
+                acc = acc + vec[0:1, bias + 256 * n:bias + 256 * n + 256]
+            dst[:, 256 * n:256 * n + 256] = acc.astype(bf16)
+    transpose_to(kk, kT, T, D)
+    transpose_to(vv, vT, T, D)
+
+def attend(p, q, kk, vT, pT, attT):
+    at = pl.multiple_of(128 * p, 128)
+    qp = q[:, pl.ds(at, 128)]
+    kp = kk[0:LT, pl.ds(at, 128)]
+    lane = lax.broadcasted_iota(jnp.int32, (LT, 128), 1)
+    for h in range(2):
+        kh = jnp.where((lane < 64) == (h == 0), kp, jnp.zeros_like(kp))
+        s = mm_nt(kh, qp)[0:LEN] * 0.125
+        e = jnp.exp(s - jnp.max(s, axis=0, keepdims=True))
+        pr = e * (1.0 / jnp.sum(e, axis=0, keepdims=True))
+        pr = jnp.concatenate([pr, jnp.zeros((T - LEN, T), f32)], axis=0).astype(bf16)
+        pT[pl.ds(pl.multiple_of((2 * (p % 2) + h) * T, T), T), :] = pr
+        rows = pl.ds(pl.multiple_of(128 * p + 64 * h, 64), 64)
+        attT[rows, :] = mm(vT[rows, :], pr).astype(bf16)
+
+def out_project(attT, att, xp, wo, vec, res):
+    for n in range(6):
+        att[:, 128 * n:128 * n + 128] = attT[128 * n:128 * n + 128, :].T
+    for n in range(3):
+        cols = slice(256 * n, 256 * n + 256)
+        acc = mm(att[0:LT, :], wo[:, cols])
+        res[:, cols] = xp[0:LT, cols].astype(f32) + acc + vec[0:1, BO + 256 * n:BO + 256 * n + 256]
+
+def up(n, norm_low, nice, vec, act, gp):
+    root = 0.7071067811865476
+    scale = 0.3989422804014327
+    c = n // 3
+    w = nice[pl.ds(pl.multiple_of(c * D, D), D), pl.ds(pl.multiple_of((n - 3 * c) * 256, 256), 256)]
+    at = pl.multiple_of(n * 256, 256)
+    h = mm(norm_low[0:LT, :], w) + vec[0:1, pl.ds(pl.multiple_of(BUP + n * 256, 256), 256)]
+    cdf = 0.5 * (1.0 + lax.erf(h * root))
+    act[0:LT, pl.ds(at, 256)] = (h * cdf).astype(bf16)
+    gp[0:LT, pl.ds(at, 256)] = (cdf + h * (scale * jnp.exp(-0.5 * h * h))).astype(bf16)
+
+def down(act, g, vec, res, wide):
+    for n in range(3):
+        cols = slice(256 * n, 256 * n + 256)
+        acc = mm(act[0:LT, :], g[6144:9216, cols])
+        res[:, cols] = wide[:, cols] + acc + vec[0:1, BDOWN + 256 * n:BDOWN + 256 * n + 256]
+
+def small_weights(g, fb, p32, c32, wproj, code, wcode):
+    for t in range(3):
+        for j in range(2):
+            p32[j, pl.ds(t, 256, stride=3), :] = g[9216:9472, 256 * t + 128 * j:256 * t + 128 * j + 128].astype(f32)
+    for j in range(2):
+        wproj[:, 128 * j:128 * j + 128] = p32[j].astype(bf16)
+    for j in range(6):
+        fb[pl.ds(j, 192, stride=6), :] = g[9472:9664, 128 * j:128 * j + 128].astype(f32)
+    a = [fb[pl.ds(j, 128, stride=5), :] for j in range(5)]
+    lo = lax.broadcasted_iota(jnp.int32, (128, 128), 1) < 64
+    r2, r3, r4 = [pltpu.roll(v, 64, 1) for v in a[2:]]
+    zero = jnp.zeros((128, 128), f32)
+    even = [a[0], a[1], jnp.where(lo, a[2], zero)]
+    odd = [jnp.where(lo, r2, r3), jnp.where(lo, r3, r4), jnp.where(lo, r4, zero)]
+    for j in range(3):
+        c32[j, pl.ds(0, 128, stride=2), :] = even[j]
+        c32[j, pl.ds(1, 128, stride=2), :] = odd[j]
+        code[:, 128 * j:128 * j + 128] = c32[j].astype(bf16)
+    for j in range(2):
+        wcode[:, 128 * j:128 * j + 128] = fb[pl.ds(640 + j, 256, stride=2), :].astype(bf16)
+
+def contrast(weight, out_low, vec, place, placeT, allowed, choose, wproj, code, wcode, fb, p32, c32, tail, dctx, small):
+    picked = mm(place[...], out_low[...]).astype(bf16)
+    chosen = mm(picked, wproj[...]) + vec[0:1, BPROJ:BPROJ + 256]
+    cv = jnp.concatenate([mm_nt(choose[g].astype(bf16), code[128 * g:128 * g + 128, :]) for g in range(2)], axis=1).astype(bf16)
+    targets = mm(cv, wcode[...]) + vec[0:1, BCODE:BCODE + 256]
+    n_l = lax.rsqrt(jnp.sum(chosen * chosen, axis=1, keepdims=True) + eps_cos)
+    n_r = lax.rsqrt(jnp.sum(targets * targets, axis=1, keepdims=True) + eps_cos)
+    left = chosen * n_l
+    right = targets * n_r
+    sim = mm_nt(left, right, lax.Precision.HIGHEST) / 0.1
+    ok = allowed[...] > 0.5
+    row = lax.broadcasted_iota(jnp.int32, (256, 256), 0)
+    col = lax.broadcasted_iota(jnp.int32, (256, 256), 1)
+    eye = jnp.where((row == col) & (row < MASKED), 1.0, 0.0)
+    pos = jnp.sum(eye * sim, axis=1, keepdims=True)
+    top = jnp.max(jnp.where(ok, sim, -1e30), axis=1, keepdims=True)
+    parts = jnp.where(ok, jnp.exp(jnp.minimum(sim - top, 0.0)), 0.0)
+    real = lax.broadcasted_iota(jnp.int32, (256, 1), 0) < MASKED
+    total = jnp.where(real, jnp.sum(parts, axis=1, keepdims=True), 1.0)
+    loss = jnp.sum(jnp.where(real, top + jnp.log(total) - pos, 0.0))
+    dsim = (weight / 0.1) * (parts / total - eye)
+    dl = hi(dsim, right)
+    dr = hi(dsim.T, left)
+    d_chosen = (n_l * dl - chosen * (n_l * n_l * n_l) * jnp.sum(chosen * dl, axis=1, keepdims=True)).astype(bf16)
+    d_target = (n_r * dr - targets * (n_r * n_r * n_r) * jnp.sum(targets * dr, axis=1, keepdims=True)).astype(bf16)
+    small[0:1, :] = jnp.sum(d_chosen.astype(f32), axis=0, keepdims=True)
+    small[1:2, :] = jnp.sum(d_target.astype(f32), axis=0, keepdims=True)
+    small[2:3, :] = jnp.broadcast_to(loss, (1, 256))
+    dctx[...] = mm(placeT[...], d_chosen).astype(bf16)
+    dproj = mm(picked.T, d_chosen)
+    for j in range(2):
+        p32[j] = dproj[:, 128 * j:128 * j + 128]
+    for t in range(3):
+        for j in range(2):
+            tail[0:256, 256 * t + 128 * j:256 * t + 128 * j + 128] = p32[j, pl.ds(t, 256, stride=3), :].astype(bf16)
+    dwcode = mm(cv.T, d_target)
+    dcv = mm_nt(d_target, wcode[...])
+    for g in range(2):
+        dc = hi(dcv[:, 128 * g:128 * g + 128].T, choose[g])
+        for j in range(3):
+            c32[j, 128 * g:128 * g + 128, :] = dc[:, 128 * j:128 * j + 128]
+    e = [c32[j, pl.ds(0, 128, stride=2), :] for j in range(3)]
+    o = [pltpu.roll(c32[j, pl.ds(1, 128, stride=2), :], 64, 1) for j in range(3)]
+    lo = lax.broadcasted_iota(jnp.int32, (128, 128), 1) < 64
+    for j, v in enumerate((e[0], e[1], jnp.where(lo, e[2], o[0]), jnp.where(lo, o[0], o[1]), jnp.where(lo, o[1], o[2]))):
+        fb[pl.ds(j, 128, stride=5), :] = v
+    for j in range(2):
+        fb[pl.ds(640 + j, 256, stride=2), :] = dwcode[:, 128 * j:128 * j + 128]
+    for j in range(6):
+        tail[256:448, 128 * j:128 * j + 128] = fb[pl.ds(j, 192, stride=6), :].astype(bf16)
 STEP = 10
 
 
@@ -30,6 +227,731 @@
 clip_level = 0.001
 
 
+def sum8(v):
+    r, n = v.shape
+    return jnp.sum(v.reshape(r // 8, 8, n), axis=0)
+
+def norm_back_first(dctx, wproj, gain, hat, rstd, low, acc):
+    acc[...] = jnp.zeros((24, D), f32)
+    def body(b, _):
+        at = pl.multiple_of(b * 48, 16)
+        dy = mm_nt(dctx[pl.ds(at, 48), :], wproj[...])
+        norm_back_rows(dy, at, gain, hat, hat, rstd, low, acc)
+        return 0
+    lax.fori_loop(0, LT // 48, body, 0)
+
+def norm_back_rows(dy, at, gain, hat, dst, rstd, low, acc):
+    xh = hat[pl.ds(at, 48), :]
+    inv = rstd[pl.ds(at, 48), 0:1]
+    a = dy * gain
+    m1 = jnp.mean(a, axis=-1, keepdims=True)
+    m2 = jnp.mean(a * xh, axis=-1, keepdims=True)
+    dr = inv * (a - m1 - xh * m2)
+    lo = dr.astype(bf16)
+    dst[pl.ds(at, 48), :] = dr
+    low[pl.ds(at, 48), :] = lo
+    acc[0:8, :] += sum8(dy * xh)
+    acc[8:16, :] += sum8(dy)
+    acc[16:24, :] += sum8(lo.astype(f32))
+
+def norm_back(dy, gain, hat, rstd, low, acc):
+    acc[...] = jnp.zeros((24, D), f32)
+    def body(b, _):
+        at = pl.multiple_of(b * 48, 16)
+        norm_back_rows(dy[pl.ds(at, 48), :], at, gain, hat, hat, rstd, low, acc)
+        return 0
+    lax.fori_loop(0, LT // 48, body, 0)
+
+def put_vec(vg, acc, offsets):
+    for i, o in enumerate(offsets):
+        vg[0:1, o:o + D] = jnp.sum(acc[8 * i:8 * i + 8, :], axis=0, keepdims=True)
+
+def down_back(n, low2, gg, actT, gp, vg):
+    at = pl.multiple_of(n * 256, 256)
+    rows = pl.ds(pl.multiple_of(6144 + n * 256, 256), 256)
+    d = mm_nt(low2[0:LT, :], gg[rows, :]) * gp[0:LT, pl.ds(at, 256)].astype(f32)
+    d = d.astype(bf16)
+    gp[0:LT, pl.ds(at, 256)] = d
+    vg[0:1, pl.ds(pl.multiple_of(BUP + at, 128), 256)] = jnp.sum(d.astype(f32), axis=0, keepdims=True)
+    gg[rows, :] = mm(actT[pl.ds(at, 256), :], low2[...]).astype(bf16)
+
+def up_back_x(n, dh, gg, dr):
+    cols = pl.ds(pl.multiple_of(n * 256, 256), 256)
+    v = dr[:, cols]
+    for c in range(4):
+        w = gg[pl.ds(pl.multiple_of(3072 + c * D + n * 256, 256), 256), :]
+        v = v + mm_nt(dh[0:LT, c * D:(c + 1) * D], w)
+    dr[:, cols] = v
+
+def weave(lhsT, rhs, parts, n, base, gg, tmp, stacked):
+    def body(m, _):
+        cols = pl.ds(pl.multiple_of(m * 256, 256), 256)
+        for t in range(parts):
+            r = rhs[t, :, cols] if stacked else rhs[:, pl.ds(pl.multiple_of(t * D + m * 256, 256), 256)]
+            acc = mm(lhsT[pl.ds(pl.multiple_of(n * 256, 256), 256), :], r)
+            for j in range(2):
+                tmp[j, pl.ds(t, 256, stride=parts), :] = acc[:, 128 * j:128 * j + 128]
+        for j in range(2):
+            gg[pl.ds(pl.multiple_of(base + n * 256 * parts, 256), 256 * parts), pl.ds(pl.multiple_of(m * 256 + 128 * j, 128), 128)] = tmp[j, 0:256 * parts, :].astype(bf16)
+        return 0
+    lax.fori_loop(0, 3, body, 0)
+
+def out_back(low1, gg, attT, da):
+    for n in range(3):
+        cols = slice(256 * n, 256 * n + 256)
+        da[0:LT, cols] = mm_nt(low1[0:LT, :], gg[2304 + 256 * n:2304 + 256 * n + 256, :]).astype(bf16)
+    for n in range(3):
+        gg[2304 + 256 * n:2304 + 256 * n + 256, :] = mm(attT[256 * n:256 * n + 256, :], low1[...]).astype(bf16)
+
+def attend_back(p, da, q, kT, vv, ring, dp, dqT):
+    at = pl.multiple_of(128 * p, 128)
+    lane = lax.broadcasted_iota(jnp.int32, (T, 128), 1)
+    dap = da[:, pl.ds(at, 128)]
+    qp = q[:, pl.ds(at, 128)]
+    vp = vv[0:LT, pl.ds(at, 128)]
+    dk = dv = None
+    for h in range(2):
+        half = (lane < 64) == (h == 0)
+        dah = jnp.where(half, dap, jnp.zeros_like(dap))
+        qh = jnp.where(half, qp, jnp.zeros_like(qp))
+        pr = ring[pl.ds(pl.multiple_of(((2 * p + h) % 6) * T, T), LT), :]
+        dpT = mm_nt(vp, dah)
+        prf = pr.astype(f32)
+        w = prf * dpT
+        ds = (w - prf * jnp.sum(w, axis=0, keepdims=True)).astype(bf16)
+        a = mm(pr, dah)
+        b = mm(ds, qh)
+        dv = a if dv is None else dv + a
+        dk = b if dk is None else dk + b
+        rows = pl.ds(pl.multiple_of(128 * p + 64 * h, 64), 64)
+        dqT[rows, :] = (mm(kT[rows, 0:LT], ds) * 0.125).astype(bf16)
+    dp[1, 0:LT, pl.ds(at, 128)] = (dk * 0.125).astype(bf16)
+    dp[2, 0:LT, pl.ds(at, 128)] = dv.astype(bf16)
+    dp[0, :, pl.ds(at, 128)] = dqT[pl.ds(at, 128), :].T
+
+def input_back(n, dp, wq, dr, out):
+    cols = slice(256 * n, 256 * n + 256)
+    v = dr[:, cols]
+    for t in range(3):
+        v = v + mm_nt(dp[t, 0:LT, :], wq[t * D + 256 * n:t * D + 256 * n + 256, :])
+    out[0, :, cols] = v[0:LEN]
+MESH = pl.DeviceIdType.MESH
+UP, DOWN, U, V_AXIS, CORE, HERE = range(6)
+PLANES = 4
+MAIN = 288
+EXTRA = 16
+HALF = MAIN + EXTRA
+PLANE = 2416
+UNIT = 608
+
+class Place:
+    def __init__(self):
+        self.z = lax.axis_index("dp")
+        self.f = f = lax.axis_index("fsdp")
+        self.c = c = f % 2
+        self.k = k = f // 2
+        x = k % 2
+        y = k // 2
+        self.fc = f + 1 - 2 * c
+        self.fx = f + 2 - 4 * x
+        self.fy = f + 4 - 8 * y
+        self.uf = self.fx * (1 - c) + self.fy * c
+        self.vf = self.fy * (1 - c) + self.fx * c
+        self.roles = (k, self.uf // 2, self.vf // 2, 3 - k)
+
+    def greet(self):
+        z = self.z
+        bar = pltpu.get_barrier_semaphore()
+        for t in (self.fc, self.fx, self.fy):
+            pl.semaphore_signal(bar, inc=1, device_id=(z, t), device_id_type=MESH)
+        @pl.when(z > 0)
+        def _(): pl.semaphore_signal(bar, inc=1, device_id=(z - 1, self.f), device_id_type=MESH)
+        @pl.when(z < PLANES - 1)
+        def _(): pl.semaphore_signal(bar, inc=1, device_id=(z + 1, self.f), device_id_type=MESH)
+        pl.semaphore_wait(bar, 3 + (z + PLANES - 1) // PLANES + (2 * PLANES - 2 - z) // PLANES)
+
+    def greet_all(self, count):
+        bar = pltpu.get_barrier_semaphore()
+        for j in range(1, count):
+            pl.semaphore_signal(bar, inc=1, device_id=(self.z, lax.rem(self.f + j, count)), device_id_type=MESH)
+        for j in range(1, PLANES):
+            pl.semaphore_signal(bar, inc=1, device_id=(lax.rem(self.z + j, PLANES), self.f), device_id_type=MESH)
+        pl.semaphore_wait(bar, count + PLANES - 2)
+
+    def span(self, p, r, c, first):
+        kk = self.roles[r]
+        m = PLANE * p + UNIT * kk
+        return (pl.multiple_of(m + HALF * c + first, 16),
+                pl.multiple_of((m + MAIN) * (1 - c) + (NROW + EXTRA * (4 * p + kk)) * c, 16))
+
+def remote(src, dst, ssem, rsem, dev):
+    return pltpu.make_async_remote_copy(src_ref=src, dst_ref=dst, send_sem=ssem, recv_sem=rsem, device_id=dev, device_id_type=MESH)
+
+def shared_blocks(g, p, out):
+    row = lax.broadcasted_iota(jnp.int32, (16, D), 0)
+    if out:
+        b = [g[PLANE * p + 16 * q:PLANE * p + 16 * q + 16, :].astype(f32) for q in (37, 75, 113)]
+        for q, v in enumerate((b[0], jnp.where(row < 8, b[1], b[0]), jnp.where(row < 4, b[2], b[1]), b[2])):
+            g[NROW + 16 * (4 * p + q):NROW + 16 * (4 * p + q) + 16, :] = v.astype(bf16)
+    else:
+        e = [g[NROW + 16 * (4 * p + q):NROW + 16 * (4 * p + q) + 16, :].astype(f32) for q in range(4)]
+        for q, bound in enumerate((12, 8, 4)):
+            at = PLANE * p + UNIT * q + 592
+            g[at:at + 16, :] = jnp.where(row < bound, e[q], e[q + 1]).astype(bf16)
+
+class Gather:
+    def __init__(self, at, g, pieces, R, O, S):
+        self.at, self.g, self.pieces, self.R, self.O, self.S = at, g, pieces, R, O, S
+        self.index = {}
+        self.made = {z: [] for z in range(PLANES)}
+        self.seen = set()
+
+    def sem(self, key):
+        return self.S.at[self.index.setdefault(key, len(self.index))]
+
+    def copies(self, i, p, r, dev, kind, c):
+        _, first, rows, extra = self.pieces[p][i]
+        a, e = self.at.span(p, r, c, first)
+        unit = 4 * p + self.at.roles[r]
+        got = self.O if kind == CORE else self.R
+        out = []
+        for j, (s, n) in enumerate([(a, rows)] + [(e, EXTRA)] * extra):
+            ref = self.g.at[pl.ds(s, n)]
+            out.append(remote(ref, ref, self.sem((kind, i, p, r, j)), got.at[unit, i + j], dev))
+        return out
+
+    def op(self, zs, kind, i, p, r):
+        at = self.at
+        if not (p == zs and r == 0) and (zs, i, p, r) not in self.seen:
+            self.seen.add((zs, i, p, r))
+            for q in self.copies(i, p, r, (zs, at.fc), HERE, at.c): q.wait_recv()
+        dev = ((zs + 1, at.f), (zs - 1, at.f), (zs, at.uf), (zs, at.vf), (zs, at.fc))[kind]
+        for q in self.copies(i, p, r, dev, kind, at.c): q.start()
+        self.made[zs].append((kind, i, p, r))
+
+    def other_core(self, zs, p):
+        for r in range(4):
+            if p == zs and r == 0: continue
+            for i in range(len(self.pieces[p])):
+                for q in self.copies(i, p, r, (zs, self.at.fc), CORE, 1 - self.at.c): q.wait_recv()
+
+    def drain(self):
+        for zs in range(PLANES):
+            @pl.when(self.at.z == zs)
+            def _():
+                for kind, i, p, r in self.made[zs]:
+                    for q in self.copies(i, p, r, (zs, self.at.fc), kind, self.at.c): q.wait_send()
+
+def own_rows(at, g, p_ref, raw, land, sem):
+    n = p_ref.shape[0]
+    copy = remote(p_ref.at[pl.ds(0, n)], land.at[pl.ds(0, n)], sem.at[0], sem.at[1], (at.z, at.fc))
+    copy.start()
+    @pl.when(at.c == 0)
+    def _(): raw[96:96 + n, :] = p_ref[...]
+    @pl.when(at.c == 1)
+    def _(): raw[96 + n:96 + 2 * n, :] = p_ref[...]
+    copy.wait()
+    @pl.when(at.c == 1)
+    def _(): raw[96:96 + n, :] = land[0:n]
+    @pl.when(at.c == 0)
+    def _(): raw[96 + n:96 + 2 * n, :] = land[0:n]
+    k = at.k
+    own = pl.multiple_of(PLANE * at.z + UNIT * k, 16)
+    extra = pl.multiple_of(NROW + EXTRA * (4 * at.z + k), 16)
+    row = lax.broadcasted_iota(jnp.int32, (16, 128), 0)
+    for j in range(6):
+        cols = slice(128 * j, 128 * j + 128)
+        g[pl.ds(own, 592), cols] = raw[pl.ds(96 + 24 * k + j, 592, stride=6), :].astype(bf16)
+        last = raw[pl.ds(96 + (592 + 4 * k) * 6 + j, 16, stride=6), :]
+        first = raw[pl.ds(24 * k + j, 16, stride=6), :]
+        g[pl.ds(extra, 16), cols] = jnp.where(row < 12 - 4 * k, last, first).astype(bf16)
+
+K1_OUT = ("w", "wproj", "tail", "dctx", "small", "hat1", "r1", "hat2", "r2", "gp", "actT", "normT", "attT", "q", "kT", "vv", "xT", "pT")
+K1_SHAPE = {"w": ((NROW, D), bf16), "wproj": ((D, 256), bf16), "tail": ((448, D), bf16), "dctx": ((T, 256), bf16), "small": ((8, 256), f32),
+            "hat1": ((LT, D), f32), "r1": ((LT, 128), f32), "hat2": ((LT, D), f32), "r2": ((LT, 128), f32), "gp": ((T, FF), bf16), "actT": ((FF, T), bf16),
+            "normT": ((D, T), bf16), "attT": ((D, T), bf16), "q": ((T, D), bf16), "kT": ((D, T), bf16), "vv": ((T, D), bf16), "xT": ((D, T), bf16),
+            "pT": ((H * T, T), bf16)}
+
+def forward_kernel(pieces, events, weight, p_ref, x, mask, dis, cho, vec_ref, *rest):
+    n_out = len(K1_OUT)
+    hbm = dict(zip(K1_OUT, rest[:n_out]))
+    (out, vec, g, raw, land, nice, tmp, wproj, tail, dctx, small, hat1, r1, hat2, r2, gp, actT, normT, attT, q, kT, vv, xT, pT,
+     xp, kk, vT, act, res, wide, low1, low2, place, placeT, allowed, choose, fb, p32, c32, code, wcode,
+     sem_raw, R, O, S, OS, PS) = rest[n_out:]
+    here = dict(wproj=wproj, tail=tail, dctx=dctx, small=small, hat1=hat1, r1=r1, hat2=hat2, r2=r2, gp=gp, actT=actT, normT=normT, attT=attT, q=q, kT=kT, vv=vv, xT=xT, pT=pT)
+    outs = []
+    count = iter(range(32))
+    def put(src, dst):
+        cp = pltpu.make_async_copy(src, dst, OS.at[next(count)])
+        cp.start()
+        outs.append(cp)
+    def save(*names):
+        for n in names: put(here[n], hbm[n])
+    at = Place()
+    ga = Gather(at, g, pieces, R, O, S)
+    at.greet()
+    own_rows(at, g, p_ref, raw, land, sem_raw)
+    def slot(i, cond=None):
+        for zs in range(PLANES):
+            if events[zs][i]:
+                @pl.when((at.z == zs) if cond is None else ((at.z == zs) & cond))
+                def _():
+                    for e in events[zs][i]: ga.op(zs, *e)
+    def plane(p):
+        for zs in range(PLANES):
+            @pl.when(at.z == zs)
+            def _(): ga.other_core(zs, p)
+        shared_blocks(g, p, False)
+    slot(0)
+    prepare(x, xp, xT, mask, dis, cho, vec_ref, vec, place, placeT, allowed, choose)
+    act[LT:T, :] = jnp.zeros((T - LT, FF), bf16)
+    gp[LT:T, :] = jnp.zeros((T - LT, FF), bf16)
+    low1[...] = jnp.zeros((T, D), bf16)
+    low2[...] = jnp.zeros((T, D), bf16)
+    small[...] = jnp.zeros((8, 256), f32)
+    save("xT")
+    slot(1)
+    plane(0)
+    split_rows(g, 0, 3, nice, 0, tmp)
+    slot(2)
+    project(xp, nice, vec, q, kk, kT, vv, vT)
+    save("q", "kT", "vv")
+    put(nice.at[pl.ds(0, 2304)], hbm["w"].at[pl.ds(0, 2304)])
+    nice_out = outs.pop()
+    slot(3)
+    slot(4)
+    def pair_out(p):
+        b = p % 2
+        return pltpu.make_async_copy(pT.at[pl.ds(pl.multiple_of(2 * T * b, T), 2 * T)], hbm["pT"].at[pl.ds(pl.multiple_of(2 * T * p, T), 2 * T)], PS.at[b])
+    def pair(p, _):
+        @pl.when(p >= 2)
+        def _(): pair_out(p - 2).wait()
+        attend(p, q, kk, vT, pT, attT)
+        pair_out(p).start()
+        for i in range(6): slot(5 + i, p == i)
+        return 0
+    lax.fori_loop(0, H // 2, pair, 0)
+    pair_out(H // 2 - 2).wait()
+    pair_out(H // 2 - 1).wait()
+    save("attT")
+    plane(1)
+    out_project(attT, kk, xp, g.at[2304:3072], vec, res)
+    put(g.at[pl.ds(2304, 768)], hbm["w"].at[pl.ds(2304, 768)])
+    norm_rows(res, vec[0:1, G1:G1 + D], vec[0:1, S1:S1 + D], low1, wide, hat1, r1)
+    save("hat1", "r1")
+    transpose_to(low1, normT, T, D)
+    save("normT")
+    slot(11)
+    plane(2)
+    nice_out.wait()
+    split_rows(g, 3072, 4, nice, 0, tmp)
+    put(nice, hbm["w"].at[pl.ds(3072, 3072)])
+    slot(12)
+    def tile(n, _):
+        up(n, low1, nice, vec, act, gp)
+        for i in range(3): slot(13 + i, n == 3 * i + 2)
+        return 0
+    lax.fori_loop(0, 12, tile, 0)
+    slot(16)
+    save("gp")
+    transpose_to(act, actT, T, FF)
+    save("actT")
+    slot(17)
+    plane(3)
+    put(g.at[pl.ds(6144, 3072)], hbm["w"].at[pl.ds(6144, 3072)])
+    down(act, g, vec, res, wide)
+    norm_rows(res, vec[0:1, G2:G2 + D], vec[0:1, S2:S2 + D], low2, None, hat2, r2)
+    save("hat2", "r2")
+    out[0] = low2[0:LEN, :]
+    small_weights(g, fb, p32, c32, wproj, code, wcode)
+    save("wproj")
+    slot(18)
+    contrast(weight, low2, vec, place, placeT, allowed, choose, wproj, code, wcode, fb, p32, c32, tail, dctx, small)
+    save("tail", "dctx", "small")
+    slot(19)
+    ga.drain()
+    for cp in outs: cp.wait()
+
+def forward(pieces, events, weight, params, x, mask, dis, cho, vec):
+    V_ = pl.BlockSpec(memory_space=pltpu.VMEM)
+    A_ = pl.BlockSpec(memory_space=pl.ANY)
+    VM = pltpu.VMEM
+    DMA = pltpu.SemaphoreType.DMA
+    sds = jax.ShapeDtypeStruct
+    n = params.shape[0] // 128
+    most = max(len(ps) for ps in pieces) + 1
+    here = [VM(*K1_SHAPE[k]) for k in K1_OUT[1:-1]] + [VM((4 * T, T), bf16)]
+    outs = pl.pallas_call(functools.partial(forward_kernel, pieces, events, weight),
+        out_shape=[sds(*K1_SHAPE[k]) for k in K1_OUT] + [sds((1, LEN, D), bf16)],
+        in_specs=[V_] * 6, out_specs=[A_] * len(K1_OUT) + [V_],
+        scratch_shapes=[VM((1, vec.shape[0]), f32), VM((GROW, D), bf16), VM((96 + 2 * n + 96, 128), f32), VM((n + 4, 128), f32), VM((4 * D, D), bf16), VM((6, 256, 128), f32)] + here
+            + [VM((T, D), bf16), VM((T, D), bf16), VM((D, T), bf16), VM((T, FF), bf16), VM((LT, D), f32), VM((LT, D), f32), VM((T, D), bf16), VM((T, D), bf16),
+               VM((256, T), bf16), VM((T, 256), bf16), VM((256, 256), f32), VM((2, 256, 384), f32), VM((1152, 128), f32), VM((2, 768, 128), f32), VM((3, 256, 128), f32),
+               VM((256, 384), bf16), VM((256, 256), bf16),
+               DMA((2,)), DMA((16, most)), DMA((16, most)), DMA((320,)), DMA((24,)), DMA((2,))],
+        compiler_params=pltpu.CompilerParams(collective_id=0, has_side_effects=True, vmem_limit_bytes=63 * 2**20),
+    )(params.reshape(n, 128), x, mask, jnp.transpose(dis, (2, 0, 1)), jnp.swapaxes(cho, 1, 2), vec.reshape(-1, 128))
+    return dict(zip(K1_OUT, outs)), outs[-1]
+TO_CORE, TO_V, TO_U, TO_Z, KEEP, SMALL = range(6)
+
+class Reduce:
+    def __init__(self, at, g, pieces, LD, LV, LZ, LU, total, RD, RV, RZ, RU, S):
+        self.at, self.g, self.pieces, self.total = at, g, pieces, total
+        self.LD, self.LV, self.LZ, self.LU = LD, LV, LZ, LU
+        self.RD, self.RV, self.RZ, self.RU, self.S = RD, RV, RZ, RU, S
+        self.index = {}
+        self.made = {z: [] for z in range(PLANES)}
+        self.seen = set()
+
+    def sem(self, key):
+        return self.S.at[self.index.setdefault(key, len(self.index))]
+
+    def copies(self, key, p, r, c, first, rows, extra, land, got, dev):
+        a, e = self.at.span(p, r, c, first)
+        out = []
+        for j, (s, n, to) in enumerate([(a, rows, first)] + [(e, EXTRA, MAIN)] * extra):
+            out.append(remote(self.g.at[pl.ds(s, n)], land.at[pl.ds(to, n)], self.sem(key + (j,)), got.at[j], dev))
+        return out
+
+    def build(self, zs, op):
+        at = self.at
+        kind, i, p, r = op
+        unit = 4 * p + at.roles[r]
+        if kind == TO_CORE:
+            return self.copies(op, p, r, 1 - at.c, 0, MAIN, True, self.LD.at[unit], self.RD.at[unit], (zs, at.fc))
+        if kind == TO_V:
+            n = 2 * p + r - 2
+            return self.copies(op, p, r, at.c, 0, MAIN, True, self.LV.at[n], self.RV.at[n], (zs, at.vf))
+        _, first, rows, extra = self.pieces[p][i]
+        if kind == TO_U:
+            return self.copies(op, p, r, at.c, first, rows, extra, self.LU.at[p], self.RU.at[p, i], (zs, at.uf))
+        up = p > zs
+        to = zs + 1 if up else zs - 1
+        n = 8 + r if (not up and to == p) else 2 * p + r
+        return self.copies(op, p, r, at.c, first, rows, extra, self.LZ.at[n], self.RZ.at[n, i], (to, at.f))
+
+    def once(self, zs, key, cs):
+        if (zs, key) not in self.seen:
+            self.seen.add((zs, key))
+            for q in cs: q.wait_recv()
+
+    def send(self, zs, op):
+        for q in self.build(zs, op): q.start()
+        self.made[zs].append(op)
+
+    def add(self, p, r, first, rows, extra, lands, final):
+        a, e = self.at.span(p, r, self.at.c, first)
+        g, total = self.g, self.total
+        def one(s, i):
+            v = g[pl.ds(s, 16), :].astype(f32)
+            for land in lands:
+                v = v + land[pl.ds(i, 16), :].astype(f32)
+            if final:
+                total[pl.ds(16 + i, 16), :] = v
+            else:
+                g[pl.ds(s, 16), :] = v.astype(bf16)
+        def body(b, _):
+            one(pl.multiple_of(a + 16 * b, 16), pl.multiple_of(first + 16 * b, 16))
+            return 0
+        lax.fori_loop(0, rows // 16, body, 0)
+        if extra: one(e, MAIN)
+
+    def op(self, zs, op):
+        at = self.at
+        kind, i, p, r = op
+        if kind == TO_CORE:
+            for rr in (2, 3, 0, 1): self.send(zs, (TO_CORE, 0, p, rr))
+            return
+        unit = 4 * p + at.roles[r]
+        self.once(zs, (TO_CORE, p, r), self.copies((HERE,), p, r, at.c, 0, MAIN, True, self.LD.at[unit], self.RD.at[unit], (zs, at.fc)))
+        if kind == TO_V:
+            self.add(p, r, 0, MAIN, True, [self.LD.at[unit]], False)
+            self.send(zs, op)
+            return
+        n = 2 * p + r
+        self.once(zs, (TO_V, p, r), self.copies((HERE,), p, r, at.c, 0, MAIN, True, self.LV.at[n], self.RV.at[n], (zs, at.fc)))
+        path, first, rows, extra = self.pieces[p][i]
+        lands = [self.LD.at[unit], self.LV.at[n]]
+        def arrived(land, got, key):
+            self.once(zs, key, self.copies((HERE,), p, r, at.c, first, rows, extra, land, got, (zs, at.fc)))
+            lands.append(land)
+        if path == 0 or r == 0:
+            if p >= zs and zs > 0: arrived(self.LZ.at[n], self.RZ.at[n, i], (UP, i, p, r))
+            if p <= zs and zs < PLANES - 1:
+                m = 8 + r if p == zs else n
+                arrived(self.LZ.at[m], self.RZ.at[m, i], (DOWN, i, p, r))
+        if r == 0 and (path == 1 or p == zs):
+            arrived(self.LU.at[p], self.RU.at[p, i], (TO_U, i, p))
+        self.add(p, r, first, rows, extra, lands, kind == KEEP)
+        if kind != KEEP: self.send(zs, op)
+
+    def drain(self):
+        for zs in range(PLANES):
+            @pl.when(self.at.z == zs)
+            def _():
+                for op in self.made[zs]:
+                    for q in self.build(zs, op): q.wait_send()
+
+class Spread:
+    def __init__(self, at, own, land, zland, S, count):
+        self.at, self.own, self.land, self.zland, self.S, self.count = at, own, land, zland, S, count
+
+    def round(self, n, me, land, base, dev):
+        return [remote(self.own, land.at[me], self.S.at[0, base + j], self.S.at[1, base + j], dev(lax.rem(me + j, n))) for j in range(1, n)]
+
+    def plane(self):
+        return self.round(self.count, self.at.f, self.land, 0, lambda t: (self.at.z, t))
+
+    def planes(self):
+        return self.round(PLANES, self.at.z, self.zland, self.count, lambda t: (t, self.at.f))
+
+    def first(self):
+        for q in self.plane(): q.start()
+
+    def total(self, land, n, me):
+        land[me] = self.own[...]
+        v = land[0]
+        for j in range(1, n): v = v + land[j]
+        return v
+
+    def second(self):
+        for q in self.plane(): q.wait()
+        self.own[...] = self.total(self.land, self.count, self.at.f)
+        for q in self.planes(): q.start()
+
+    def last(self):
+        for q in self.planes(): q.wait()
+        self.own[...] = self.total(self.zland, PLANES, self.at.z)
+
+K2_IN = K1_OUT
+K2_HERE = ("wproj", "dctx", "small", "hat1", "r1", "hat2", "r2", "gp", "ring", "normT", "attT", "q", "kT", "vv", "xT", "wq")
+
+def backward_kernel(pieces, events, vec_ref, *rest):
+    n_in = len(K2_IN)
+    hbm = dict(zip(K2_IN, rest[:n_in]))
+    (grad, vsum, sq, ig, g, vec, wproj, dctx, small, hat1, r1, hat2, r2, gp, ring, normT, attT, q, kT, vv, xT, wq,
+     low1, low2, acc, tmp, dp, LD, LV, LZ, LU, total, flat, vg, vland, vzland, sqv, sland, szland,
+     IS, RD, RV, RZ, RU, S, TS, VS, SS) = rest[n_in:]
+    here = dict(wproj=wproj, dctx=dctx, small=small, hat1=hat1, r1=r1, hat2=hat2, r2=r2, gp=gp, normT=normT, attT=attT, q=q, kT=kT, vv=vv, xT=xT)
+    loads = {}
+    def load(name, src=None, dst=None):
+        cp = pltpu.make_async_copy(hbm[name] if src is None else src, here[name] if dst is None else dst, IS.at[len(loads)])
+        cp.start()
+        loads[name if src is None else (name, len(loads))] = cp
+        return cp
+    w = hbm["w"]
+    first = [load(n) for n in ("dctx", "wproj", "hat2", "r2")]
+    second = [load("w", w.at[pl.ds(6144, 3072)], g.at[pl.ds(6144, 3072)]), load("gp"), load("actT", hbm["actT"], ring)]
+    tail = load("tail", hbm["tail"], g.at[pl.ds(9216, 448)])
+    third = [load("w", w.at[pl.ds(3072, 3072)], g.at[pl.ds(3072, 3072)]), load("normT")]
+    fourth = [load("hat1"), load("r1"), load("small")]
+    fifth = [load("w", w.at[pl.ds(2304, 768)], g.at[pl.ds(2304, 768)]), load("attT")]
+    sixth = [load("q"), load("kT"), load("vv")]
+    seventh = [load("xT"), load("w", w.at[pl.ds(0, 2304)], wq)]
+    def ready(cs):
+        for cp in cs: cp.wait()
+    at = Place()
+    at.greet_all(vland.shape[0])
+    re = Reduce(at, g, pieces, LD, LV, LZ, LU, total, RD, RV, RZ, RU, S)
+    vs = Spread(at, vg, vland, vzland, VS, vland.shape[0])
+    ss = Spread(at, sqv, sland, szland, SS, vland.shape[0])
+    def slot(i, cond=None):
+        for zs in range(PLANES):
+            if events[zs][i]:
+                @pl.when((at.z == zs) if cond is None else ((at.z == zs) & cond))
+                def _():
+                    for e in events[zs][i]:
+                        if e[0] == SMALL: (vs.first, vs.second, vs.last)[e[1]]()
+                        else: re.op(zs, e)
+    for i in range(vec_ref.shape[0]):
+        vec[0:1, 128 * i:128 * i + 128] = vec_ref[i:i + 1, :]
+    low2[...] = jnp.zeros((T, D), bf16)
+    low1[...] = jnp.zeros((T, D), bf16)
+    for t in range(3):
+        dp[t] = jnp.zeros((T, D), bf16)
+    ready(first)
+    norm_back_first(dctx, wproj, vec[0:1, G2:G2 + D], hat2, r2, low2, acc)
+    put_vec(vg, acc, (G2, S2, BDOWN))
+    ready(second)
+    lax.fori_loop(0, 12, lambda n, _: (down_back(n, low2, g, ring, gp, vg), 0)[1], 0)
+    ready([tail])
+    shared_blocks(g, 3, True)
+    def head(h):
+        return pltpu.make_async_copy(hbm["pT"].at[pl.ds(pl.multiple_of(h * T, T), T)], ring.at[pl.ds(pl.multiple_of((h % 6) * T, T), T)], TS.at[h % 6])
+    for h in range(6): head(h).start()
+    slot(1)
+    ready(third)
+    lax.fori_loop(0, 3, lambda n, _: (up_back_x(n, gp, g, hat2), 0)[1], 0)
+    slot(2)
+    def woven(n, _):
+        weave(normT, gp, 4, 2 - n, 3072, g, tmp, False)
+        slot(3, n == 0)
+        slot(4, n == 1)
+        return 0
+    lax.fori_loop(0, 2, woven, 0)
+    shared_blocks(g, 2, True)
+    slot(5)
+    lax.fori_loop(2, 3, woven, 0)
+    slot(6)
+    ready(fourth)
+    norm_back(hat2, vec[0:1, G1:G1 + D], hat1, r1, low1, acc)
+    put_vec(vg, acc, (G1, S1, BO))
+    ready(fifth)
+    da, dqT = low2, normT
+    out_back(low1, g, attT, da)
+    shared_blocks(g, 1, True)
+    slot(7)
+    slot(8)
+    ready(sixth)
+    def pair(p, _):
+        head(2 * p).wait()
+        head(2 * p + 1).wait()
+        attend_back(p, da, q, kT, vv, ring, dp, dqT)
+        @pl.when(p < 3)
+        def _():
+            head(2 * p + 6).start()
+            head(2 * p + 7).start()
+        for i in range(6): slot(9 + i, p == i)
+        return 0
+    lax.fori_loop(0, 6, pair, 0)
+    ready(seventh)
+    def wove(n, _):
+        weave(xT, dp, 3, n, 0, g, tmp, True)
+        for i in range(3): slot(15 + i, n == i)
+        return 0
+    lax.fori_loop(0, 3, wove, 0)
+    shared_blocks(g, 0, True)
+    slot(18)
+    vg[0:1, BQ:BQ + D] = jnp.sum(dp[0].astype(f32), axis=0, keepdims=True)
+    vg[0:1, BV:BV + D] = jnp.sum(dp[2].astype(f32), axis=0, keepdims=True)
+    vg[0:1, BPROJ:BPROJ + 256] = small[0:1, :]
+    vg[0:1, BCODE:BCODE + 256] = small[1:2, :]
+    vg[0:1, BCODE + 256:BCODE + 512] = small[2:3, :]
+    slot(19)
+    slot(20)
+    for n in range(3):
+        input_back(n, dp, wq, hat1, ig)
+    slot(21)
+    z, c, k = at.z, at.c, at.k
+    edge = remote(total.at[pl.ds(HALF, 16)], total.at[pl.ds(0, 16)], TS.at[6], TS.at[7], (z, at.fc))
+    edge.start()
+    vsum[...] = vg[...]
+    edge.wait()
+    part = jnp.zeros((8, 128), f32)
+    n = grad.shape[0] // 6
+    for j in range(6):
+        flat[pl.ds(j, 320, stride=6), :] = total[:, 128 * j:128 * j + 128]
+    for j in range(6):
+        v = flat[pl.ds(6 * (16 - 2 * c - 4 * k) + j, n, stride=6), :]
+        grad[pl.ds(j, n, stride=6), :] = v
+        v = v * v
+        part = part + sum8(v[0:n // 8 * 8])
+        if n % 8: part = part + jnp.concatenate([v[n // 8 * 8:], jnp.zeros((8 - n % 8, 128), f32)], axis=0)
+    sqv[...] = part
+    ss.first()
+    ss.second()
+    ss.last()
+    sq[...] = sqv[...]
+    re.drain()
+
+def backward(pieces, events, vec, hbm, count, n):
+    V_ = pl.BlockSpec(memory_space=pltpu.VMEM)
+    A_ = pl.BlockSpec(memory_space=pl.ANY)
+    VM = pltpu.VMEM
+    DMA = pltpu.SemaphoreType.DMA
+    sds = jax.ShapeDtypeStruct
+    most = max(len(ps) for ps in pieces)
+    nv = vec.shape[0] + 256
+    shape = dict(K1_SHAPE, ring=((FF, T), bf16), wq=((3 * D, D), bf16))
+    return pl.pallas_call(functools.partial(backward_kernel, pieces, events),
+        out_shape=[sds((n, 128), f32), sds((1, nv), f32), sds((8, 128), f32), sds((1, LEN, D), f32)],
+        in_specs=[V_] + [A_] * len(K2_IN), out_specs=[V_] * 4,
+        scratch_shapes=[VM((GROW, D), bf16), VM((1, vec.shape[0]), f32)] + [VM(*shape[k]) for k in K2_HERE]
+            + [VM((T, D), bf16), VM((T, D), bf16), VM((24, D), f32), VM((2, 1024, 128), f32), VM((3, T, D), bf16),
+               VM((16, HALF, D), bf16), VM((8, HALF, D), bf16), VM((10, HALF, D), bf16), VM((4, HALF, D), bf16), VM((HALF + 16, D), f32), VM((6 * (HALF + 16), 128), f32),
+               VM((1, nv), f32), VM((count, 1, nv), f32), VM((PLANES, 1, nv), f32), VM((8, 128), f32), VM((count, 8, 128), f32), VM((PLANES, 8, 128), f32),
+               DMA((24,)), DMA((16, 2)), DMA((8, 2)), DMA((10, most, 2)), DMA((4, most, 2)), DMA((200,)), DMA((8,)), DMA((2, count + PLANES)), DMA((2, count + PLANES))],
+        compiler_params=pltpu.CompilerParams(collective_id=1, has_side_effects=True, vmem_limit_bytes=63 * 2**20),
+    )(vec.reshape(-1, 128), *[hbm[k] for k in K2_IN])
+
+PIECES_OUT = (((1, 0, 64, False), (1, 64, 64, False), (1, 128, 80, False), (1, 208, 80, True)), ((0, 0, 80, False), (1, 80, 112, False), (1, 192, 96, True)),
+ ((0, 0, 96, False), (0, 96, 96, False), (0, 192, 96, True)), ((0, 0, 112, False), (0, 112, 96, False), (1, 208, 80, True)))
+PIECES_BACK = (((0, 0, 80, False), (0, 80, 64, False), (1, 144, 80, False), (1, 224, 64, True)),
+ ((0, 0, 80, False), (0, 80, 64, False), (1, 144, 80, False), (1, 224, 64, True)),
+ ((0, 0, 80, False), (0, 80, 64, False), (1, 144, 80, False), (1, 224, 64, True)), ((0, 0, 208, False), (1, 208, 80, True)))
+SENDS_OUT = ((((0, 0, 0, 0), (2, 0, 0, 0), (2, 1, 0, 0), (0, 1, 0, 0), (2, 2, 0, 0)),
+  ((4, 0, 0, 1), (4, 1, 0, 1), (0, 2, 0, 0), (2, 3, 0, 0), (4, 2, 0, 1), (3, 0, 0, 0), (4, 0, 1, 0), (0, 3, 0, 0), (3, 1, 0, 0), (3, 2, 0, 0),
+   (3, 3, 0, 0), (4, 3, 0, 1), (4, 0, 0, 2), (3, 0, 0, 1), (4, 1, 0, 2), (4, 1, 1, 0), (3, 1, 0, 1), (4, 2, 0, 2), (3, 2, 0, 1), (3, 3, 0, 1),
+   (4, 3, 0, 2), (4, 0, 0, 3), (4, 2, 1, 0), (2, 1, 1, 0), (4, 1, 0, 3), (2, 2, 1, 0), (4, 2, 0, 3), (4, 0, 1, 1), (4, 3, 0, 3), (3, 0, 1, 0),
+   (3, 1, 1, 0), (4, 1, 1, 1), (4, 0, 2, 0)),
+  ((4, 2, 1, 1), (4, 0, 1, 2), (3, 2, 1, 0), (4, 1, 2, 0), (3, 0, 1, 1)),
+  ((4, 1, 1, 2), (4, 2, 1, 2), (3, 1, 1, 1), (4, 0, 1, 3), (3, 2, 1, 1), (4, 2, 2, 0)), (), ((4, 0, 2, 1), (3, 0, 2, 0)),
+  ((4, 1, 1, 3), (3, 1, 2, 0)), ((4, 2, 1, 3), (4, 1, 2, 1), (3, 2, 2, 0)), ((4, 0, 2, 2), (3, 0, 2, 1)), ((4, 1, 2, 2), (3, 1, 2, 1)),
+  ((4, 2, 2, 2), (4, 2, 2, 1), (3, 2, 2, 1)), ((4, 0, 2, 3), (4, 1, 2, 3), (4, 2, 2, 3), (4, 0, 3, 0), (3, 0, 3, 0), (4, 1, 3, 0), (3, 1, 3, 0)),
+  ((4, 0, 3, 2), (4, 2, 3, 0), (4, 1, 3, 2), (2, 2, 3, 0), (3, 2, 3, 0)), (), ((4, 0, 3, 1), (3, 0, 3, 1), (4, 2, 3, 1), (3, 2, 3, 1)),
+  ((4, 2, 3, 2), (4, 1, 3, 1), (3, 1, 3, 1)), ((4, 0, 3, 3),), ((4, 2, 3, 3), (4, 1, 3, 3)), (), ()),
+ (((0, 0, 1, 0), (1, 0, 1, 0), (2, 0, 1, 0), (2, 1, 1, 0)),
+  ((4, 0, 0, 0), (0, 0, 0, 0), (2, 0, 0, 0), (3, 0, 0, 0), (4, 0, 1, 1), (4, 1, 1, 1), (0, 1, 1, 0), (1, 1, 1, 0), (2, 2, 1, 0), (4, 0, 2, 0),
+   (4, 1, 0, 0), (2, 1, 0, 0), (1, 2, 1, 0), (4, 0, 0, 1), (3, 1, 0, 0), (4, 0, 0, 2), (0, 1, 0, 0), (3, 0, 0, 1), (4, 2, 0, 0), (4, 1, 2, 0),
+   (2, 2, 0, 0), (4, 2, 1, 1), (0, 2, 0, 0), (1, 0, 1, 1), (3, 2, 0, 0), (4, 1, 0, 1), (4, 3, 0, 0), (4, 1, 0, 2), (2, 3, 0, 0), (0, 3, 0, 0),
+   (4, 0, 0, 3), (1, 0, 2, 0), (4, 2, 2, 0), (3, 1, 0, 1), (4, 2, 0, 1), (3, 3, 0, 0), (4, 2, 0, 2), (0, 2, 1, 0), (1, 1, 2, 0), (3, 2, 0, 1),
+   (4, 0, 2, 1), (4, 3, 0, 1), (3, 3, 0, 1), (4, 1, 0, 3), (3, 0, 1, 0), (1, 2, 2, 0), (4, 1, 2, 1), (0, 0, 1, 1), (4, 3, 0, 2), (3, 1, 1, 0),
+   (4, 2, 0, 3), (3, 2, 1, 0), (4, 3, 0, 3), (1, 0, 2, 1), (4, 2, 2, 1), (4, 0, 1, 2), (3, 0, 1, 1)),
+  ((4, 1, 1, 2), (4, 2, 1, 2), (3, 1, 1, 1), (1, 1, 2, 1), (3, 2, 1, 1), (4, 0, 3, 0)),
+  ((4, 0, 1, 3), (4, 1, 1, 3), (1, 2, 2, 1), (3, 0, 2, 0), (3, 1, 2, 0), (4, 1, 3, 0), (4, 2, 1, 3), (4, 2, 3, 0)), (), ((3, 2, 2, 0), (1, 0, 3, 0)),
+  ((4, 0, 2, 2), (3, 0, 2, 1), (4, 0, 3, 1)), ((4, 1, 2, 2), (3, 1, 2, 1), (1, 1, 3, 0), (3, 2, 2, 1)),
+  ((4, 2, 2, 2), (4, 0, 2, 3), (4, 1, 3, 1), (1, 2, 3, 0), (2, 2, 3, 0)), ((4, 1, 2, 3), (3, 0, 3, 0)), ((4, 2, 2, 3), (1, 0, 3, 1), (3, 1, 3, 0)),
+  ((4, 2, 3, 1), (4, 0, 3, 2), (1, 1, 3, 1), (4, 1, 3, 2), (3, 2, 3, 0), (3, 0, 3, 1)), ((3, 1, 3, 1),), ((4, 2, 3, 2), (3, 2, 3, 1)),
+  ((4, 0, 3, 3),), ((4, 1, 3, 3),), ((4, 2, 3, 3),), (), (), ()),
+ (((0, 0, 2, 0), (1, 0, 2, 0), (2, 0, 2, 0), (2, 1, 2, 0)),
+  ((4, 0, 1, 0), (0, 0, 1, 0), (3, 0, 1, 0), (4, 0, 2, 1), (4, 1, 2, 1), (1, 1, 2, 0), (2, 2, 2, 0), (4, 0, 3, 0), (0, 1, 2, 0), (3, 0, 2, 0),
+   (1, 2, 2, 0), (3, 1, 2, 0), (4, 0, 1, 2), (4, 0, 0, 0), (0, 0, 0, 0), (4, 1, 3, 0), (2, 0, 0, 0), (4, 2, 2, 1), (1, 0, 2, 1), (3, 0, 0, 0),
+   (0, 2, 2, 0), (4, 0, 2, 2), (3, 2, 2, 0), (4, 1, 1, 0), (4, 2, 3, 0), (4, 1, 2, 2), (2, 1, 1, 0), (1, 1, 2, 1), (4, 0, 0, 1), (4, 1, 0, 0),
+   (0, 1, 0, 0), (4, 0, 0, 2), (2, 1, 0, 0), (4, 0, 3, 1), (3, 0, 0, 1), (0, 1, 1, 0), (1, 2, 2, 1), (4, 2, 2, 2), (4, 2, 0, 0), (2, 2, 0, 0),
+   (3, 1, 0, 0), (4, 1, 1, 1), (4, 1, 3, 1), (3, 2, 0, 0), (4, 1, 0, 1), (4, 3, 0, 0), (0, 2, 0, 0), (1, 0, 3, 0), (4, 0, 0, 3), (2, 3, 0, 0),
+   (4, 2, 0, 1), (3, 1, 0, 1), (0, 3, 0, 0), (4, 1, 0, 2), (3, 3, 0, 0), (4, 2, 1, 0), (1, 1, 3, 0), (4, 2, 0, 2), (3, 2, 0, 1), (4, 3, 0, 1),
+   (0, 2, 1, 0), (4, 0, 1, 1), (3, 3, 0, 1), (4, 1, 0, 3), (1, 2, 3, 0), (2, 2, 1, 0), (4, 3, 0, 2), (0, 0, 1, 1), (3, 1, 1, 0), (4, 2, 0, 3),
+   (1, 0, 3, 1), (4, 3, 0, 3), (3, 1, 1, 1), (0, 0, 2, 1), (4, 2, 1, 1), (3, 2, 1, 0)),
+  ((4, 1, 1, 2), (3, 0, 1, 1), (3, 2, 1, 1), (0, 1, 2, 1), (4, 1, 1, 3), (1, 1, 3, 1)),
+  ((4, 2, 1, 2), (4, 0, 1, 3), (0, 2, 2, 1), (3, 0, 2, 1), (4, 2, 1, 3), (3, 1, 2, 1)), (), ((3, 2, 2, 1),), ((4, 0, 2, 3), (2, 2, 3, 0)),
+  ((4, 1, 2, 3), (3, 0, 3, 0)), ((4, 2, 2, 3), (3, 1, 3, 0)), ((4, 2, 3, 1), (3, 2, 3, 0)), ((4, 0, 3, 2), (3, 0, 3, 1)),
+  ((4, 1, 3, 2), (4, 2, 3, 2), (4, 0, 3, 3), (3, 1, 3, 1), (3, 2, 3, 1)), (), ((4, 1, 3, 3),), ((4, 2, 3, 3),), (), (), (), (), ()),
+ (((1, 0, 3, 0), (2, 0, 3, 0)),
+  ((4, 0, 3, 1), (1, 1, 3, 0), (2, 1, 3, 0), (2, 2, 3, 0), (4, 0, 2, 0), (1, 2, 3, 0), (3, 0, 2, 0), (3, 0, 3, 0), (4, 1, 3, 1), (1, 0, 3, 1),
+   (4, 0, 1, 0), (3, 0, 1, 0), (4, 2, 3, 1), (3, 1, 3, 0), (4, 0, 2, 2), (4, 1, 2, 0), (3, 1, 2, 0), (1, 1, 3, 1), (4, 0, 3, 2), (3, 2, 3, 0),
+   (4, 0, 1, 2), (4, 0, 0, 0), (2, 0, 0, 0), (4, 1, 3, 2), (3, 0, 0, 0), (4, 1, 2, 2), (3, 0, 3, 1), (4, 2, 2, 0), (4, 2, 3, 2), (3, 2, 2, 0),
+   (4, 0, 0, 1), (4, 1, 0, 0), (4, 0, 0, 2), (2, 1, 0, 0), (3, 0, 0, 1), (4, 0, 3, 3), (3, 1, 0, 0), (4, 1, 1, 0), (2, 1, 1, 0), (4, 2, 2, 2),
+   (4, 1, 0, 1), (3, 1, 0, 1), (4, 2, 0, 0), (4, 0, 0, 3), (2, 2, 0, 0), (4, 1, 0, 2), (3, 2, 0, 0), (4, 3, 0, 0), (4, 1, 1, 1), (2, 3, 0, 0),
+   (4, 1, 0, 3), (3, 3, 0, 0), (4, 2, 0, 1), (3, 2, 0, 1), (4, 2, 1, 0), (4, 2, 0, 2), (2, 2, 1, 0), (4, 3, 0, 1), (4, 0, 1, 1), (3, 3, 0, 1),
+   (4, 3, 0, 2), (3, 1, 1, 0), (4, 2, 0, 3), (4, 0, 2, 1), (3, 1, 1, 1), (4, 2, 1, 1), (4, 3, 0, 3), (3, 2, 1, 0), (4, 1, 2, 1), (4, 1, 1, 2),
+   (3, 0, 1, 1)),
+  ((4, 1, 1, 3), (3, 2, 1, 1)), ((4, 2, 1, 2), (4, 0, 1, 3), (4, 2, 1, 3), (4, 2, 2, 1), (3, 0, 2, 1), (3, 1, 2, 1)), (), ((3, 2, 2, 1),),
+  ((4, 0, 2, 3), (3, 1, 3, 1)), ((4, 1, 2, 3), (3, 2, 3, 1)), ((4, 2, 2, 3),), ((4, 1, 3, 3),), ((4, 2, 3, 3),), (), (), (), (), (), (), (), (), ()))
+SENDS_BACK = (((), ((0, 0, 3, 0),), (), ((1, 0, 3, 2), (1, 0, 3, 3)), (), ((0, 0, 2, 0),), (), ((3, 0, 3, 0), (1, 0, 2, 2), (1, 0, 2, 3), (3, 0, 3, 1)),
+  ((0, 0, 1, 0),), ((2, 1, 3, 1),), ((3, 0, 2, 0), (1, 0, 1, 2), (3, 1, 2, 0)), ((1, 0, 1, 3),), ((3, 1, 3, 0), (3, 0, 2, 1), (2, 2, 2, 1)),
+  ((3, 1, 2, 1), (2, 3, 2, 1)), ((3, 0, 1, 0),), ((3, 1, 1, 0),), ((3, 0, 1, 1), (2, 2, 1, 1), (2, 3, 1, 1)), ((3, 2, 2, 0),), ((0, 0, 0, 0),), (),
+  ((5, 0, 0, 0), (3, 3, 2, 0)),
+  ((3, 1, 1, 1), (1, 0, 0, 2), (3, 2, 1, 0), (1, 0, 0, 3), (5, 1, 0, 0), (3, 3, 1, 0), (2, 2, 0, 1), (2, 3, 0, 1), (2, 0, 0, 1), (2, 1, 0, 1),
+   (5, 2, 0, 0), (4, 0, 0, 0), (4, 2, 0, 0), (4, 1, 0, 0), (4, 3, 0, 0))),
+ ((), ((0, 0, 3, 0),), (), ((1, 0, 3, 2), (1, 0, 3, 3)), (), ((0, 0, 2, 0),), (), ((1, 0, 2, 2), (1, 0, 2, 3)), ((0, 0, 1, 0),), ((2, 1, 3, 1),),
+  ((1, 0, 1, 2),), ((3, 0, 3, 0), (1, 0, 1, 3)), (), ((2, 2, 2, 1), (3, 0, 3, 1), (2, 3, 2, 1)), ((3, 0, 2, 0),), ((3, 1, 2, 0),), (),
+  ((3, 1, 3, 0), (2, 2, 1, 1), (2, 3, 1, 1)), ((0, 0, 0, 0), (3, 0, 2, 1)), (), ((5, 0, 0, 0),),
+  ((3, 1, 2, 1), (1, 0, 0, 2), (1, 0, 0, 3), (2, 0, 1, 1), (3, 2, 2, 0), (3, 3, 2, 0), (5, 1, 0, 0), (2, 1, 1, 1), (2, 2, 0, 1), (2, 3, 0, 1),
+   (4, 0, 1, 0), (4, 2, 1, 0), (4, 1, 1, 0), (4, 3, 1, 0), (5, 2, 0, 0), (3, 0, 0, 0), (3, 1, 0, 0), (3, 0, 0, 1), (3, 1, 0, 1), (3, 2, 0, 0),
+   (3, 3, 0, 0))),
+ ((), ((0, 0, 3, 0),), (), ((1, 0, 3, 2), (1, 0, 3, 3)), (), ((0, 0, 2, 0),), (), ((1, 0, 2, 2), (1, 0, 2, 3)), ((0, 0, 1, 0),), ((2, 1, 3, 1),),
+  ((1, 0, 1, 2),), (), ((1, 0, 1, 3),), ((2, 2, 2, 1),), ((2, 3, 2, 1),), ((3, 0, 3, 0),), (), (),
+  ((0, 0, 0, 0), (3, 0, 1, 0), (2, 2, 1, 1), (2, 3, 1, 1)), (), ((5, 0, 0, 0), (3, 0, 3, 1), (3, 1, 1, 0), (1, 0, 0, 2)),
+  ((3, 0, 1, 1), (3, 1, 1, 1), (1, 0, 0, 3), (3, 1, 3, 0), (2, 0, 2, 1), (2, 1, 2, 1), (5, 1, 0, 0), (3, 2, 1, 0), (2, 2, 0, 1), (2, 3, 0, 1),
+   (4, 0, 2, 0), (3, 3, 1, 0), (4, 1, 2, 0), (4, 2, 2, 0), (3, 0, 0, 0), (5, 2, 0, 0), (4, 3, 2, 0), (3, 1, 0, 0), (3, 0, 0, 1), (3, 1, 0, 1),
+   (3, 2, 0, 0), (3, 3, 0, 0))),
+ ((), ((0, 0, 3, 0),), (), ((1, 0, 3, 2), (1, 0, 3, 3)), (), ((0, 0, 2, 0),), (), ((1, 0, 2, 2), (1, 0, 2, 3)), ((0, 0, 1, 0),), ((2, 1, 3, 1),),
+  ((1, 0, 1, 2), (3, 0, 2, 0), (3, 1, 2, 0)), ((1, 0, 1, 3),), ((3, 0, 2, 1), (3, 1, 2, 1)), ((2, 2, 2, 1), (2, 3, 2, 1)),
+  ((3, 0, 1, 0), (3, 1, 1, 0)), (), (), ((3, 0, 1, 1), (3, 1, 1, 1), (3, 2, 2, 0), (2, 2, 1, 1), (2, 3, 1, 1)), ((0, 0, 0, 0), (3, 3, 2, 0)), (),
+  ((5, 0, 0, 0),),
+  ((3, 2, 1, 0), (3, 3, 1, 0), (1, 0, 0, 2), (1, 0, 0, 3), (2, 0, 3, 1), (5, 1, 0, 0), (4, 1, 3, 0), (3, 0, 0, 0), (3, 1, 0, 0), (3, 0, 0, 1),
+   (3, 1, 0, 1), (5, 2, 0, 0), (2, 2, 0, 1), (2, 3, 0, 1), (4, 0, 3, 0), (3, 2, 0, 0), (3, 3, 0, 0))))
+
 def unpack(flat_values):
     shapes = [(D, 3 * D), (D, D), (D, FF), (FF, D), (D, FINAL), (G * CD, V), (G * CD, FINAL)]
     pieces = []
@@ -56,34 +978,25 @@
     return centered * lax.rsqrt(variance + eps_norm) * scale_gain + shift_bias
 
 
-def pick_rows(source, index_rows):
-    return source[index_rows]
-
-
-def place_rows(template, index_rows, values):
-    return template.at[index_rows].set(values)
-
-
-def contrast_loss(chosen, targets, distract):
-    encoder_unit_heading = chosen * lax.rsqrt(
-        jnp.sum(chosen * chosen, axis=-1, keepdims=True) + eps_cos
-    )
-    quantized_unit_heading = targets * lax.rsqrt(
-        jnp.sum(targets * targets, axis=-1, keepdims=True) + eps_cos
-    )
-    angular_agreement = (
-        jnp.einsum(
-            "rby,roy->rbo",
-            encoder_unit_heading,
-            quantized_unit_heading,
-            precision=lax.Precision.HIGHEST,
-        )
-        / softness_divisor
-    )
-    positive = jnp.diagonal(angular_agreement, axis1=1, axis2=2)
-    negative = jnp.take_along_axis(angular_agreement, distract, axis=2)
-    logits_all = jnp.concatenate([positive[..., None], negative], axis=-1)
-    return jnp.sum(jax.nn.logsumexp(logits_all, axis=-1) - positive)
+def contrast_dense(chosen, targets, distract, weight):
+    hi = dict(precision=lax.Precision.HIGHEST)
+    frames = jnp.arange(MASKED, dtype=jnp.int32)
+    allowed = jnp.any(distract[:, :, None] == frames, axis=1) | (frames[:, None] == frames)
+
+    def agreement(chosen, targets):
+        left = chosen * lax.rsqrt(jnp.sum(chosen * chosen, axis=-1, keepdims=True) + eps_cos)
+        right = targets * lax.rsqrt(jnp.sum(targets * targets, axis=-1, keepdims=True) + eps_cos)
+        return jnp.einsum("by,oy->bo", left, right, **hi) / softness_divisor
+
+    similar, back = jax.vjp(agreement, chosen, targets)
+    same = frames[:, None] == frames
+    positive = jnp.sum(jnp.where(same, similar, 0.0), axis=1)
+    top = jnp.max(jnp.where(allowed, similar, -jnp.inf), axis=1)
+    parts = jnp.where(allowed, jnp.exp(similar - top[:, None]), 0.0)
+    total = jnp.sum(parts, axis=1)
+    loss = jnp.sum(top + jnp.log(total) - positive)
+    d_similar = weight * (parts / total[:, None] - same.astype(jnp.float32))
+    return (loss,) + back(d_similar)
 
 
 def adamw_update(master, first_moment, second, gradient, step_rate):
@@ -101,7 +1014,7 @@
     return jnp.sum(values.astype(jnp.float32), axis=tuple(range(values.ndim - 1)))
 
 
-def on_device(
+def by_collectives(
     layer_input,
     mask_index,
     distract,
@@ -118,8 +1031,7 @@
     count_utts = layer_input.shape[0]
     total_masked = count_utts * lax.axis_size(("dp", "fsdp")) * MASKED
     token_rows = count_utts * LEN
-    shard_low = params.astype(bf16)
-    gathered = lax.all_gather(shard_low, ("dp", "fsdp"), axis=0, tiled=True)
+    gathered = lax.all_gather(params.astype(bf16), ("dp", "fsdp"), axis=0, tiled=True)
     qkv_weight, out_weight, up_weight, down_weight, proj_weight, codebook, code_weight = unpack(
         gathered
     )
@@ -154,12 +1066,14 @@
     normed, back_one = jax.vjp(layer_norm, residual_one, gain_one, shift_one)
     normed_low = normed.astype(bf16)
     hidden = jnp.dot(normed_low, up_weight, preferred_element_type=f32) + bias_up
-    active, gelu_back = jax.vjp(partial(jax.nn.gelu, approximate=False), hidden)
+    active, gelu_back = jax.vjp(functools.partial(jax.nn.gelu, approximate=False), hidden)
     active_low = active.astype(bf16)
     residual_two = normed + jnp.dot(active_low, down_weight, preferred_element_type=f32) + bias_down
     output, back_two = jax.vjp(layer_norm, residual_two, gain_two, shift_two)
     output_low = output.astype(bf16)
-    context = jnp.dot(output_low, proj_weight, preferred_element_type=f32) + bias_proj
+    place = (mask_index[0][:, None] == jnp.arange(LEN, dtype=jnp.int32)).astype(bf16)
+    picked = jnp.dot(place, output_low, preferred_element_type=f32).astype(bf16)
+    chosen = jnp.dot(picked, proj_weight, preferred_element_type=f32) + bias_proj
     choose = (code_choice[..., None] == jnp.arange(V, dtype=jnp.int32)).astype(bf16)
     code_vectors = jnp.einsum(
         "bmgv,gcv->bmgc", choose, codebook.reshape(G, CD, V), preferred_element_type=f32
@@ -168,12 +1082,8 @@
     targets = (
         jnp.einsum("bmc,cf->bmf", code_vectors, code_weight, preferred_element_type=f32) + bias_code
     )
-    chosen = jax.vmap(pick_rows)(context.reshape(count_utts, LEN, FINAL), mask_index)
-    loss_local, contrast_back = jax.vjp(partial(contrast_loss, distract=distract), chosen, targets)
-    qkv_weight, out_weight, up_weight, down_weight, proj_weight, codebook, code_weight = unpack(
-        lax.all_gather(shard_low, ("dp", "fsdp"), axis=0, tiled=True)
-    )
-    d_selected_code, d_targets = contrast_back(jnp.asarray(1.0 / total_masked, f32))
+    loss_local, d_chosen, d_targets = contrast_dense(chosen, targets[0], distract[0], 1.0 / total_masked)
+    d_targets = d_targets[None]
     d_targets_low = d_targets.astype(bf16)
     quantized_offset_slope = column_sum(d_targets_low)
     d_code_weight = jnp.einsum(
@@ -188,12 +1098,10 @@
         choose.astype(f32),
         precision=lax.Precision.HIGHEST,
     ).reshape(G * CD, V)
-    d_context = jax.vmap(place_rows)(
-        jnp.zeros((count_utts, LEN, FINAL), f32), mask_index, d_selected_code
-    )
-    d_context_low = d_context.reshape(token_rows, FINAL).astype(bf16)
-    d_bias_proj = column_sum(d_context_low)
-    d_proj_weight = jnp.einsum("td,tf->df", output_low, d_context_low, preferred_element_type=f32)
+    d_chosen_low = d_chosen.astype(bf16)
+    d_bias_proj = column_sum(d_chosen_low)
+    d_proj_weight = jnp.einsum("td,tf->df", picked, d_chosen_low, preferred_element_type=f32)
+    d_context_low = jnp.einsum("mt,mf->tf", place, d_chosen_low, preferred_element_type=f32).astype(bf16)
     result_sensitivity = jnp.einsum(
         "tf,df->td", d_context_low, proj_weight, preferred_element_type=f32
     )
@@ -265,29 +1173,24 @@
         ]
     )
     vector_sum, loss_sum = lax.psum((vector_gradient, loss_local), ("dp", "fsdp"))
-    owner_rows = params.shape[0]
-    grad_shard = lax.psum_scatter(
-        lax.slice_in_dim(flat_grad, 0, lax.axis_size(("dp", "fsdp")) * owner_rows, axis=0),
-        ("dp", "fsdp"),
-        scatter_dimension=0,
-        tiled=True,
-    )
-    local_squares = jnp.sum(grad_shard * grad_shard)
-    square_sum = lax.psum(local_squares, ("dp", "fsdp"))
+    grad_shard = lax.psum_scatter(flat_grad, ("dp", "fsdp"), scatter_dimension=0, tiled=True)
+    square_sum = lax.psum(jnp.sum(grad_shard * grad_shard), ("dp", "fsdp"))
+    return finish(
+        total_masked, square_sum, vector_sum, loss_sum, grad_shard, output_low.reshape(count_utts, LEN, D),
+        input_grad.reshape(count_utts, LEN, D), params, moment_one, moment_two, vectors, vector_one, vector_two,
+    )
+
+
+def finish(total_masked, square_sum, vector_sum, loss_sum, grad_shard, output, input_grad, params, moment_one, moment_two, vectors, vector_one, vector_two):
     grad_norm = jnp.sqrt(square_sum + jnp.sum(vector_sum * vector_sum))
     factor = jnp.minimum(1.0, clip_level / (grad_norm + 1e-06))
-    refreshed_weights, new_one, new_two = adamw_update(
-        params, moment_one, moment_two, grad_shard * factor, rate_matrix
-    )
-    new_vectors, new_vector_first, new_vector_second = adamw_update(
-        vectors, vector_one, vector_two, vector_sum * factor, rate_vector
-    )
-    total_loss = loss_sum / total_masked
+    refreshed_weights, new_one, new_two = adamw_update(params, moment_one, moment_two, grad_shard * factor, rate_matrix)
+    new_vectors, new_vector_first, new_vector_second = adamw_update(vectors, vector_one, vector_two, vector_sum * factor, rate_vector)
     return (
-        total_loss,
+        loss_sum / total_masked,
         grad_norm,
-        output_low.reshape(count_utts, LEN, D),
-        input_grad.reshape(count_utts, LEN, D),
+        output,
+        input_grad,
         refreshed_weights,
         refreshed_weights.astype(bf16),
         new_one,
@@ -295,6 +1198,17 @@
         new_vectors,
         new_vector_first,
         new_vector_second,
+    )
+
+
+def by_kernels(layer_input, mask_index, distract, code_choice, params, moment_one, moment_two, vectors, vector_one, vector_two):
+    total_masked = layer_input.shape[0] * lax.axis_size(("dp", "fsdp")) * MASKED
+    kept, output = forward(PIECES_OUT, SENDS_OUT, 1.0 / total_masked, params, layer_input, mask_index, distract, code_choice, vectors)
+    grads, sums, squares, input_grad = backward(PIECES_BACK, SENDS_BACK, vectors, kept, lax.axis_size("fsdp"), params.shape[0] // 128)
+    sums = sums.reshape(-1)
+    return finish(
+        total_masked, jnp.sum(squares), sums[: vectors.shape[0]], sums[vectors.shape[0]], grads.reshape(-1), output, input_grad,
+        params, moment_one, moment_two, vectors, vector_one, vector_two,
     )
 
 
@@ -324,6 +1238,7 @@
         P(),
         P(),
     )
+    fits = mesh.shape["dp"] == PLANES and mesh.shape["fsdp"] == 8
     return jax.shard_map(
-        on_device, mesh=mesh, in_specs=in_specs, out_specs=out_specs, check_vma=False
-    )
+        by_kernels if fits else by_collectives, mesh=mesh, in_specs=in_specs, out_specs=out_specs, check_vma=False
+    )

time: 1600 us -> 230 us (0.14)
  waiting for transfers between devices: 611 us -> 0 us
  other arithmetic: 476 us -> 9.07 us
  local copies, waits for them, and re-layouts: 335 us -> 3.15 us
  Pallas kernels: 0 us -> 213 us
  matrix products: 108 us -> 0 us
  blocking collectives: 40.5 us -> 0 us
    unnamed x3 -> x0, waiting for transfers between devices: 438 us -> none
    all_gather x1 -> x0, other arithmetic: 284 us -> none  [on_device(): gathered = lax.all_gather(shard_low, ('dp', 'fsdp'), axis=0, tiled=True)]
    pallas_call x0 -> x2, Pallas kernels: none -> 213 us  [the longest x1 126 us: backward(): pl.pallas_call(functools.partial(backward_kernel, pieces, events), out_sh...]
    gather x7 -> x0, local copies, waits for them, and re-layouts: 180 us -> none  [the longest x4 175 us: contrast_loss(): negative = jnp.take_along_axis(angular_agreement, distract, axis=2)]
    all_gather x1 -> x0, waiting for transfers between devices: 174 us -> none  [on_device(): gathered = lax.all_gather(shard_low, ('dp', 'fsdp'), axis=0, tiled=True)]
    unnamed x8 -> x0, other arithmetic: 156 us -> none
    dot_general x28 -> x0, matrix products: 101 us -> none  [the longest x1 18.9 us: on_device(): jnp.dot(normed_low, up_weight, preferred_element_type=f32) + bias_up]
    unnamed x205 -> x10, local copies, waits for them, and re-layouts: 74.4 us -> 1.98 us
  transfers between devices with their start and end apart: 2 -> 0, of which waited for: 2 -> 0; matrix products, arithmetic and copies ran while one was open for 1% -> 0% of each run, Pallas kernels for 0% -> 0%
where the time goes in v2:
time: 230 us
  Pallas kernels  213 us (93%)
  other arithmetic  9.07 us (4%)
  between operations  4.99 us (2%)
  local copies, waits for them, and re-layouts  3.15 us (1%)
    pallas_call x1, Pallas kernels, backward(): pl.pallas_call(functools.partial(backward_kernel, pieces, events), out_sh...  126 us
    pallas_call x1, Pallas kernels, forward(): pl.pallas_call(functools.partial(forward_kernel, pieces, events, weight),...  86.8 us

profile of v2, /device:TPU:0, one launch (start us, length us, event | category | flops | bytes accessed | tf_op | source)
XLA Modules:
  0.0 229.8 jit_solution(17320363195822111538)
XLA Ops:
  0.6 86.8 %shard_map.185 = (bf16[9664,768]{1,0:T(8,128)(2,1)}, bf16[768,256]{1,0:T(8,128)(2,1)}, bf16[448,768]{1,0:T(8,128)(2,1)}, bf16[512,256]{1,0:T(8,128)(2,1)}, f32[8...) custom-call(f32[1812,128]{1,0:T(8,128)} %bitcast.12, ...), custom_call_target="tpu_custom_call" | custom-call | tf_op jit(solution)/shard_map/pallas_call | solution.py:584
  87.4 0.0 copy-start.3
  87.5 0.0 copy-start
  87.5 125.8 %shard_map.186 = (f32[1812,128]{1,0:T(8,128)}, f32[1,9984]{1,0:T(1,128)}, f32[8,128]{1,0:T(8,128)}, f32[1,472,768]{2,1,0:T(8,128)}) custom-call(f32[76,128]{1,0:T(8,128)} %bitcast.14, bf16[9664,768]{1,0:T(8,128)(2,1)} %get-tuple-element.34.rest_0_, bf16[768,256]{1,0:T(8,128)(2,1)} %get-tuple-element.35.rest_1_, bf16[448,768]{1,0:T(8,128)(2,1)} %get-tuple-element.36.rest_2_, ...), custom_call_target="tpu_custom_call" | custom-call | tf_op jit(solution)/shard_map/pallas_call | solution.py:866
  213.3 1.5 multiply_reduce_fusion.1
  214.8 1.2 slice.8
  216.6 1.3 reduce_sum.18
  219.3 0.9 multiply_reduce_fusion
  220.1 0.0 copy-done.3
  220.2 1.5 divide_subtract_fusion.1
  221.6 0.0 copy-done
  221.6 0.0 copy-start.2
  221.6 0.0 copy-start.1
  221.6 4.0 %fusion.4 = (bf16[231936]{0:T(1024)(128)(2,1)}, f32[231936]{0:T(1024)}, f32[231936]{0:T(1024)}, f32[231936]{0:T(1024)}) fusion(f32[231936]{0:T(1024)S(1)} %copy-done, f32[1812,128]{1,0:T(8,128)} %get-tuple-element.56, f32[]{:T(128)S(6)} %min_shard_map.3, f32[231936]{0:T(1024)} %param.15, f32[231936]{0:T(1024)} %param.16), kind=kLoop, calls=%fused_computation.11 | loop fusion | flops 3479040 | bytes 6958084 | tf_op jit(solution)/shard_map/convert_element_type | solution.py:1195
  225.6 0.0 copy-done.2
  225.6 0.9 copy.23
  226.5 0.0 copy-done.1
  226.5 1.1 copy.24
Async XLA Ops:
  87.4 132.7 %copy-start.3 = (f32[9728]{0:T(1024)S(1)}, f32[9728]{0:T(1024)}, u32[]{:S(2)}) copy-start(f32[9728]{0:T(1024)} %param.17) | copy-start | bytes 116740
  87.5 134.2 %copy-start = (f32[231936]{0:T(1024)S(1)}, f32[231936]{0:T(1024)}, u32[]{:S(2)}) copy-start(f32[231936]{0:T(1024)} %param.14) | copy-start | bytes 2783236
  221.6 4.0 %copy-start.2 = (bf16[1,472,768]{2,1,0:T(8,128)(2,1)S(1)}, bf16[1,472,768]{2,1,0:T(8,128)(2,1)}, u32[]{:S(2)}) copy-start(bf16[1,472,768]{2,1,0:T(8,128)(2,1)} %get-tuple-element.77) | copy-start | bytes 2174980
  221.6 4.9 %copy-start.1 = (f32[1,472,768]{2,1,0:T(8,128)S(1)}, f32[1,472,768]{2,1,0:T(8,128)}, u32[]{:S(2)}) copy-start(f32[1,472,768]{2,1,0:T(8,128)} %get-tuple-element.78) | copy-start | bytes 4349956

commit v3 on v2

--- a/solution.py
+++ b/solution.py
@@ -417,7 +417,7 @@
         out = []
         for j, (s, n) in enumerate([(a, rows)] + [(e, EXTRA)] * extra):
             ref = self.g.at[pl.ds(s, n)]
-            out.append(remote(ref, ref, self.sem((kind, i, p, r, j)), got.at[unit, i + j], dev))
+            out.append(remote(ref, ref, self.sem((HERE, j) if kind == HERE else (kind, i, p, r, j)), got.at[unit, i + j], dev))
         return out
 
     def op(self, zs, kind, i, p, r):
@@ -580,6 +580,7 @@
     sds = jax.ShapeDtypeStruct
     n = params.shape[0] // 128
     most = max(len(ps) for ps in pieces) + 1
+    keys = len({e + (j,) for z in events for s in z for e in s for j in range(1 + pieces[e[2]][e[1]][3])})
     here = [VM(*K1_SHAPE[k]) for k in K1_OUT[1:-1]] + [VM((4 * T, T), bf16)]
     outs = pl.pallas_call(functools.partial(forward_kernel, pieces, events, weight),
         out_shape=[sds(*K1_SHAPE[k]) for k in K1_OUT] + [sds((1, LEN, D), bf16)],
@@ -588,7 +589,7 @@
             + [VM((T, D), bf16), VM((T, D), bf16), VM((D, T), bf16), VM((T, FF), bf16), VM((LT, D), f32), VM((LT, D), f32), VM((T, D), bf16), VM((T, D), bf16),
                VM((256, T), bf16), VM((T, 256), bf16), VM((256, 256), f32), VM((2, 256, 384), f32), VM((1152, 128), f32), VM((2, 768, 128), f32), VM((3, 256, 128), f32),
                VM((256, 384), bf16), VM((256, 256), bf16),
-               DMA((2,)), DMA((16, most)), DMA((16, most)), DMA((320,)), DMA((24,)), DMA((2,))],
+               DMA((2,)), DMA((16, most)), DMA((16, most)), DMA((keys + 2,)), DMA((24,)), DMA((2,))],
         compiler_params=pltpu.CompilerParams(collective_id=0, has_side_effects=True, vmem_limit_bytes=63 * 2**20),
     )(params.reshape(n, 128), x, mask, jnp.transpose(dis, (2, 0, 1)), jnp.swapaxes(cho, 1, 2), vec.reshape(-1, 128))
     return dict(zip(K1_OUT, outs)), outs[-1]
@@ -619,10 +620,10 @@
         unit = 4 * p + at.roles[r]
         if kind == TO_CORE:
             return self.copies(op, p, r, 1 - at.c, 0, MAIN, True, self.LD.at[unit], self.RD.at[unit], (zs, at.fc))
+        _, first, rows, extra = self.pieces[p][i]
         if kind == TO_V:
             n = 2 * p + r - 2
-            return self.copies(op, p, r, at.c, 0, MAIN, True, self.LV.at[n], self.RV.at[n], (zs, at.vf))
-        _, first, rows, extra = self.pieces[p][i]
+            return self.copies(op, p, r, at.c, first, rows, extra, self.LV.at[n], self.RV.at[n, i], (zs, at.vf))
         if kind == TO_U:
             return self.copies(op, p, r, at.c, first, rows, extra, self.LU.at[p], self.RU.at[p, i], (zs, at.uf))
         up = p > zs
@@ -664,13 +665,13 @@
             return
         unit = 4 * p + at.roles[r]
         self.once(zs, (TO_CORE, p, r), self.copies((HERE,), p, r, at.c, 0, MAIN, True, self.LD.at[unit], self.RD.at[unit], (zs, at.fc)))
+        path, first, rows, extra = self.pieces[p][i]
         if kind == TO_V:
-            self.add(p, r, 0, MAIN, True, [self.LD.at[unit]], False)
+            self.add(p, r, first, rows, extra, [self.LD.at[unit]], False)
             self.send(zs, op)
             return
         n = 2 * p + r
-        self.once(zs, (TO_V, p, r), self.copies((HERE,), p, r, at.c, 0, MAIN, True, self.LV.at[n], self.RV.at[n], (zs, at.fc)))
-        path, first, rows, extra = self.pieces[p][i]
+        self.once(zs, ("v", i, p, r), self.copies((HERE,), p, r, at.c, first, rows, extra, self.LV.at[n], self.RV.at[n, i], (zs, at.fc)))
         lands = [self.LD.at[unit], self.LV.at[n]]
         def arrived(land, got, key):
             self.once(zs, key, self.copies((HERE,), p, r, at.c, first, rows, extra, land, got, (zs, at.fc)))
@@ -744,7 +745,6 @@
     second = [load("w", w.at[pl.ds(6144, 3072)], g.at[pl.ds(6144, 3072)]), load("gp"), load("actT", hbm["actT"], ring)]
     tail = load("tail", hbm["tail"], g.at[pl.ds(9216, 448)])
     third = [load("w", w.at[pl.ds(3072, 3072)], g.at[pl.ds(3072, 3072)]), load("normT")]
-    fourth = [load("hat1"), load("r1"), load("small")]
     fifth = [load("w", w.at[pl.ds(2304, 768)], g.at[pl.ds(2304, 768)]), load("attT")]
     sixth = [load("q"), load("kT"), load("vv")]
     seventh = [load("xT"), load("w", w.at[pl.ds(0, 2304)], wq)]
@@ -770,29 +770,35 @@
     for t in range(3):
         dp[t] = jnp.zeros((T, D), bf16)
     ready(first)
-    norm_back_first(dctx, wproj, vec[0:1, G2:G2 + D], hat2, r2, low2, acc)
+    for n in range(3):
+        hat1[:, 256 * n:256 * n + 256] = mm_nt(dctx[0:LT, :], wproj[256 * n:256 * n + 256, :])
+    norm_back(hat1, vec[0:1, G2:G2 + D], hat2, r2, low2, acc)
+    fourth = [load("hat1"), load("r1"), load("small")]
     put_vec(vg, acc, (G2, S2, BDOWN))
     ready(second)
-    lax.fori_loop(0, 12, lambda n, _: (down_back(n, low2, g, ring, gp, vg), 0)[1], 0)
+    lax.fori_loop(0, 8, lambda n, _: (down_back(11 - n, low2, g, ring, gp, vg), 0)[1], 0)
     ready([tail])
     shared_blocks(g, 3, True)
+    slot(0)
+    slot(1)
+    lax.fori_loop(8, 12, lambda n, _: (down_back(11 - n, low2, g, ring, gp, vg), 0)[1], 0)
     def head(h):
         return pltpu.make_async_copy(hbm["pT"].at[pl.ds(pl.multiple_of(h * T, T), T)], ring.at[pl.ds(pl.multiple_of((h % 6) * T, T), T)], TS.at[h % 6])
     for h in range(6): head(h).start()
-    slot(1)
+    slot(2)
     ready(third)
     lax.fori_loop(0, 3, lambda n, _: (up_back_x(n, gp, g, hat2), 0)[1], 0)
-    slot(2)
+    slot(3)
     def woven(n, _):
         weave(normT, gp, 4, 2 - n, 3072, g, tmp, False)
-        slot(3, n == 0)
-        slot(4, n == 1)
+        slot(4, n == 0)
+        slot(5, n == 1)
         return 0
     lax.fori_loop(0, 2, woven, 0)
     shared_blocks(g, 2, True)
-    slot(5)
+    slot(6)
     lax.fori_loop(2, 3, woven, 0)
-    slot(6)
+    slot(7)
     ready(fourth)
     norm_back(hat2, vec[0:1, G1:G1 + D], hat1, r1, low1, acc)
     put_vec(vg, acc, (G1, S1, BO))
@@ -800,8 +806,8 @@
     da, dqT = low2, normT
     out_back(low1, g, attT, da)
     shared_blocks(g, 1, True)
-    slot(7)
     slot(8)
+    slot(9)
     ready(sixth)
     def pair(p, _):
         head(2 * p).wait()
@@ -811,31 +817,32 @@
         def _():
             head(2 * p + 6).start()
             head(2 * p + 7).start()
-        for i in range(6): slot(9 + i, p == i)
+        for i in range(6): slot(10 + i, p == i)
         return 0
     lax.fori_loop(0, 6, pair, 0)
     ready(seventh)
     def wove(n, _):
         weave(xT, dp, 3, n, 0, g, tmp, True)
-        for i in range(3): slot(15 + i, n == i)
+        for i in range(3): slot(16 + i, n == i)
         return 0
     lax.fori_loop(0, 3, wove, 0)
     shared_blocks(g, 0, True)
-    slot(18)
+    slot(19)
     vg[0:1, BQ:BQ + D] = jnp.sum(dp[0].astype(f32), axis=0, keepdims=True)
     vg[0:1, BV:BV + D] = jnp.sum(dp[2].astype(f32), axis=0, keepdims=True)
     vg[0:1, BPROJ:BPROJ + 256] = small[0:1, :]
     vg[0:1, BCODE:BCODE + 256] = small[1:2, :]
     vg[0:1, BCODE + 256:BCODE + 512] = small[2:3, :]
-    slot(19)
     slot(20)
+    slot(21)
     for n in range(3):
         input_back(n, dp, wq, hat1, ig)
-    slot(21)
+    slot(22)
     z, c, k = at.z, at.c, at.k
     edge = remote(total.at[pl.ds(HALF, 16)], total.at[pl.ds(0, 16)], TS.at[6], TS.at[7], (z, at.fc))
     edge.start()
-    vsum[...] = vg[...]
+    for i in range(vsum.shape[0]):
+        vsum[i:i + 1, :] = vg[0:1, 128 * i:128 * i + 128]
     edge.wait()
     part = jnp.zeros((8, 128), f32)
     n = grad.shape[0] // 6
@@ -861,96 +868,149 @@
     DMA = pltpu.SemaphoreType.DMA
     sds = jax.ShapeDtypeStruct
     most = max(len(ps) for ps in pieces)
+    keys = 32 + len({e + (j,) for z in events for s in z for e in s if e[0] in (TO_V, TO_U, TO_Z) for j in range(1 + pieces[e[2]][e[1]][3])})
     nv = vec.shape[0] + 256
     shape = dict(K1_SHAPE, ring=((FF, T), bf16), wq=((3 * D, D), bf16))
     return pl.pallas_call(functools.partial(backward_kernel, pieces, events),
-        out_shape=[sds((n, 128), f32), sds((1, nv), f32), sds((8, 128), f32), sds((1, LEN, D), f32)],
+        out_shape=[sds((n, 128), f32), sds((nv // 128, 128), f32), sds((8, 128), f32), sds((1, LEN, D), f32)],
         in_specs=[V_] + [A_] * len(K2_IN), out_specs=[V_] * 4,
         scratch_shapes=[VM((GROW, D), bf16), VM((1, vec.shape[0]), f32)] + [VM(*shape[k]) for k in K2_HERE]
             + [VM((T, D), bf16), VM((T, D), bf16), VM((24, D), f32), VM((2, 1024, 128), f32), VM((3, T, D), bf16),
                VM((16, HALF, D), bf16), VM((8, HALF, D), bf16), VM((10, HALF, D), bf16), VM((4, HALF, D), bf16), VM((HALF + 16, D), f32), VM((6 * (HALF + 16), 128), f32),
                VM((1, nv), f32), VM((count, 1, nv), f32), VM((PLANES, 1, nv), f32), VM((8, 128), f32), VM((count, 8, 128), f32), VM((PLANES, 8, 128), f32),
-               DMA((24,)), DMA((16, 2)), DMA((8, 2)), DMA((10, most, 2)), DMA((4, most, 2)), DMA((200,)), DMA((8,)), DMA((2, count + PLANES)), DMA((2, count + PLANES))],
+               DMA((24,)), DMA((16, 2)), DMA((8, most, 2)), DMA((10, most, 2)), DMA((4, most, 2)), DMA((keys + 2,)), DMA((8,)), DMA((2, count + PLANES)), DMA((2, count + PLANES))],
         compiler_params=pltpu.CompilerParams(collective_id=1, has_side_effects=True, vmem_limit_bytes=63 * 2**20),
     )(vec.reshape(-1, 128), *[hbm[k] for k in K2_IN])
 
-PIECES_OUT = (((1, 0, 64, False), (1, 64, 64, False), (1, 128, 80, False), (1, 208, 80, True)), ((0, 0, 80, False), (1, 80, 112, False), (1, 192, 96, True)),
- ((0, 0, 96, False), (0, 96, 96, False), (0, 192, 96, True)), ((0, 0, 112, False), (0, 112, 96, False), (1, 208, 80, True)))
-PIECES_BACK = (((0, 0, 80, False), (0, 80, 64, False), (1, 144, 80, False), (1, 224, 64, True)),
- ((0, 0, 80, False), (0, 80, 64, False), (1, 144, 80, False), (1, 224, 64, True)),
- ((0, 0, 80, False), (0, 80, 64, False), (1, 144, 80, False), (1, 224, 64, True)), ((0, 0, 208, False), (1, 208, 80, True)))
-SENDS_OUT = ((((0, 0, 0, 0), (2, 0, 0, 0), (2, 1, 0, 0), (0, 1, 0, 0), (2, 2, 0, 0)),
-  ((4, 0, 0, 1), (4, 1, 0, 1), (0, 2, 0, 0), (2, 3, 0, 0), (4, 2, 0, 1), (3, 0, 0, 0), (4, 0, 1, 0), (0, 3, 0, 0), (3, 1, 0, 0), (3, 2, 0, 0),
-   (3, 3, 0, 0), (4, 3, 0, 1), (4, 0, 0, 2), (3, 0, 0, 1), (4, 1, 0, 2), (4, 1, 1, 0), (3, 1, 0, 1), (4, 2, 0, 2), (3, 2, 0, 1), (3, 3, 0, 1),
-   (4, 3, 0, 2), (4, 0, 0, 3), (4, 2, 1, 0), (2, 1, 1, 0), (4, 1, 0, 3), (2, 2, 1, 0), (4, 2, 0, 3), (4, 0, 1, 1), (4, 3, 0, 3), (3, 0, 1, 0),
-   (3, 1, 1, 0), (4, 1, 1, 1), (4, 0, 2, 0)),
-  ((4, 2, 1, 1), (4, 0, 1, 2), (3, 2, 1, 0), (4, 1, 2, 0), (3, 0, 1, 1)),
-  ((4, 1, 1, 2), (4, 2, 1, 2), (3, 1, 1, 1), (4, 0, 1, 3), (3, 2, 1, 1), (4, 2, 2, 0)), (), ((4, 0, 2, 1), (3, 0, 2, 0)),
-  ((4, 1, 1, 3), (3, 1, 2, 0)), ((4, 2, 1, 3), (4, 1, 2, 1), (3, 2, 2, 0)), ((4, 0, 2, 2), (3, 0, 2, 1)), ((4, 1, 2, 2), (3, 1, 2, 1)),
-  ((4, 2, 2, 2), (4, 2, 2, 1), (3, 2, 2, 1)), ((4, 0, 2, 3), (4, 1, 2, 3), (4, 2, 2, 3), (4, 0, 3, 0), (3, 0, 3, 0), (4, 1, 3, 0), (3, 1, 3, 0)),
-  ((4, 0, 3, 2), (4, 2, 3, 0), (4, 1, 3, 2), (2, 2, 3, 0), (3, 2, 3, 0)), (), ((4, 0, 3, 1), (3, 0, 3, 1), (4, 2, 3, 1), (3, 2, 3, 1)),
-  ((4, 2, 3, 2), (4, 1, 3, 1), (3, 1, 3, 1)), ((4, 0, 3, 3),), ((4, 2, 3, 3), (4, 1, 3, 3)), (), ()),
- (((0, 0, 1, 0), (1, 0, 1, 0), (2, 0, 1, 0), (2, 1, 1, 0)),
-  ((4, 0, 0, 0), (0, 0, 0, 0), (2, 0, 0, 0), (3, 0, 0, 0), (4, 0, 1, 1), (4, 1, 1, 1), (0, 1, 1, 0), (1, 1, 1, 0), (2, 2, 1, 0), (4, 0, 2, 0),
-   (4, 1, 0, 0), (2, 1, 0, 0), (1, 2, 1, 0), (4, 0, 0, 1), (3, 1, 0, 0), (4, 0, 0, 2), (0, 1, 0, 0), (3, 0, 0, 1), (4, 2, 0, 0), (4, 1, 2, 0),
-   (2, 2, 0, 0), (4, 2, 1, 1), (0, 2, 0, 0), (1, 0, 1, 1), (3, 2, 0, 0), (4, 1, 0, 1), (4, 3, 0, 0), (4, 1, 0, 2), (2, 3, 0, 0), (0, 3, 0, 0),
-   (4, 0, 0, 3), (1, 0, 2, 0), (4, 2, 2, 0), (3, 1, 0, 1), (4, 2, 0, 1), (3, 3, 0, 0), (4, 2, 0, 2), (0, 2, 1, 0), (1, 1, 2, 0), (3, 2, 0, 1),
-   (4, 0, 2, 1), (4, 3, 0, 1), (3, 3, 0, 1), (4, 1, 0, 3), (3, 0, 1, 0), (1, 2, 2, 0), (4, 1, 2, 1), (0, 0, 1, 1), (4, 3, 0, 2), (3, 1, 1, 0),
-   (4, 2, 0, 3), (3, 2, 1, 0), (4, 3, 0, 3), (1, 0, 2, 1), (4, 2, 2, 1), (4, 0, 1, 2), (3, 0, 1, 1)),
-  ((4, 1, 1, 2), (4, 2, 1, 2), (3, 1, 1, 1), (1, 1, 2, 1), (3, 2, 1, 1), (4, 0, 3, 0)),
-  ((4, 0, 1, 3), (4, 1, 1, 3), (1, 2, 2, 1), (3, 0, 2, 0), (3, 1, 2, 0), (4, 1, 3, 0), (4, 2, 1, 3), (4, 2, 3, 0)), (), ((3, 2, 2, 0), (1, 0, 3, 0)),
-  ((4, 0, 2, 2), (3, 0, 2, 1), (4, 0, 3, 1)), ((4, 1, 2, 2), (3, 1, 2, 1), (1, 1, 3, 0), (3, 2, 2, 1)),
-  ((4, 2, 2, 2), (4, 0, 2, 3), (4, 1, 3, 1), (1, 2, 3, 0), (2, 2, 3, 0)), ((4, 1, 2, 3), (3, 0, 3, 0)), ((4, 2, 2, 3), (1, 0, 3, 1), (3, 1, 3, 0)),
-  ((4, 2, 3, 1), (4, 0, 3, 2), (1, 1, 3, 1), (4, 1, 3, 2), (3, 2, 3, 0), (3, 0, 3, 1)), ((3, 1, 3, 1),), ((4, 2, 3, 2), (3, 2, 3, 1)),
-  ((4, 0, 3, 3),), ((4, 1, 3, 3),), ((4, 2, 3, 3),), (), (), ()),
- (((0, 0, 2, 0), (1, 0, 2, 0), (2, 0, 2, 0), (2, 1, 2, 0)),
-  ((4, 0, 1, 0), (0, 0, 1, 0), (3, 0, 1, 0), (4, 0, 2, 1), (4, 1, 2, 1), (1, 1, 2, 0), (2, 2, 2, 0), (4, 0, 3, 0), (0, 1, 2, 0), (3, 0, 2, 0),
-   (1, 2, 2, 0), (3, 1, 2, 0), (4, 0, 1, 2), (4, 0, 0, 0), (0, 0, 0, 0), (4, 1, 3, 0), (2, 0, 0, 0), (4, 2, 2, 1), (1, 0, 2, 1), (3, 0, 0, 0),
-   (0, 2, 2, 0), (4, 0, 2, 2), (3, 2, 2, 0), (4, 1, 1, 0), (4, 2, 3, 0), (4, 1, 2, 2), (2, 1, 1, 0), (1, 1, 2, 1), (4, 0, 0, 1), (4, 1, 0, 0),
-   (0, 1, 0, 0), (4, 0, 0, 2), (2, 1, 0, 0), (4, 0, 3, 1), (3, 0, 0, 1), (0, 1, 1, 0), (1, 2, 2, 1), (4, 2, 2, 2), (4, 2, 0, 0), (2, 2, 0, 0),
-   (3, 1, 0, 0), (4, 1, 1, 1), (4, 1, 3, 1), (3, 2, 0, 0), (4, 1, 0, 1), (4, 3, 0, 0), (0, 2, 0, 0), (1, 0, 3, 0), (4, 0, 0, 3), (2, 3, 0, 0),
-   (4, 2, 0, 1), (3, 1, 0, 1), (0, 3, 0, 0), (4, 1, 0, 2), (3, 3, 0, 0), (4, 2, 1, 0), (1, 1, 3, 0), (4, 2, 0, 2), (3, 2, 0, 1), (4, 3, 0, 1),
-   (0, 2, 1, 0), (4, 0, 1, 1), (3, 3, 0, 1), (4, 1, 0, 3), (1, 2, 3, 0), (2, 2, 1, 0), (4, 3, 0, 2), (0, 0, 1, 1), (3, 1, 1, 0), (4, 2, 0, 3),
-   (1, 0, 3, 1), (4, 3, 0, 3), (3, 1, 1, 1), (0, 0, 2, 1), (4, 2, 1, 1), (3, 2, 1, 0)),
-  ((4, 1, 1, 2), (3, 0, 1, 1), (3, 2, 1, 1), (0, 1, 2, 1), (4, 1, 1, 3), (1, 1, 3, 1)),
-  ((4, 2, 1, 2), (4, 0, 1, 3), (0, 2, 2, 1), (3, 0, 2, 1), (4, 2, 1, 3), (3, 1, 2, 1)), (), ((3, 2, 2, 1),), ((4, 0, 2, 3), (2, 2, 3, 0)),
-  ((4, 1, 2, 3), (3, 0, 3, 0)), ((4, 2, 2, 3), (3, 1, 3, 0)), ((4, 2, 3, 1), (3, 2, 3, 0)), ((4, 0, 3, 2), (3, 0, 3, 1)),
-  ((4, 1, 3, 2), (4, 2, 3, 2), (4, 0, 3, 3), (3, 1, 3, 1), (3, 2, 3, 1)), (), ((4, 1, 3, 3),), ((4, 2, 3, 3),), (), (), (), (), ()),
- (((1, 0, 3, 0), (2, 0, 3, 0)),
-  ((4, 0, 3, 1), (1, 1, 3, 0), (2, 1, 3, 0), (2, 2, 3, 0), (4, 0, 2, 0), (1, 2, 3, 0), (3, 0, 2, 0), (3, 0, 3, 0), (4, 1, 3, 1), (1, 0, 3, 1),
-   (4, 0, 1, 0), (3, 0, 1, 0), (4, 2, 3, 1), (3, 1, 3, 0), (4, 0, 2, 2), (4, 1, 2, 0), (3, 1, 2, 0), (1, 1, 3, 1), (4, 0, 3, 2), (3, 2, 3, 0),
-   (4, 0, 1, 2), (4, 0, 0, 0), (2, 0, 0, 0), (4, 1, 3, 2), (3, 0, 0, 0), (4, 1, 2, 2), (3, 0, 3, 1), (4, 2, 2, 0), (4, 2, 3, 2), (3, 2, 2, 0),
-   (4, 0, 0, 1), (4, 1, 0, 0), (4, 0, 0, 2), (2, 1, 0, 0), (3, 0, 0, 1), (4, 0, 3, 3), (3, 1, 0, 0), (4, 1, 1, 0), (2, 1, 1, 0), (4, 2, 2, 2),
-   (4, 1, 0, 1), (3, 1, 0, 1), (4, 2, 0, 0), (4, 0, 0, 3), (2, 2, 0, 0), (4, 1, 0, 2), (3, 2, 0, 0), (4, 3, 0, 0), (4, 1, 1, 1), (2, 3, 0, 0),
-   (4, 1, 0, 3), (3, 3, 0, 0), (4, 2, 0, 1), (3, 2, 0, 1), (4, 2, 1, 0), (4, 2, 0, 2), (2, 2, 1, 0), (4, 3, 0, 1), (4, 0, 1, 1), (3, 3, 0, 1),
-   (4, 3, 0, 2), (3, 1, 1, 0), (4, 2, 0, 3), (4, 0, 2, 1), (3, 1, 1, 1), (4, 2, 1, 1), (4, 3, 0, 3), (3, 2, 1, 0), (4, 1, 2, 1), (4, 1, 1, 2),
-   (3, 0, 1, 1)),
-  ((4, 1, 1, 3), (3, 2, 1, 1)), ((4, 2, 1, 2), (4, 0, 1, 3), (4, 2, 1, 3), (4, 2, 2, 1), (3, 0, 2, 1), (3, 1, 2, 1)), (), ((3, 2, 2, 1),),
-  ((4, 0, 2, 3), (3, 1, 3, 1)), ((4, 1, 2, 3), (3, 2, 3, 1)), ((4, 2, 2, 3),), ((4, 1, 3, 3),), ((4, 2, 3, 3),), (), (), (), (), (), (), (), (), ()))
-SENDS_BACK = (((), ((0, 0, 3, 0),), (), ((1, 0, 3, 2), (1, 0, 3, 3)), (), ((0, 0, 2, 0),), (), ((3, 0, 3, 0), (1, 0, 2, 2), (1, 0, 2, 3), (3, 0, 3, 1)),
-  ((0, 0, 1, 0),), ((2, 1, 3, 1),), ((3, 0, 2, 0), (1, 0, 1, 2), (3, 1, 2, 0)), ((1, 0, 1, 3),), ((3, 1, 3, 0), (3, 0, 2, 1), (2, 2, 2, 1)),
-  ((3, 1, 2, 1), (2, 3, 2, 1)), ((3, 0, 1, 0),), ((3, 1, 1, 0),), ((3, 0, 1, 1), (2, 2, 1, 1), (2, 3, 1, 1)), ((3, 2, 2, 0),), ((0, 0, 0, 0),), (),
-  ((5, 0, 0, 0), (3, 3, 2, 0)),
-  ((3, 1, 1, 1), (1, 0, 0, 2), (3, 2, 1, 0), (1, 0, 0, 3), (5, 1, 0, 0), (3, 3, 1, 0), (2, 2, 0, 1), (2, 3, 0, 1), (2, 0, 0, 1), (2, 1, 0, 1),
-   (5, 2, 0, 0), (4, 0, 0, 0), (4, 2, 0, 0), (4, 1, 0, 0), (4, 3, 0, 0))),
- ((), ((0, 0, 3, 0),), (), ((1, 0, 3, 2), (1, 0, 3, 3)), (), ((0, 0, 2, 0),), (), ((1, 0, 2, 2), (1, 0, 2, 3)), ((0, 0, 1, 0),), ((2, 1, 3, 1),),
-  ((1, 0, 1, 2),), ((3, 0, 3, 0), (1, 0, 1, 3)), (), ((2, 2, 2, 1), (3, 0, 3, 1), (2, 3, 2, 1)), ((3, 0, 2, 0),), ((3, 1, 2, 0),), (),
-  ((3, 1, 3, 0), (2, 2, 1, 1), (2, 3, 1, 1)), ((0, 0, 0, 0), (3, 0, 2, 1)), (), ((5, 0, 0, 0),),
-  ((3, 1, 2, 1), (1, 0, 0, 2), (1, 0, 0, 3), (2, 0, 1, 1), (3, 2, 2, 0), (3, 3, 2, 0), (5, 1, 0, 0), (2, 1, 1, 1), (2, 2, 0, 1), (2, 3, 0, 1),
-   (4, 0, 1, 0), (4, 2, 1, 0), (4, 1, 1, 0), (4, 3, 1, 0), (5, 2, 0, 0), (3, 0, 0, 0), (3, 1, 0, 0), (3, 0, 0, 1), (3, 1, 0, 1), (3, 2, 0, 0),
-   (3, 3, 0, 0))),
- ((), ((0, 0, 3, 0),), (), ((1, 0, 3, 2), (1, 0, 3, 3)), (), ((0, 0, 2, 0),), (), ((1, 0, 2, 2), (1, 0, 2, 3)), ((0, 0, 1, 0),), ((2, 1, 3, 1),),
-  ((1, 0, 1, 2),), (), ((1, 0, 1, 3),), ((2, 2, 2, 1),), ((2, 3, 2, 1),), ((3, 0, 3, 0),), (), (),
-  ((0, 0, 0, 0), (3, 0, 1, 0), (2, 2, 1, 1), (2, 3, 1, 1)), (), ((5, 0, 0, 0), (3, 0, 3, 1), (3, 1, 1, 0), (1, 0, 0, 2)),
-  ((3, 0, 1, 1), (3, 1, 1, 1), (1, 0, 0, 3), (3, 1, 3, 0), (2, 0, 2, 1), (2, 1, 2, 1), (5, 1, 0, 0), (3, 2, 1, 0), (2, 2, 0, 1), (2, 3, 0, 1),
-   (4, 0, 2, 0), (3, 3, 1, 0), (4, 1, 2, 0), (4, 2, 2, 0), (3, 0, 0, 0), (5, 2, 0, 0), (4, 3, 2, 0), (3, 1, 0, 0), (3, 0, 0, 1), (3, 1, 0, 1),
-   (3, 2, 0, 0), (3, 3, 0, 0))),
- ((), ((0, 0, 3, 0),), (), ((1, 0, 3, 2), (1, 0, 3, 3)), (), ((0, 0, 2, 0),), (), ((1, 0, 2, 2), (1, 0, 2, 3)), ((0, 0, 1, 0),), ((2, 1, 3, 1),),
-  ((1, 0, 1, 2), (3, 0, 2, 0), (3, 1, 2, 0)), ((1, 0, 1, 3),), ((3, 0, 2, 1), (3, 1, 2, 1)), ((2, 2, 2, 1), (2, 3, 2, 1)),
-  ((3, 0, 1, 0), (3, 1, 1, 0)), (), (), ((3, 0, 1, 1), (3, 1, 1, 1), (3, 2, 2, 0), (2, 2, 1, 1), (2, 3, 1, 1)), ((0, 0, 0, 0), (3, 3, 2, 0)), (),
-  ((5, 0, 0, 0),),
-  ((3, 2, 1, 0), (3, 3, 1, 0), (1, 0, 0, 2), (1, 0, 0, 3), (2, 0, 3, 1), (5, 1, 0, 0), (4, 1, 3, 0), (3, 0, 0, 0), (3, 1, 0, 0), (3, 0, 0, 1),
-   (3, 1, 0, 1), (5, 2, 0, 0), (2, 2, 0, 1), (2, 3, 0, 1), (4, 0, 3, 0), (3, 2, 0, 0), (3, 3, 0, 0))))
+def update_kernel(total, g, p, m1, m2, vg, v, v1, v2, sq, np_, low, n1, n2, nv, nv1, nv2, loss, norm, scale):
+    @pl.when(pl.program_id(0) == 0)
+    def _():
+        n = v.shape[0]
+        gv = vg[0:n, :]
+        s = jnp.sum(jnp.sum(sq[...], axis=0, keepdims=True), axis=1, keepdims=True)
+        s = s + jnp.sum(jnp.sum(gv * gv, axis=0, keepdims=True), axis=1, keepdims=True)
+        s = jnp.sqrt(s)
+        f = jnp.minimum(1.0, clip_level / (s + 1e-06))
+        norm[...] = s
+        loss[...] = vg[n:n + 1, 0:1] / total
+        scale[...] = jnp.broadcast_to(f, (8, 128))
+        nv[...], nv1[...], nv2[...] = adamw_update(v[...], v1[...], v2[...], gv * f, rate_vector)
+    new, first, second = adamw_update(p[...], m1[...], m2[...], g[...] * scale[0:1, 0:1], rate_matrix)
+    np_[...] = new
+    low[...] = new.astype(bf16)
+    n1[...] = first
+    n2[...] = second
+
+def update(total, g, p, m1, m2, vg, v, v1, v2, sq):
+    n, nv = g.shape[0], v.shape[0] // 128
+    sds = jax.ShapeDtypeStruct
+    rows = 608
+    part = pl.BlockSpec((rows, 128), lambda i: (i, 0))
+    def whole(*shape): return pl.BlockSpec(shape, lambda i: (0, 0))
+    flat = lambda a: a.reshape(-1, 128)
+    out = pl.pallas_call(functools.partial(update_kernel, total), grid=(pl.cdiv(n, rows),),
+        out_shape=[sds((n, 128), f32), sds((n, 128), bf16), sds((n, 128), f32), sds((n, 128), f32)] + [sds((nv, 128), f32)] * 3 + [sds((1, 1), f32)] * 2,
+        in_specs=[part] * 4 + [whole(*vg.shape)] + [whole(nv, 128)] * 3 + [whole(8, 128)],
+        out_specs=[part] * 4 + [whole(nv, 128)] * 3 + [whole(1, 1)] * 2,
+        scratch_shapes=[pltpu.VMEM((8, 128), f32)],
+    )(g, flat(p), flat(m1), flat(m2), vg, flat(v), flat(v1), flat(v2), sq)
+    return [a.reshape(-1) for a in out[:7]] + [a.reshape(()) for a in out[7:]]
+
+PIECES_OUT = (((0, 0, 48, False), (0, 48, 48, False), (0, 96, 48, False), (1, 144, 48, False), (1, 192, 48, False), (1, 240, 48, True)),
+ ((0, 0, 96, False), (0, 96, 96, False), (1, 192, 96, True)), ((1, 0, 96, False), (1, 96, 96, False), (1, 192, 96, True)),
+ ((0, 0, 144, False), (0, 144, 144, True)))
+PIECES_BACK = (((0, 0, 80, False), (0, 80, 64, False), (1, 144, 48, False), (1, 192, 48, False), (1, 240, 48, True)),
+ ((0, 0, 80, False), (0, 80, 64, False), (1, 144, 48, False), (1, 192, 48, False), (1, 240, 48, True)),
+ ((0, 0, 80, False), (0, 80, 64, False), (1, 144, 48, False), (1, 192, 48, False), (1, 240, 48, True)),
+ ((0, 0, 96, False), (0, 96, 96, False), (0, 192, 96, True)))
+SENDS_OUT = ((((0, 0, 0, 0), (0, 1, 0, 0), (2, 0, 0, 0), (2, 1, 0, 0), (2, 2, 0, 0)),
+  ((0, 2, 0, 0), (0, 3, 0, 0), (2, 3, 0, 0), (2, 4, 0, 0), (2, 5, 0, 0), (4, 0, 0, 1), (4, 1, 0, 1), (0, 4, 0, 0), (4, 2, 0, 1), (3, 0, 0, 0),
+   (3, 1, 0, 0), (4, 0, 1, 0), (4, 3, 0, 1), (0, 5, 0, 0), (3, 2, 0, 0), (4, 4, 0, 1), (3, 3, 0, 0), (3, 4, 0, 0), (4, 5, 0, 1), (0, 0, 0, 1),
+   (3, 5, 0, 0), (4, 0, 0, 2), (4, 1, 1, 0), (4, 1, 0, 2), (3, 0, 0, 1), (0, 1, 0, 1), (4, 2, 0, 2), (3, 1, 0, 1), (4, 3, 0, 2), (3, 2, 0, 1),
+   (0, 2, 0, 1), (4, 4, 0, 2), (3, 3, 0, 1), (4, 2, 1, 0), (3, 4, 0, 1), (4, 5, 0, 2), (3, 5, 0, 1), (4, 0, 0, 3), (4, 1, 0, 3), (2, 2, 1, 0),
+   (4, 2, 0, 3), (4, 0, 1, 1), (4, 3, 0, 3), (3, 0, 1, 0), (4, 4, 0, 3), (4, 5, 0, 3), (3, 1, 1, 0), (4, 1, 1, 1), (3, 2, 1, 0), (4, 2, 1, 1)),
+  (), ((4, 0, 1, 2), (4, 1, 1, 2), (3, 0, 1, 1), (3, 1, 1, 1), (4, 0, 2, 0), (4, 2, 1, 2)), (), ((3, 2, 1, 1), (4, 1, 2, 0)),
+  ((4, 0, 1, 3), (2, 0, 2, 0)), ((4, 1, 1, 3), (2, 1, 2, 0), (4, 2, 2, 0)), ((4, 2, 1, 3), (2, 2, 2, 0)),
+  ((4, 0, 2, 1), (3, 0, 2, 0), (4, 0, 3, 0), (4, 1, 2, 1), (3, 1, 2, 0)), ((3, 2, 2, 0), (4, 2, 2, 1)),
+  ((4, 0, 2, 2), (4, 1, 2, 2), (3, 0, 2, 1), (3, 1, 2, 1), (4, 1, 3, 0), (4, 2, 2, 2), (3, 2, 2, 1), (4, 0, 2, 3), (3, 0, 3, 0), (4, 0, 3, 1),
+   (4, 1, 2, 3), (3, 1, 3, 0), (4, 2, 2, 3), (3, 0, 3, 1), (4, 1, 3, 1), (4, 0, 3, 2)),
+  (), ((3, 1, 3, 1),), ((4, 1, 3, 2),), (), ((4, 0, 3, 3),), ((4, 1, 3, 3),), (), ()),
+ (((0, 0, 1, 0), (2, 0, 1, 0), (2, 1, 1, 0), (1, 0, 1, 0)),
+  ((0, 1, 1, 0), (4, 0, 0, 0), (3, 0, 0, 0), (2, 2, 1, 0), (4, 0, 1, 1), (1, 1, 1, 0), (0, 0, 0, 0), (4, 1, 0, 0), (3, 1, 0, 0), (4, 1, 1, 1),
+   (3, 0, 1, 0), (1, 2, 1, 0), (0, 1, 0, 0), (4, 0, 0, 2), (4, 2, 0, 0), (4, 0, 2, 0), (3, 2, 0, 0), (0, 2, 0, 0), (4, 2, 1, 1), (2, 3, 0, 0),
+   (4, 3, 0, 0), (4, 1, 0, 2), (3, 3, 0, 0), (0, 3, 0, 0), (3, 1, 1, 0), (4, 4, 0, 0), (1, 0, 1, 1), (4, 0, 1, 2), (4, 1, 2, 0), (0, 4, 0, 0),
+   (2, 4, 0, 0), (4, 2, 0, 2), (3, 4, 0, 0), (4, 5, 0, 0), (4, 3, 0, 1), (0, 5, 0, 0), (2, 5, 0, 0), (4, 3, 0, 2), (1, 1, 1, 1), (4, 0, 0, 1),
+   (3, 5, 0, 0), (4, 2, 2, 0), (4, 1, 1, 2), (0, 0, 0, 1), (3, 3, 0, 1), (4, 1, 0, 1), (4, 4, 0, 1), (3, 0, 0, 1), (4, 4, 0, 2), (0, 1, 0, 1),
+   (3, 1, 0, 1), (4, 2, 0, 1), (4, 5, 0, 1), (3, 4, 0, 1), (1, 0, 2, 0), (0, 2, 0, 1), (4, 5, 0, 2), (3, 2, 0, 1), (4, 0, 3, 0), (4, 3, 0, 3),
+   (3, 5, 0, 1), (0, 2, 1, 0), (4, 0, 0, 3), (3, 2, 1, 0), (1, 1, 2, 0), (4, 1, 0, 3), (4, 4, 0, 3), (3, 0, 1, 1), (4, 2, 0, 3), (1, 2, 2, 0),
+   (4, 1, 3, 0), (0, 0, 1, 1), (4, 5, 0, 3), (3, 1, 1, 1), (3, 2, 1, 1), (4, 2, 1, 2)),
+  ((0, 1, 1, 1), (4, 0, 1, 3), (2, 0, 2, 0), (1, 0, 3, 0), (4, 0, 3, 1)),
+  ((4, 1, 1, 3), (4, 2, 1, 3), (2, 1, 2, 0), (2, 2, 2, 0), (1, 1, 3, 0), (4, 0, 2, 1)), (), ((3, 0, 2, 0), (4, 1, 3, 1)),
+  ((4, 1, 2, 1), (3, 1, 2, 0)), ((4, 2, 2, 1), (3, 2, 2, 0), (1, 0, 3, 1)), ((4, 0, 2, 2), (3, 0, 2, 1)),
+  ((4, 1, 2, 2), (3, 1, 2, 1), (1, 1, 3, 1), (3, 2, 2, 1), (4, 2, 2, 2)), (), ((4, 0, 2, 3), (4, 1, 2, 3), (3, 0, 3, 0), (4, 2, 2, 3), (3, 1, 3, 0)),
+  ((3, 0, 3, 1),), ((4, 0, 3, 2),), ((3, 1, 3, 1),), ((4, 1, 3, 2),), ((4, 0, 3, 3),), ((4, 1, 3, 3),), (), ()),
+ (((0, 0, 2, 0), (2, 0, 2, 0), (2, 1, 2, 0), (1, 0, 2, 0)),
+  ((0, 1, 2, 0), (2, 2, 2, 0), (4, 0, 2, 1), (3, 0, 2, 0), (1, 1, 2, 0), (0, 2, 2, 0), (4, 0, 1, 0), (4, 1, 2, 1), (3, 0, 1, 0), (1, 2, 2, 0),
+   (4, 0, 3, 0), (3, 1, 2, 0), (4, 2, 2, 1), (4, 1, 1, 0), (0, 0, 1, 0), (3, 1, 1, 0), (4, 0, 2, 2), (1, 0, 3, 0), (4, 0, 0, 0), (3, 0, 0, 0),
+   (4, 0, 1, 2), (3, 2, 2, 0), (4, 1, 0, 0), (0, 0, 0, 0), (4, 1, 2, 2), (4, 1, 3, 0), (3, 1, 0, 0), (4, 2, 0, 0), (0, 1, 0, 0), (4, 1, 1, 2),
+   (3, 2, 0, 0), (1, 1, 3, 0), (2, 3, 0, 0), (0, 2, 0, 0), (4, 0, 0, 2), (4, 3, 0, 0), (3, 3, 0, 0), (3, 0, 2, 1), (4, 4, 0, 0), (0, 3, 0, 0),
+   (4, 2, 2, 2), (4, 1, 0, 2), (4, 0, 3, 1), (2, 4, 0, 0), (4, 2, 0, 2), (0, 4, 0, 0), (4, 5, 0, 0), (2, 5, 0, 0), (4, 3, 0, 1), (4, 3, 0, 2),
+   (0, 5, 0, 0), (4, 0, 0, 1), (3, 4, 0, 0), (3, 5, 0, 0), (1, 0, 3, 1), (4, 0, 2, 3), (4, 1, 0, 1), (3, 3, 0, 1), (0, 0, 0, 1), (4, 4, 0, 1),
+   (3, 0, 0, 1), (4, 1, 3, 1), (4, 5, 0, 1), (4, 2, 0, 1), (0, 1, 0, 1), (4, 4, 0, 2), (3, 1, 0, 1), (3, 4, 0, 1), (1, 1, 3, 1), (4, 5, 0, 2),
+   (0, 2, 0, 1), (3, 5, 0, 1), (4, 3, 0, 3), (3, 2, 0, 1), (4, 0, 0, 3), (0, 1, 1, 0), (2, 2, 1, 0), (4, 2, 1, 0), (4, 1, 0, 3), (4, 4, 0, 3),
+   (3, 2, 1, 0), (4, 5, 0, 3), (0, 2, 1, 0), (4, 2, 0, 3), (4, 0, 1, 1), (3, 0, 1, 1), (4, 2, 1, 1), (3, 2, 1, 1)),
+  (), ((0, 0, 1, 1), (4, 1, 1, 1), (4, 2, 1, 2), (4, 0, 1, 3), (3, 1, 1, 1), (3, 1, 2, 1), (4, 2, 1, 3), (0, 1, 1, 1)), (), ((3, 2, 2, 1),),
+  ((4, 1, 1, 3), (3, 0, 3, 0)), ((4, 1, 2, 3),), ((4, 2, 2, 3), (3, 1, 3, 0)), ((3, 0, 3, 1),), ((4, 0, 3, 2),), ((4, 1, 3, 2), (3, 1, 3, 1)),
+  ((4, 0, 3, 3),), (), (), ((4, 1, 3, 3),), (), (), (), ()),
+ (((2, 0, 3, 0), (1, 0, 3, 0)),
+  ((2, 1, 3, 0), (1, 1, 3, 0), (3, 0, 3, 0), (4, 0, 3, 1), (4, 0, 2, 0), (2, 0, 2, 0), (4, 1, 3, 1), (3, 0, 2, 0), (4, 1, 2, 0), (1, 0, 3, 1),
+   (2, 1, 2, 0), (4, 0, 3, 2), (3, 1, 2, 0), (4, 0, 2, 1), (4, 2, 2, 0), (2, 2, 2, 0), (4, 0, 2, 2), (1, 1, 3, 1), (4, 1, 2, 1), (3, 0, 2, 1),
+   (4, 0, 1, 0), (4, 1, 2, 2), (3, 0, 1, 0), (4, 0, 0, 0), (3, 0, 0, 0), (4, 2, 2, 1), (4, 1, 0, 0), (3, 1, 0, 0), (3, 2, 2, 0), (4, 0, 2, 3),
+   (4, 2, 0, 0), (4, 0, 1, 2), (3, 2, 0, 0), (4, 3, 0, 0), (4, 0, 0, 2), (2, 3, 0, 0), (4, 1, 0, 2), (3, 3, 0, 0), (4, 4, 0, 0), (2, 4, 0, 0),
+   (3, 4, 0, 0), (4, 2, 2, 2), (4, 5, 0, 0), (2, 5, 0, 0), (4, 2, 0, 2), (4, 3, 0, 1), (3, 5, 0, 0), (4, 0, 0, 1), (4, 3, 0, 2), (3, 3, 0, 1),
+   (4, 4, 0, 1), (3, 0, 0, 1), (4, 1, 0, 1), (4, 4, 0, 2), (3, 4, 0, 1), (4, 5, 0, 1), (4, 2, 0, 1), (3, 1, 0, 1), (3, 5, 0, 1), (4, 5, 0, 2),
+   (4, 3, 0, 3), (3, 2, 0, 1), (4, 0, 0, 3), (3, 1, 2, 1), (4, 1, 1, 0), (4, 4, 0, 3), (4, 1, 0, 3), (3, 1, 1, 0), (4, 5, 0, 3), (3, 2, 2, 1),
+   (4, 2, 0, 3), (4, 2, 1, 0), (4, 1, 2, 3), (2, 2, 1, 0)),
+  (), ((4, 1, 1, 2), (4, 0, 1, 1), (3, 2, 1, 0), (4, 2, 2, 3), (3, 0, 1, 1), (4, 2, 1, 1)), (), ((4, 1, 1, 1), (3, 2, 1, 1)),
+  ((4, 2, 1, 2), (3, 1, 1, 1)), ((4, 0, 1, 3), (3, 1, 3, 0)), ((4, 2, 1, 3),), ((4, 1, 1, 3), (3, 0, 3, 1)), ((3, 1, 3, 1),),
+  ((4, 1, 3, 2), (4, 0, 3, 3)), (), ((4, 1, 3, 3),), (), (), (), (), (), ()))
+SENDS_BACK = (((), ((0, 0, 3, 0),), (), ((1, 0, 3, 2), (1, 1, 3, 2)), ((1, 2, 3, 2),), ((1, 0, 3, 3),), ((0, 0, 2, 0), (3, 0, 3, 0)), ((1, 1, 3, 3), (3, 1, 3, 0)),
+  ((1, 2, 3, 3), (3, 2, 3, 0), (1, 0, 2, 2)), ((0, 0, 1, 0), (1, 1, 2, 2)), ((1, 2, 2, 2), (1, 3, 2, 2)), ((3, 0, 3, 1), (1, 4, 2, 2), (1, 0, 2, 3)),
+  ((3, 1, 3, 1), (1, 0, 1, 2)), ((1, 1, 1, 2),), ((3, 2, 3, 1), (1, 2, 1, 2), (1, 3, 1, 2), (1, 4, 1, 2)), ((1, 0, 1, 3),),
+  ((1, 1, 1, 3), (3, 0, 1, 0)), ((1, 2, 1, 3), (1, 3, 1, 3)), ((1, 4, 1, 3), (3, 1, 1, 0), (1, 1, 2, 3)), ((0, 0, 0, 0),), (),
+  ((5, 0, 0, 0), (1, 2, 2, 3)),
+  ((2, 2, 1, 1), (2, 3, 1, 1), (3, 0, 1, 1), (1, 0, 0, 2), (3, 1, 1, 1), (1, 1, 0, 2), (1, 2, 0, 2), (3, 0, 2, 0), (1, 3, 0, 2), (1, 4, 0, 2),
+   (1, 0, 0, 3), (3, 2, 1, 0), (1, 1, 0, 3), (5, 1, 0, 0), (3, 3, 1, 0), (1, 2, 0, 3), (1, 3, 0, 3), (3, 1, 2, 0), (1, 4, 0, 3), (2, 4, 1, 1),
+   (3, 0, 2, 1), (1, 3, 2, 3), (1, 4, 2, 3), (2, 2, 0, 1), (3, 1, 2, 1), (2, 3, 0, 1), (2, 4, 0, 1), (3, 4, 1, 0), (5, 2, 0, 0), (2, 2, 2, 1),
+   (2, 3, 2, 1), (2, 4, 2, 1), (3, 2, 2, 0), (3, 3, 2, 0), (3, 4, 2, 0), (2, 0, 0, 1), (2, 1, 0, 1), (4, 0, 0, 0), (4, 2, 0, 0), (4, 1, 0, 0),
+   (4, 3, 0, 0), (4, 4, 0, 0))),
+ ((), ((0, 0, 3, 0),), (), ((1, 0, 3, 2), (1, 1, 3, 2)), ((1, 2, 3, 2),), ((1, 0, 3, 3),), ((0, 0, 2, 0),), ((1, 1, 3, 3),),
+  ((1, 2, 3, 3), (1, 0, 2, 2)), ((0, 0, 1, 0), (3, 0, 3, 0)), ((1, 1, 2, 2), (1, 2, 2, 2)), ((3, 1, 3, 0), (1, 3, 2, 2), (1, 4, 2, 2)),
+  ((1, 0, 1, 2), (1, 1, 1, 2)), ((3, 2, 3, 0), (1, 2, 1, 2), (1, 3, 1, 2)), ((1, 4, 1, 2),), ((3, 0, 3, 1), (1, 0, 1, 3), (1, 1, 1, 3)),
+  ((1, 2, 1, 3),), ((3, 1, 3, 1), (1, 3, 1, 3), (1, 4, 1, 3)), ((1, 0, 2, 3),), ((0, 0, 0, 0),), ((1, 1, 2, 3),), ((5, 0, 0, 0),),
+  ((3, 2, 3, 1), (2, 2, 1, 1), (1, 0, 0, 2), (1, 1, 0, 2), (1, 2, 0, 2), (1, 3, 0, 2), (1, 4, 0, 2), (1, 0, 0, 3), (1, 1, 0, 3), (1, 2, 0, 3),
+   (1, 3, 0, 3), (1, 4, 0, 3), (2, 3, 1, 1), (2, 4, 1, 1), (5, 1, 0, 0), (3, 0, 2, 0), (2, 0, 1, 1), (2, 2, 0, 1), (4, 2, 1, 0), (2, 3, 0, 1),
+   (2, 4, 0, 1), (2, 1, 1, 1), (3, 1, 2, 0), (1, 2, 2, 3), (4, 0, 1, 0), (3, 0, 0, 0), (1, 3, 2, 3), (1, 4, 2, 3), (3, 0, 2, 1), (3, 1, 0, 0),
+   (4, 1, 1, 0), (5, 2, 0, 0), (3, 1, 2, 1), (2, 2, 2, 1), (3, 0, 0, 1), (2, 3, 2, 1), (2, 4, 2, 1), (3, 1, 0, 1), (3, 2, 2, 0), (3, 2, 0, 0),
+   (3, 3, 2, 0), (3, 3, 0, 0), (3, 4, 2, 0), (3, 4, 0, 0), (4, 3, 1, 0), (4, 4, 1, 0))),
+ ((), ((0, 0, 3, 0),), (), ((1, 0, 3, 2), (1, 1, 3, 2)), ((1, 2, 3, 2),), ((1, 0, 3, 3),), ((0, 0, 2, 0),), ((1, 1, 3, 3),),
+  ((1, 2, 3, 3), (1, 0, 2, 2)), ((0, 0, 1, 0),), ((1, 1, 2, 2), (1, 2, 2, 2)), ((1, 3, 2, 2), (1, 4, 2, 2)), ((1, 0, 2, 3), (3, 0, 3, 0)),
+  ((1, 0, 1, 2), (1, 1, 1, 2)), ((3, 1, 3, 0), (1, 2, 1, 2), (1, 3, 1, 2)), ((1, 4, 1, 2),), ((1, 0, 1, 3),),
+  ((3, 2, 3, 0), (1, 1, 1, 3), (1, 2, 1, 3)), ((1, 3, 1, 3),), ((0, 0, 0, 0), (1, 4, 1, 3)), (), ((5, 0, 0, 0), (3, 0, 3, 1), (1, 1, 2, 3)),
+  ((2, 2, 1, 1), (1, 0, 0, 2), (3, 0, 1, 0), (1, 1, 0, 2), (3, 1, 3, 1), (3, 1, 1, 0), (1, 2, 0, 2), (1, 3, 0, 2), (1, 4, 0, 2), (3, 0, 1, 1),
+   (1, 0, 0, 3), (3, 2, 3, 1), (1, 1, 0, 3), (3, 1, 1, 1), (1, 2, 0, 3), (5, 1, 0, 0), (1, 3, 0, 3), (1, 4, 0, 3), (2, 3, 1, 1), (3, 2, 1, 0),
+   (2, 4, 1, 1), (1, 2, 2, 3), (2, 2, 0, 1), (3, 0, 0, 0), (2, 3, 0, 1), (2, 4, 0, 1), (3, 1, 0, 0), (1, 3, 2, 3), (1, 4, 2, 3), (2, 2, 2, 1),
+   (3, 0, 0, 1), (5, 2, 0, 0), (3, 1, 0, 1), (2, 3, 2, 1), (2, 4, 2, 1), (3, 2, 0, 0), (3, 3, 0, 0), (2, 0, 2, 1), (3, 4, 0, 0), (2, 1, 2, 1),
+   (3, 3, 1, 0), (4, 0, 2, 0), (4, 1, 2, 0), (3, 4, 1, 0), (4, 2, 2, 0), (4, 3, 2, 0), (4, 4, 2, 0))),
+ ((), ((0, 0, 3, 0),), (), ((1, 0, 3, 2), (1, 1, 3, 2)), ((1, 2, 3, 2),), ((1, 0, 3, 3),), ((0, 0, 2, 0),), ((1, 1, 3, 3),),
+  ((1, 2, 3, 3), (1, 0, 2, 2)), ((0, 0, 1, 0),), ((1, 1, 2, 2), (1, 2, 2, 2)), ((1, 3, 2, 2), (1, 4, 2, 2)), ((1, 0, 2, 3), (3, 0, 2, 0)),
+  ((1, 0, 1, 2), (1, 1, 1, 2), (3, 1, 2, 0)), ((1, 2, 1, 2), (1, 3, 1, 2)), ((1, 4, 1, 2), (3, 0, 2, 1), (1, 0, 1, 3)), ((3, 0, 1, 0), (1, 1, 1, 3)),
+  ((1, 2, 1, 3), (3, 1, 1, 0)), ((1, 3, 1, 3), (1, 4, 1, 3)), ((0, 0, 0, 0),), ((1, 1, 2, 3),), ((5, 0, 0, 0), (3, 0, 1, 1)),
+  ((2, 2, 1, 1), (3, 1, 1, 1), (1, 0, 0, 2), (1, 1, 0, 2), (1, 2, 0, 2), (1, 3, 0, 2), (3, 1, 2, 1), (1, 4, 0, 2), (3, 2, 1, 0), (1, 0, 0, 3),
+   (3, 0, 0, 0), (1, 1, 0, 3), (1, 2, 0, 3), (1, 3, 0, 3), (5, 1, 0, 0), (3, 1, 0, 0), (1, 4, 0, 3), (2, 0, 3, 1), (3, 0, 0, 1), (2, 1, 3, 1),
+   (2, 2, 0, 1), (3, 1, 0, 1), (2, 3, 0, 1), (2, 4, 0, 1), (4, 0, 3, 0), (2, 2, 3, 1), (4, 1, 3, 0), (2, 3, 1, 1), (3, 2, 0, 0), (2, 4, 1, 1),
+   (5, 2, 0, 0), (3, 3, 0, 0), (1, 2, 2, 3), (3, 4, 0, 0), (1, 3, 2, 3), (1, 4, 2, 3), (4, 2, 3, 0), (3, 3, 1, 0), (3, 4, 1, 0), (2, 2, 2, 1),
+   (2, 3, 2, 1), (2, 4, 2, 1), (3, 2, 2, 0), (3, 3, 2, 0), (3, 4, 2, 0))))
 
 def unpack(flat_values):
     shapes = [(D, 3 * D), (D, D), (D, FF), (FF, D), (D, FINAL), (G * CD, V), (G * CD, FINAL)]
@@ -1012,6 +1072,26 @@
 
 def column_sum(values):
     return jnp.sum(values.astype(jnp.float32), axis=tuple(range(values.ndim - 1)))
+
+
+def finish(total_masked, square_sum, vector_sum, loss_sum, grad_shard, output, input_grad, params, moment_one, moment_two, vectors, vector_one, vector_two):
+    grad_norm = jnp.sqrt(square_sum + jnp.sum(vector_sum * vector_sum))
+    factor = jnp.minimum(1.0, clip_level / (grad_norm + 1e-06))
+    refreshed_weights, new_one, new_two = adamw_update(params, moment_one, moment_two, grad_shard * factor, rate_matrix)
+    new_vectors, new_vector_first, new_vector_second = adamw_update(vectors, vector_one, vector_two, vector_sum * factor, rate_vector)
+    return (
+        loss_sum / total_masked,
+        grad_norm,
+        output,
+        input_grad,
+        refreshed_weights,
+        refreshed_weights.astype(bf16),
+        new_one,
+        new_two,
+        new_vectors,
+        new_vector_first,
+        new_vector_second,
+    )
 
 
 def by_collectives(
@@ -1181,35 +1261,14 @@
     )
 
 
-def finish(total_masked, square_sum, vector_sum, loss_sum, grad_shard, output, input_grad, params, moment_one, moment_two, vectors, vector_one, vector_two):
-    grad_norm = jnp.sqrt(square_sum + jnp.sum(vector_sum * vector_sum))
-    factor = jnp.minimum(1.0, clip_level / (grad_norm + 1e-06))
-    refreshed_weights, new_one, new_two = adamw_update(params, moment_one, moment_two, grad_shard * factor, rate_matrix)
-    new_vectors, new_vector_first, new_vector_second = adamw_update(vectors, vector_one, vector_two, vector_sum * factor, rate_vector)
-    return (
-        loss_sum / total_masked,
-        grad_norm,
-        output,
-        input_grad,
-        refreshed_weights,
-        refreshed_weights.astype(bf16),
-        new_one,
-        new_two,
-        new_vectors,
-        new_vector_first,
-        new_vector_second,
-    )
-
-
 def by_kernels(layer_input, mask_index, distract, code_choice, params, moment_one, moment_two, vectors, vector_one, vector_two):
     total_masked = layer_input.shape[0] * lax.axis_size(("dp", "fsdp")) * MASKED
     kept, output = forward(PIECES_OUT, SENDS_OUT, 1.0 / total_masked, params, layer_input, mask_index, distract, code_choice, vectors)
     grads, sums, squares, input_grad = backward(PIECES_BACK, SENDS_BACK, vectors, kept, lax.axis_size("fsdp"), params.shape[0] // 128)
-    sums = sums.reshape(-1)
-    return finish(
-        total_masked, jnp.sum(squares), sums[: vectors.shape[0]], sums[vectors.shape[0]], grads.reshape(-1), output, input_grad,
-        params, moment_one, moment_two, vectors, vector_one, vector_two,
-    )
+    new, low, first, second, new_v, first_v, second_v, loss, norm = update(
+        total_masked, grads, params, moment_one, moment_two, sums, vectors, vector_one, vector_two, squares
+    )
+    return loss, norm, output, input_grad, new, low, first, second, new_v, first_v, second_v
 
 
 def solution(mesh):

time: 230 us -> 199 us (0.87)
  Pallas kernels: 213 us -> 197 us
  other arithmetic: 9.07 us -> 0 us
  between operations: 4.99 us -> 0.69 us
    pallas_call x1, Pallas kernels: 126 us -> 102 us  [backward(): pl.pallas_call(functools.partial(backward_kernel, pieces, events), out_sh...]
    pallas_call x0 -> x1, Pallas kernels: none -> 5.58 us  [update(): pl.pallas_call(functools.partial(update_kernel, total), grid=(pl.cdiv(n,...]
    convert_element_type x1 -> x0, other arithmetic: 3.98 us -> none  [finish(): refreshed_weights.astype(bf16)]
    reduce_sum x2 -> x0, other arithmetic: 2.75 us -> none  [the longest x1 1.46 us: finish(): grad_norm = jnp.sqrt(square_sum + jnp.sum(vector_sum * vector_sum))]
where the time goes in v3:
time: 199 us
  Pallas kernels  197 us (99%)
    pallas_call x1, Pallas kernels, backward(): pl.pallas_call(functools.partial(backward_kernel, pieces, events), out_sh...  102 us
    pallas_call x1, Pallas kernels, forward(): pl.pallas_call(functools.partial(forward_kernel, pieces, events, weight),...  88.6 us
    pallas_call x1, Pallas kernels, update(): pl.pallas_call(functools.partial(update_kernel, total), grid=(pl.cdiv(n,...  5.58 us

profile of v3, /device:TPU:0, one launch (start us, length us, event | category | flops | bytes accessed | tf_op | source)
XLA Modules:
  0.0 199.2 jit_solution(14144789560565112787)
XLA Ops:
  0.6 88.6 %shard_map.185 = (bf16[9664,768]{1,0:T(8,128)(2,1)}, bf16[768,256]{1,0:T(8,128)(2,1)}, bf16[448,768]{1,0:T(8,128)(2,1)}, bf16[512,256]{1,0:T(8,128)(2,1)}, f32[8...) custom-call(f32[1812,128]{1,0:T(8,128)} %bitcast.17, ...), custom_call_target="tpu_custom_call" | custom-call | tf_op jit(solution)/shard_map/pallas_call | solution.py:585
  89.3 102.4 %shard_map.186 = (f32[1812,128]{1,0:T(8,128)}, f32[78,128]{1,0:T(8,128)}, f32[8,128]{1,0:T(8,128)}, f32[1,472,768]{2,1,0:T(8,128)}) custom-call(f32[76,128]{1,0:T(8,128)} %bitcast.22, bf16[9664,768]{1,0:T(8,128)(2,1)} %get-tuple-element.43.rest_0_, bf16[768,256]{1,0:T(8,128)(2,1)} %get-tuple-element.44.rest_1_, bf16[448,768]{1,0:T(8,128)(2,1)} %get-tuple-element.45.rest_2_, ...), custom_call_target="tpu_custom_call" | custom-call | tf_op jit(solution)/shard_map/pallas_call | solution.py:874
  191.6 0.0 copy-start.1
  191.6 0.0 copy-start
  191.6 5.6 %shard_map.187 = (f32[1812,128]{1,0:T(8,128)}, bf16[1812,128]{1,0:T(8,128)(2,1)}, f32[1812,128]{1,0:T(8,128)}, f32[1812,128]{1,0:T(8,128)}, f32[76,128]{1,0:T(8,...) custom-call(f32[1812,128]{1,0:T(8,128)} %get-tuple-element.61.g, ...), custom_call_target="tpu_custom_call" | custom-call | tf_op jit(solution)/shard_map/pallas_call | solution.py:911
  197.2 0.0 copy-done.1
  197.2 0.9 copy.23
  198.1 0.0 copy-done
  198.1 1.1 copy.24
Async XLA Ops:
  191.6 5.6 %copy-start.1 = (bf16[1,472,768]{2,1,0:T(8,128)(2,1)S(1)}, bf16[1,472,768]{2,1,0:T(8,128)(2,1)}, u32[]{:S(2)}) copy-start(bf16[1,472,768]{2,1,0:T(8,128)(2,1)} %get-tuple-element.88) | copy-start | bytes 2174980
  191.6 6.5 %copy-start = (f32[1,472,768]{2,1,0:T(8,128)S(1)}, f32[1,472,768]{2,1,0:T(8,128)}, u32[]{:S(2)}) copy-start(f32[1,472,768]{2,1,0:T(8,128)} %get-tuple-element.89) | copy-start | bytes 4349956

commit v4 on v3

--- a/solution.py
+++ b/solution.py
@@ -10,6 +10,9 @@
 NROW = 9664; GROW = NROW + 256
 T = 512
 LT = 480
+NB = 240
+TILE = 768
+STEP_T = 512
 bf16 = jnp.bfloat16
 f32 = jnp.float32
 NT = (((1,), (1,)), ((), ()))
@@ -38,28 +41,29 @@
 
 def norm_rows(r, gain, shift, low, wide, hat, rstd):
     def body(b, _):
-        at = pl.multiple_of(b * 48, 16)
-        v = r[pl.ds(at, 48), :]
+        at = pl.multiple_of(b * NB, 16)
+        v = r[pl.ds(at, NB), :]
         m = jnp.mean(v, axis=-1, keepdims=True)
         c = v - m
         var = jnp.mean(c * c, axis=-1, keepdims=True)
         inv = lax.rsqrt(var + eps_norm)
         xh = c * inv
         o = xh * gain + shift
-        hat[pl.ds(at, 48), :] = xh
-        rstd[pl.ds(at, 48), :] = jnp.broadcast_to(inv, (48, 128))
+        hat[pl.ds(at, NB), :] = xh
+        rstd[pl.ds(at, NB), :] = jnp.broadcast_to(inv, (NB, 128))
         if wide is not None:
-            wide[pl.ds(at, 48), :] = o
-        low[pl.ds(at, 48), :] = o.astype(bf16)
+            wide[pl.ds(at, NB), :] = o
+        low[pl.ds(at, NB), :] = o.astype(bf16)
         return 0
-    lax.fori_loop(0, LT // 48, body, 0)
+    lax.fori_loop(0, LT // NB, body, 0)
 
 def transpose_to(src, dst, rows, cols):
+    step = min(STEP_T, cols // 3)
     def body(n, _):
-        at = pl.multiple_of(n * 128, 128)
-        dst[pl.ds(at, 128), :] = src[:, pl.ds(at, 128)].T
+        at = pl.multiple_of(n * step, step)
+        dst[pl.ds(at, step), :] = src[:, pl.ds(at, step)].T
         return 0
-    lax.fori_loop(0, cols // 128, body, 0)
+    lax.fori_loop(0, cols // step, body, 0)
 
 def prepare(x_ref, xp, xT, mask_ref, distract_ref, choice_ref, vec_ref, vec, place, placeT, allowed, choose):
     for i in range(vec_ref.shape[0]):
@@ -127,13 +131,13 @@
 def up(n, norm_low, nice, vec, act, gp):
     root = 0.7071067811865476
     scale = 0.3989422804014327
-    c = n // 3
-    w = nice[pl.ds(pl.multiple_of(c * D, D), D), pl.ds(pl.multiple_of((n - 3 * c) * 256, 256), 256)]
-    at = pl.multiple_of(n * 256, 256)
-    h = mm(norm_low[0:LT, :], w) + vec[0:1, pl.ds(pl.multiple_of(BUP + n * 256, 256), 256)]
+    c = n * TILE // D
+    at = pl.multiple_of(n * TILE, TILE)
+    w = nice[pl.ds(pl.multiple_of(c * D, D), D), pl.ds(pl.multiple_of(at - c * D, TILE), TILE)]
+    h = mm(norm_low[0:LT, :], w) + vec[0:1, pl.ds(pl.multiple_of(BUP + at, 256), TILE)]
     cdf = 0.5 * (1.0 + lax.erf(h * root))
-    act[0:LT, pl.ds(at, 256)] = (h * cdf).astype(bf16)
-    gp[0:LT, pl.ds(at, 256)] = (cdf + h * (scale * jnp.exp(-0.5 * h * h))).astype(bf16)
+    act[0:LT, pl.ds(at, TILE)] = (h * cdf).astype(bf16)
+    gp[0:LT, pl.ds(at, TILE)] = (cdf + h * (scale * jnp.exp(-0.5 * h * h))).astype(bf16)
 
 def down(act, g, vec, res, wide):
     for n in range(3):
@@ -241,15 +245,15 @@
     lax.fori_loop(0, LT // 48, body, 0)
 
 def norm_back_rows(dy, at, gain, hat, dst, rstd, low, acc):
-    xh = hat[pl.ds(at, 48), :]
-    inv = rstd[pl.ds(at, 48), 0:1]
+    xh = hat[pl.ds(at, NB), :]
+    inv = rstd[pl.ds(at, NB), 0:1]
     a = dy * gain
     m1 = jnp.mean(a, axis=-1, keepdims=True)
     m2 = jnp.mean(a * xh, axis=-1, keepdims=True)
     dr = inv * (a - m1 - xh * m2)
     lo = dr.astype(bf16)
-    dst[pl.ds(at, 48), :] = dr
-    low[pl.ds(at, 48), :] = lo
+    dst[pl.ds(at, NB), :] = dr
+    low[pl.ds(at, NB), :] = lo
     acc[0:8, :] += sum8(dy * xh)
     acc[8:16, :] += sum8(dy)
     acc[16:24, :] += sum8(lo.astype(f32))
@@ -257,23 +261,23 @@
 def norm_back(dy, gain, hat, rstd, low, acc):
     acc[...] = jnp.zeros((24, D), f32)
     def body(b, _):
-        at = pl.multiple_of(b * 48, 16)
-        norm_back_rows(dy[pl.ds(at, 48), :], at, gain, hat, hat, rstd, low, acc)
+        at = pl.multiple_of(b * NB, 16)
+        norm_back_rows(dy[pl.ds(at, NB), :], at, gain, hat, hat, rstd, low, acc)
         return 0
-    lax.fori_loop(0, LT // 48, body, 0)
+    lax.fori_loop(0, LT // NB, body, 0)
 
 def put_vec(vg, acc, offsets):
     for i, o in enumerate(offsets):
         vg[0:1, o:o + D] = jnp.sum(acc[8 * i:8 * i + 8, :], axis=0, keepdims=True)
 
 def down_back(n, low2, gg, actT, gp, vg):
-    at = pl.multiple_of(n * 256, 256)
-    rows = pl.ds(pl.multiple_of(6144 + n * 256, 256), 256)
-    d = mm_nt(low2[0:LT, :], gg[rows, :]) * gp[0:LT, pl.ds(at, 256)].astype(f32)
+    at = pl.multiple_of(n * TILE, TILE)
+    rows = pl.ds(pl.multiple_of(6144 + n * TILE, 256), TILE)
+    d = mm_nt(low2[0:LT, :], gg[rows, :]) * gp[0:LT, pl.ds(at, TILE)].astype(f32)
     d = d.astype(bf16)
-    gp[0:LT, pl.ds(at, 256)] = d
-    vg[0:1, pl.ds(pl.multiple_of(BUP + at, 128), 256)] = jnp.sum(d.astype(f32), axis=0, keepdims=True)
-    gg[rows, :] = mm(actT[pl.ds(at, 256), :], low2[...]).astype(bf16)
+    gp[0:LT, pl.ds(at, TILE)] = d
+    vg[0:1, pl.ds(pl.multiple_of(BUP + at, 128), TILE)] = jnp.sum(d.astype(f32), axis=0, keepdims=True)
+    gg[rows, :] = mm(actT[pl.ds(at, TILE), :], low2[...]).astype(bf16)
 
 def up_back_x(n, dh, gg, dr):
     cols = pl.ds(pl.multiple_of(n * 256, 256), 256)
@@ -341,6 +345,7 @@
 MAIN = 288
 EXTRA = 16
 HALF = MAIN + EXTRA
+RAW = 96
 PLANE = 2416
 UNIT = 608
 
@@ -378,26 +383,29 @@
             pl.semaphore_signal(bar, inc=1, device_id=(lax.rem(self.z + j, PLANES), self.f), device_id_type=MESH)
         pl.semaphore_wait(bar, count + PLANES - 2)
 
-    def span(self, p, r, c, first):
-        kk = self.roles[r]
+    def span_of(self, p, kk, c, first):
         m = PLANE * p + UNIT * kk
         return (pl.multiple_of(m + HALF * c + first, 16),
                 pl.multiple_of((m + MAIN) * (1 - c) + (NROW + EXTRA * (4 * p + kk)) * c, 16))
 
+    def span(self, p, r, c, first):
+        return self.span_of(p, self.roles[r], c, first)
+
 def remote(src, dst, ssem, rsem, dev):
     return pltpu.make_async_remote_copy(src_ref=src, dst_ref=dst, send_sem=ssem, recv_sem=rsem, device_id=dev, device_id_type=MESH)
 
-def shared_blocks(g, p, out):
+def shared_blocks(g, p):
     row = lax.broadcasted_iota(jnp.int32, (16, D), 0)
-    if out:
-        b = [g[PLANE * p + 16 * q:PLANE * p + 16 * q + 16, :].astype(f32) for q in (37, 75, 113)]
-        for q, v in enumerate((b[0], jnp.where(row < 8, b[1], b[0]), jnp.where(row < 4, b[2], b[1]), b[2])):
-            g[NROW + 16 * (4 * p + q):NROW + 16 * (4 * p + q) + 16, :] = v.astype(bf16)
-    else:
-        e = [g[NROW + 16 * (4 * p + q):NROW + 16 * (4 * p + q) + 16, :].astype(f32) for q in range(4)]
-        for q, bound in enumerate((12, 8, 4)):
-            at = PLANE * p + UNIT * q + 592
-            g[at:at + 16, :] = jnp.where(row < bound, e[q], e[q + 1]).astype(bf16)
+    e = [g[NROW + 16 * (4 * p + q):NROW + 16 * (4 * p + q) + 16, :].astype(f32) for q in range(4)]
+    for q, bound in enumerate((12, 8, 4)):
+        at = PLANE * p + UNIT * q + 592
+        g[at:at + 16, :] = jnp.where(row < bound, e[q], e[q + 1]).astype(bf16)
+
+def extra_rows(g, p, q):
+    row = lax.broadcasted_iota(jnp.int32, (16, D), 0)
+    b = [g[PLANE * p + UNIT * i + 592:PLANE * p + UNIT * i + 608, :].astype(f32) for i in range(max(q - 1, 0), min(q, 2) + 1)]
+    v = b[0] if len(b) == 1 else jnp.where(row < 12 - 4 * q, b[1], b[0])
+    g[NROW + 16 * (4 * p + q):NROW + 16 * (4 * p + q) + 16, :] = v.astype(bf16)
 
 class Gather:
     def __init__(self, at, g, pieces, R, O, S):
@@ -442,28 +450,27 @@
                 for kind, i, p, r in self.made[zs]:
                     for q in self.copies(i, p, r, (zs, self.at.fc), kind, self.at.c): q.wait_send()
 
-def own_rows(at, g, p_ref, raw, land, sem):
+def own_rows(at, g, p_ref, raw, sem):
     n = p_ref.shape[0]
-    copy = remote(p_ref.at[pl.ds(0, n)], land.at[pl.ds(0, n)], sem.at[0], sem.at[1], (at.z, at.fc))
-    copy.start()
-    @pl.when(at.c == 0)
-    def _(): raw[96:96 + n, :] = p_ref[...]
-    @pl.when(at.c == 1)
-    def _(): raw[96 + n:96 + 2 * n, :] = p_ref[...]
-    copy.wait()
-    @pl.when(at.c == 1)
-    def _(): raw[96:96 + n, :] = land[0:n]
-    @pl.when(at.c == 0)
-    def _(): raw[96 + n:96 + 2 * n, :] = land[0:n]
+    gap = -n % 8
+    base = pl.multiple_of(RAW + (n + gap) * at.c, 8)
+    mine = pltpu.make_async_copy(p_ref.at[pl.ds(0, n)], raw.at[pl.ds(base, n)], sem.at[2])
+    mine.start()
+    both = remote(p_ref.at[pl.ds(0, n)], raw.at[pl.ds(base, n)], sem.at[0], sem.at[1], (at.z, at.fc))
+    both.start()
+    mine.wait()
+    both.wait()
     k = at.k
     own = pl.multiple_of(PLANE * at.z + UNIT * k, 16)
     extra = pl.multiple_of(NROW + EXTRA * (4 * at.z + k), 16)
     row = lax.broadcasted_iota(jnp.int32, (16, 128), 0)
+    first_core = lax.broadcasted_iota(jnp.int32, (592, 128), 0) + 4 * k < n // 6
     for j in range(6):
         cols = slice(128 * j, 128 * j + 128)
-        g[pl.ds(own, 592), cols] = raw[pl.ds(96 + 24 * k + j, 592, stride=6), :].astype(bf16)
-        last = raw[pl.ds(96 + (592 + 4 * k) * 6 + j, 16, stride=6), :]
-        first = raw[pl.ds(24 * k + j, 16, stride=6), :]
+        v = [raw[pl.ds(RAW + gap * i + 24 * k + j, 592, stride=6), :] for i in range(2)]
+        g[pl.ds(own, 592), cols] = jnp.where(first_core, v[0], v[1]).astype(bf16)
+        last = raw[pl.ds(RAW + gap + (592 + 4 * k) * 6 + j, 16, stride=6), :]
+        first = raw[pl.ds(RAW - 96 + 24 * k + j, 16, stride=6), :]
         g[pl.ds(extra, 16), cols] = jnp.where(row < 12 - 4 * k, last, first).astype(bf16)
 
 K1_OUT = ("w", "wproj", "tail", "dctx", "small", "hat1", "r1", "hat2", "r2", "gp", "actT", "normT", "attT", "q", "kT", "vv", "xT", "pT")
@@ -475,7 +482,7 @@
 def forward_kernel(pieces, events, weight, p_ref, x, mask, dis, cho, vec_ref, *rest):
     n_out = len(K1_OUT)
     hbm = dict(zip(K1_OUT, rest[:n_out]))
-    (out, vec, g, raw, land, nice, tmp, wproj, tail, dctx, small, hat1, r1, hat2, r2, gp, actT, normT, attT, q, kT, vv, xT, pT,
+    (out, vec, g, raw, nice, tmp, wproj, tail, dctx, small, hat1, r1, hat2, r2, gp, actT, normT, attT, q, kT, vv, xT, pT,
      xp, kk, vT, act, res, wide, low1, low2, place, placeT, allowed, choose, fb, p32, c32, code, wcode,
      sem_raw, R, O, S, OS, PS) = rest[n_out:]
     here = dict(wproj=wproj, tail=tail, dctx=dctx, small=small, hat1=hat1, r1=r1, hat2=hat2, r2=r2, gp=gp, actT=actT, normT=normT, attT=attT, q=q, kT=kT, vv=vv, xT=xT, pT=pT)
@@ -490,7 +497,7 @@
     at = Place()
     ga = Gather(at, g, pieces, R, O, S)
     at.greet()
-    own_rows(at, g, p_ref, raw, land, sem_raw)
+    own_rows(at, g, p_ref, raw, sem_raw)
     def slot(i, cond=None):
         for zs in range(PLANES):
             if events[zs][i]:
@@ -501,7 +508,7 @@
         for zs in range(PLANES):
             @pl.when(at.z == zs)
             def _(): ga.other_core(zs, p)
-        shared_blocks(g, p, False)
+        shared_blocks(g, p)
     slot(0)
     prepare(x, xp, xT, mask, dis, cho, vec_ref, vec, place, placeT, allowed, choose)
     act[LT:T, :] = jnp.zeros((T - LT, FF), bf16)
@@ -523,14 +530,19 @@
     def pair_out(p):
         b = p % 2
         return pltpu.make_async_copy(pT.at[pl.ds(pl.multiple_of(2 * T * b, T), 2 * T)], hbm["pT"].at[pl.ds(pl.multiple_of(2 * T * p, T), 2 * T)], PS.at[b])
-    def pair(p, _):
-        @pl.when(p >= 2)
-        def _(): pair_out(p - 2).wait()
+    def pairs(b, _):
+        p = 2 * b
+        @pl.when(b > 0)
+        def _():
+            pair_out(p - 2).wait()
+            pair_out(p - 1).wait()
         attend(p, q, kk, vT, pT, attT)
+        attend(p + 1, q, kk, vT, pT, attT)
         pair_out(p).start()
-        for i in range(6): slot(5 + i, p == i)
+        pair_out(p + 1).start()
+        for i in range(3): slot(5 + i, b == i)
         return 0
-    lax.fori_loop(0, H // 2, pair, 0)
+    lax.fori_loop(0, H // 4, pairs, 0)
     pair_out(H // 2 - 2).wait()
     pair_out(H // 2 - 1).wait()
     save("attT")
@@ -541,22 +553,22 @@
     save("hat1", "r1")
     transpose_to(low1, normT, T, D)
     save("normT")
-    slot(11)
+    slot(8)
     plane(2)
     nice_out.wait()
     split_rows(g, 3072, 4, nice, 0, tmp)
     put(nice, hbm["w"].at[pl.ds(3072, 3072)])
-    slot(12)
+    slot(9)
     def tile(n, _):
         up(n, low1, nice, vec, act, gp)
-        for i in range(3): slot(13 + i, n == 3 * i + 2)
+        for i in range(3): slot(10 + i, n == i)
         return 0
-    lax.fori_loop(0, 12, tile, 0)
-    slot(16)
+    lax.fori_loop(0, FF // TILE, tile, 0)
+    slot(13)
     save("gp")
     transpose_to(act, actT, T, FF)
     save("actT")
-    slot(17)
+    slot(14)
     plane(3)
     put(g.at[pl.ds(6144, 3072)], hbm["w"].at[pl.ds(6144, 3072)])
     down(act, g, vec, res, wide)
@@ -565,10 +577,10 @@
     out[0] = low2[0:LEN, :]
     small_weights(g, fb, p32, c32, wproj, code, wcode)
     save("wproj")
-    slot(18)
+    slot(15)
     contrast(weight, low2, vec, place, placeT, allowed, choose, wproj, code, wcode, fb, p32, c32, tail, dctx, small)
     save("tail", "dctx", "small")
-    slot(19)
+    slot(16)
     ga.drain()
     for cp in outs: cp.wait()
 
@@ -584,22 +596,22 @@
     here = [VM(*K1_SHAPE[k]) for k in K1_OUT[1:-1]] + [VM((4 * T, T), bf16)]
     outs = pl.pallas_call(functools.partial(forward_kernel, pieces, events, weight),
         out_shape=[sds(*K1_SHAPE[k]) for k in K1_OUT] + [sds((1, LEN, D), bf16)],
-        in_specs=[V_] * 6, out_specs=[A_] * len(K1_OUT) + [V_],
-        scratch_shapes=[VM((1, vec.shape[0]), f32), VM((GROW, D), bf16), VM((96 + 2 * n + 96, 128), f32), VM((n + 4, 128), f32), VM((4 * D, D), bf16), VM((6, 256, 128), f32)] + here
+        in_specs=[A_] + [V_] * 5, out_specs=[A_] * len(K1_OUT) + [V_],
+        scratch_shapes=[VM((1, vec.shape[0]), f32), VM((GROW, D), bf16), VM((RAW + 2 * (n + 4) + 96, 128), f32), VM((4 * D, D), bf16), VM((6, 256, 128), f32)] + here
             + [VM((T, D), bf16), VM((T, D), bf16), VM((D, T), bf16), VM((T, FF), bf16), VM((LT, D), f32), VM((LT, D), f32), VM((T, D), bf16), VM((T, D), bf16),
                VM((256, T), bf16), VM((T, 256), bf16), VM((256, 256), f32), VM((2, 256, 384), f32), VM((1152, 128), f32), VM((2, 768, 128), f32), VM((3, 256, 128), f32),
                VM((256, 384), bf16), VM((256, 256), bf16),
-               DMA((2,)), DMA((16, most)), DMA((16, most)), DMA((keys + 2,)), DMA((24,)), DMA((2,))],
+               DMA((3,)), DMA((16, most)), DMA((16, most)), DMA((keys + 2,)), DMA((24,)), DMA((2,))],
         compiler_params=pltpu.CompilerParams(collective_id=0, has_side_effects=True, vmem_limit_bytes=63 * 2**20),
     )(params.reshape(n, 128), x, mask, jnp.transpose(dis, (2, 0, 1)), jnp.swapaxes(cho, 1, 2), vec.reshape(-1, 128))
     return dict(zip(K1_OUT, outs)), outs[-1]
 TO_CORE, TO_V, TO_U, TO_Z, KEEP, SMALL = range(6)
 
 class Reduce:
-    def __init__(self, at, g, pieces, LD, LV, LZ, LU, total, RD, RV, RZ, RU, S):
+    def __init__(self, at, g, pieces, LD, LV, LZ, LU, total, RD, RV, RZ, RU, S, SD):
         self.at, self.g, self.pieces, self.total = at, g, pieces, total
         self.LD, self.LV, self.LZ, self.LU = LD, LV, LZ, LU
-        self.RD, self.RV, self.RZ, self.RU, self.S = RD, RV, RZ, RU, S
+        self.RD, self.RV, self.RZ, self.RU, self.S, self.SD = RD, RV, RZ, RU, S, SD
         self.index = {}
         self.made = {z: [] for z in range(PLANES)}
         self.seen = set()
@@ -618,8 +630,6 @@
         at = self.at
         kind, i, p, r = op
         unit = 4 * p + at.roles[r]
-        if kind == TO_CORE:
-            return self.copies(op, p, r, 1 - at.c, 0, MAIN, True, self.LD.at[unit], self.RD.at[unit], (zs, at.fc))
         _, first, rows, extra = self.pieces[p][i]
         if kind == TO_V:
             n = 2 * p + r - 2
@@ -660,9 +670,6 @@
     def op(self, zs, op):
         at = self.at
         kind, i, p, r = op
-        if kind == TO_CORE:
-            for rr in (2, 3, 0, 1): self.send(zs, (TO_CORE, 0, p, rr))
-            return
         unit = 4 * p + at.roles[r]
         self.once(zs, (TO_CORE, p, r), self.copies((HERE,), p, r, at.c, 0, MAIN, True, self.LD.at[unit], self.RD.at[unit], (zs, at.fc)))
         path, first, rows, extra = self.pieces[p][i]
@@ -686,12 +693,26 @@
         self.add(p, r, first, rows, extra, lands, kind == KEEP)
         if kind != KEEP: self.send(zs, op)
 
+    def core_copies(self, p, kk):
+        a, e = self.at.span_of(p, kk, 1 - self.at.c, 0)
+        land = self.LD.at[4 * p + kk]
+        dev = (self.at.z, self.at.fc)
+        return [remote(self.g.at[pl.ds(s, n)], land.at[pl.ds(to, n)], self.SD.at[4 * p + kk, j], self.RD.at[4 * p + kk, j], dev)
+                for j, (s, n, to) in enumerate(((a, MAIN, 0), (e, EXTRA, MAIN)))]
+
+    def to_core(self, p, kk):
+        extra_rows(self.g, p, kk)
+        for q in self.core_copies(p, kk): q.start()
+
     def drain(self):
         for zs in range(PLANES):
             @pl.when(self.at.z == zs)
             def _():
                 for op in self.made[zs]:
                     for q in self.build(zs, op): q.wait_send()
+        for p in range(PLANES):
+            for kk in range(4):
+                for q in self.core_copies(p, kk): q.wait_send()
 
 class Spread:
     def __init__(self, at, own, land, zland, S, count):
@@ -730,9 +751,9 @@
 def backward_kernel(pieces, events, vec_ref, *rest):
     n_in = len(K2_IN)
     hbm = dict(zip(K2_IN, rest[:n_in]))
-    (grad, vsum, sq, ig, g, vec, wproj, dctx, small, hat1, r1, hat2, r2, gp, ring, normT, attT, q, kT, vv, xT, wq,
+    (grad, vsum, sq, ig_out, ig, g, vec, wproj, dctx, small, hat1, r1, hat2, r2, gp, ring, normT, attT, q, kT, vv, xT, wq,
      low1, low2, acc, tmp, dp, LD, LV, LZ, LU, total, flat, vg, vland, vzland, sqv, sland, szland,
-     IS, RD, RV, RZ, RU, S, TS, VS, SS) = rest[n_in:]
+     IS, RD, RV, RZ, RU, S, SD, TS, TL, VS, SS) = rest[n_in:]
     here = dict(wproj=wproj, dctx=dctx, small=small, hat1=hat1, r1=r1, hat2=hat2, r2=r2, gp=gp, normT=normT, attT=attT, q=q, kT=kT, vv=vv, xT=xT)
     loads = {}
     def load(name, src=None, dst=None):
@@ -742,7 +763,13 @@
         return cp
     w = hbm["w"]
     first = [load(n) for n in ("dctx", "wproj", "hat2", "r2")]
-    second = [load("w", w.at[pl.ds(6144, 3072)], g.at[pl.ds(6144, 3072)]), load("gp"), load("actT", hbm["actT"], ring)]
+    def second(n):
+        rows = pl.ds(pl.multiple_of(6144 + n * TILE, 256), TILE)
+        own = pl.ds(pl.multiple_of(n * TILE, TILE), TILE)
+        pairs = ((w.at[rows], g.at[rows]), (hbm["actT"].at[own], ring.at[own]), (hbm["gp"].at[:, own], gp.at[:, own]))
+        return [pltpu.make_async_copy(s, d, TL.at[3 * n + i]) for i, (s, d) in enumerate(pairs)]
+    for n in range(FF // TILE - 1, -1, -1):
+        for cp in second(n): cp.start()
     tail = load("tail", hbm["tail"], g.at[pl.ds(9216, 448)])
     third = [load("w", w.at[pl.ds(3072, 3072)], g.at[pl.ds(3072, 3072)]), load("normT")]
     fifth = [load("w", w.at[pl.ds(2304, 768)], g.at[pl.ds(2304, 768)]), load("attT")]
@@ -752,7 +779,7 @@
         for cp in cs: cp.wait()
     at = Place()
     at.greet_all(vland.shape[0])
-    re = Reduce(at, g, pieces, LD, LV, LZ, LU, total, RD, RV, RZ, RU, S)
+    re = Reduce(at, g, pieces, LD, LV, LZ, LU, total, RD, RV, RZ, RU, S, SD)
     vs = Spread(at, vg, vland, vzland, VS, vland.shape[0])
     ss = Spread(at, sqv, sland, szland, SS, vland.shape[0])
     def slot(i, cond=None):
@@ -775,13 +802,19 @@
     norm_back(hat1, vec[0:1, G2:G2 + D], hat2, r2, low2, acc)
     fourth = [load("hat1"), load("r1"), load("small")]
     put_vec(vg, acc, (G2, S2, BDOWN))
-    ready(second)
-    lax.fori_loop(0, 8, lambda n, _: (down_back(11 - n, low2, g, ring, gp, vg), 0)[1], 0)
     ready([tail])
-    shared_blocks(g, 3, True)
+    def downs(n, _):
+        ready(second(3 - n))
+        down_back(3 - n, low2, g, ring, gp, vg)
+        for kk, last in ((3, 0), (2, 0), (1, 1), (0, 2)):
+            @pl.when(n == last)
+            def _(): re.to_core(3, kk)
+        return 0
+    lax.fori_loop(0, 3, downs, 0)
     slot(0)
     slot(1)
-    lax.fori_loop(8, 12, lambda n, _: (down_back(11 - n, low2, g, ring, gp, vg), 0)[1], 0)
+    ready(second(0))
+    down_back(0, low2, g, ring, gp, vg)
     def head(h):
         return pltpu.make_async_copy(hbm["pT"].at[pl.ds(pl.multiple_of(h * T, T), T)], ring.at[pl.ds(pl.multiple_of((h % 6) * T, T), T)], TS.at[h % 6])
     for h in range(6): head(h).start()
@@ -791,13 +824,17 @@
     slot(3)
     def woven(n, _):
         weave(normT, gp, 4, 2 - n, 3072, g, tmp, False)
+        for kk in range(4):
+            @pl.when(n == int(kk == 0))
+            def _(): re.to_core(2, kk)
         slot(4, n == 0)
         slot(5, n == 1)
         return 0
     lax.fori_loop(0, 2, woven, 0)
-    shared_blocks(g, 2, True)
     slot(6)
-    lax.fori_loop(2, 3, woven, 0)
+    weave(normT, gp, 4, 0, 3072, g, tmp, False)
+    re.to_core(1, 2)
+    re.to_core(1, 3)
     slot(7)
     ready(fourth)
     norm_back(hat2, vec[0:1, G1:G1 + D], hat1, r1, low1, acc)
@@ -805,60 +842,71 @@
     ready(fifth)
     da, dqT = low2, normT
     out_back(low1, g, attT, da)
-    shared_blocks(g, 1, True)
+    re.to_core(1, 0)
+    re.to_core(1, 1)
     slot(8)
     slot(9)
     ready(sixth)
-    def pair(p, _):
-        head(2 * p).wait()
-        head(2 * p + 1).wait()
-        attend_back(p, da, q, kT, vv, ring, dp, dqT)
-        @pl.when(p < 3)
-        def _():
-            head(2 * p + 6).start()
-            head(2 * p + 7).start()
-        for i in range(6): slot(10 + i, p == i)
+    def pairs(b, _):
+        for p in (2 * b, 2 * b + 1):
+            head(2 * p).wait()
+            head(2 * p + 1).wait()
+        attend_back(2 * b, da, q, kT, vv, ring, dp, dqT)
+        attend_back(2 * b + 1, da, q, kT, vv, ring, dp, dqT)
+        for p in (2 * b, 2 * b + 1):
+            @pl.when(p < 3)
+            def _():
+                head(2 * p + 6).start()
+                head(2 * p + 7).start()
+        for i in range(3): slot(10 + i, b == i)
         return 0
-    lax.fori_loop(0, 6, pair, 0)
+    lax.fori_loop(0, H // 4, pairs, 0)
     ready(seventh)
     def wove(n, _):
         weave(xT, dp, 3, n, 0, g, tmp, True)
-        for i in range(3): slot(16 + i, n == i)
+        for kk in range(4):
+            @pl.when(n == min(kk, 2))
+            def _(): re.to_core(0, kk)
+        for i in range(3): slot(13 + i, n == i)
         return 0
     lax.fori_loop(0, 3, wove, 0)
-    shared_blocks(g, 0, True)
-    slot(19)
+    slot(16)
     vg[0:1, BQ:BQ + D] = jnp.sum(dp[0].astype(f32), axis=0, keepdims=True)
     vg[0:1, BV:BV + D] = jnp.sum(dp[2].astype(f32), axis=0, keepdims=True)
     vg[0:1, BPROJ:BPROJ + 256] = small[0:1, :]
     vg[0:1, BCODE:BCODE + 256] = small[1:2, :]
     vg[0:1, BCODE + 256:BCODE + 512] = small[2:3, :]
-    slot(20)
-    slot(21)
+    slot(17)
+    slot(18)
     for n in range(3):
         input_back(n, dp, wq, hat1, ig)
-    slot(22)
+    put_ig = pltpu.make_async_copy(ig, ig_out, IS.at[len(loads)])
+    put_ig.start()
+    slot(19)
     z, c, k = at.z, at.c, at.k
     edge = remote(total.at[pl.ds(HALF, 16)], total.at[pl.ds(0, 16)], TS.at[6], TS.at[7], (z, at.fc))
     edge.start()
+    row = lax.broadcasted_iota(jnp.int32, (16, D), 0)
+    def square(b, acc):
+        v = total[pl.ds(pl.multiple_of(16 + 16 * b, 16), 16), :]
+        return acc + sum8(v * v)
+    acc = lax.fori_loop(0, MAIN // 16, square, jnp.zeros((8, D), f32))
+    v = jnp.where((c == 0) | (row < 12 - 4 * k) | (row >= 16 - 4 * k), total[16 + MAIN:16 + HALF, :], 0.0)
+    acc = acc + sum8(v * v)
+    sqv[...] = sum(acc[:, 128 * j:128 * j + 128] for j in range(6))
+    ss.first()
     for i in range(vsum.shape[0]):
         vsum[i:i + 1, :] = vg[0:1, 128 * i:128 * i + 128]
+    n = grad.shape[0] // 6
     edge.wait()
-    part = jnp.zeros((8, 128), f32)
-    n = grad.shape[0] // 6
     for j in range(6):
         flat[pl.ds(j, 320, stride=6), :] = total[:, 128 * j:128 * j + 128]
+    ss.second()
     for j in range(6):
-        v = flat[pl.ds(6 * (16 - 2 * c - 4 * k) + j, n, stride=6), :]
-        grad[pl.ds(j, n, stride=6), :] = v
-        v = v * v
-        part = part + sum8(v[0:n // 8 * 8])
-        if n % 8: part = part + jnp.concatenate([v[n // 8 * 8:], jnp.zeros((8 - n % 8, 128), f32)], axis=0)
-    sqv[...] = part
-    ss.first()
-    ss.second()
+        grad[pl.ds(j, n, stride=6), :] = flat[pl.ds(6 * (16 - 2 * c - 4 * k) + j, n, stride=6), :]
     ss.last()
     sq[...] = sqv[...]
+    put_ig.wait()
     re.drain()
 
 def backward(pieces, events, vec, hbm, count, n):
@@ -868,17 +916,17 @@
     DMA = pltpu.SemaphoreType.DMA
     sds = jax.ShapeDtypeStruct
     most = max(len(ps) for ps in pieces)
-    keys = 32 + len({e + (j,) for z in events for s in z for e in s if e[0] in (TO_V, TO_U, TO_Z) for j in range(1 + pieces[e[2]][e[1]][3])})
+    keys = len({e + (j,) for z in events for s in z for e in s if e[0] in (TO_V, TO_U, TO_Z) for j in range(1 + pieces[e[2]][e[1]][3])})
     nv = vec.shape[0] + 256
     shape = dict(K1_SHAPE, ring=((FF, T), bf16), wq=((3 * D, D), bf16))
     return pl.pallas_call(functools.partial(backward_kernel, pieces, events),
         out_shape=[sds((n, 128), f32), sds((nv // 128, 128), f32), sds((8, 128), f32), sds((1, LEN, D), f32)],
-        in_specs=[V_] + [A_] * len(K2_IN), out_specs=[V_] * 4,
-        scratch_shapes=[VM((GROW, D), bf16), VM((1, vec.shape[0]), f32)] + [VM(*shape[k]) for k in K2_HERE]
+        in_specs=[V_] + [A_] * len(K2_IN), out_specs=[V_] * 3 + [A_],
+        scratch_shapes=[VM((1, LEN, D), f32), VM((GROW, D), bf16), VM((1, vec.shape[0]), f32)] + [VM(*shape[k]) for k in K2_HERE]
             + [VM((T, D), bf16), VM((T, D), bf16), VM((24, D), f32), VM((2, 1024, 128), f32), VM((3, T, D), bf16),
                VM((16, HALF, D), bf16), VM((8, HALF, D), bf16), VM((10, HALF, D), bf16), VM((4, HALF, D), bf16), VM((HALF + 16, D), f32), VM((6 * (HALF + 16), 128), f32),
                VM((1, nv), f32), VM((count, 1, nv), f32), VM((PLANES, 1, nv), f32), VM((8, 128), f32), VM((count, 8, 128), f32), VM((PLANES, 8, 128), f32),
-               DMA((24,)), DMA((16, 2)), DMA((8, most, 2)), DMA((10, most, 2)), DMA((4, most, 2)), DMA((keys + 2,)), DMA((8,)), DMA((2, count + PLANES)), DMA((2, count + PLANES))],
+               DMA((24,)), DMA((16, 2)), DMA((8, most, 2)), DMA((10, most, 2)), DMA((4, most, 2)), DMA((keys + 2,)), DMA((16, 2)), DMA((8,)), DMA((12,)), DMA((2, count + PLANES)), DMA((2, count + PLANES))],
         compiler_params=pltpu.CompilerParams(collective_id=1, has_side_effects=True, vmem_limit_bytes=63 * 2**20),
     )(vec.reshape(-1, 128), *[hbm[k] for k in K2_IN])
 
@@ -916,101 +964,94 @@
     )(g, flat(p), flat(m1), flat(m2), vg, flat(v), flat(v1), flat(v2), sq)
     return [a.reshape(-1) for a in out[:7]] + [a.reshape(()) for a in out[7:]]
 
-PIECES_OUT = (((0, 0, 48, False), (0, 48, 48, False), (0, 96, 48, False), (1, 144, 48, False), (1, 192, 48, False), (1, 240, 48, True)),
- ((0, 0, 96, False), (0, 96, 96, False), (1, 192, 96, True)), ((1, 0, 96, False), (1, 96, 96, False), (1, 192, 96, True)),
+PIECES_OUT = (((0, 0, 48, False), (0, 48, 48, False), (0, 96, 48, False), (1, 144, 48, False), (1, 192, 32, False), (1, 224, 32, False), (1, 256, 32, True)),
+ ((0, 0, 96, False), (0, 96, 96, False), (0, 192, 96, True)), ((1, 0, 144, False), (1, 144, 144, True)), ((0, 0, 192, False), (1, 192, 96, True)))
+PIECES_BACK = (((0, 0, 48, False), (0, 48, 48, False), (0, 96, 48, False), (1, 144, 48, False), (1, 192, 32, False), (1, 224, 32, False), (1, 256, 32, True)),
+ ((0, 0, 192, False), (1, 192, 48, False), (1, 240, 48, True)), ((1, 0, 96, False), (1, 96, 96, False), (1, 192, 96, True)),
  ((0, 0, 144, False), (0, 144, 144, True)))
-PIECES_BACK = (((0, 0, 80, False), (0, 80, 64, False), (1, 144, 48, False), (1, 192, 48, False), (1, 240, 48, True)),
- ((0, 0, 80, False), (0, 80, 64, False), (1, 144, 48, False), (1, 192, 48, False), (1, 240, 48, True)),
- ((0, 0, 80, False), (0, 80, 64, False), (1, 144, 48, False), (1, 192, 48, False), (1, 240, 48, True)),
- ((0, 0, 96, False), (0, 96, 96, False), (0, 192, 96, True)))
-SENDS_OUT = ((((0, 0, 0, 0), (0, 1, 0, 0), (2, 0, 0, 0), (2, 1, 0, 0), (2, 2, 0, 0)),
-  ((0, 2, 0, 0), (0, 3, 0, 0), (2, 3, 0, 0), (2, 4, 0, 0), (2, 5, 0, 0), (4, 0, 0, 1), (4, 1, 0, 1), (0, 4, 0, 0), (4, 2, 0, 1), (3, 0, 0, 0),
-   (3, 1, 0, 0), (4, 0, 1, 0), (4, 3, 0, 1), (0, 5, 0, 0), (3, 2, 0, 0), (4, 4, 0, 1), (3, 3, 0, 0), (3, 4, 0, 0), (4, 5, 0, 1), (0, 0, 0, 1),
-   (3, 5, 0, 0), (4, 0, 0, 2), (4, 1, 1, 0), (4, 1, 0, 2), (3, 0, 0, 1), (0, 1, 0, 1), (4, 2, 0, 2), (3, 1, 0, 1), (4, 3, 0, 2), (3, 2, 0, 1),
-   (0, 2, 0, 1), (4, 4, 0, 2), (3, 3, 0, 1), (4, 2, 1, 0), (3, 4, 0, 1), (4, 5, 0, 2), (3, 5, 0, 1), (4, 0, 0, 3), (4, 1, 0, 3), (2, 2, 1, 0),
-   (4, 2, 0, 3), (4, 0, 1, 1), (4, 3, 0, 3), (3, 0, 1, 0), (4, 4, 0, 3), (4, 5, 0, 3), (3, 1, 1, 0), (4, 1, 1, 1), (3, 2, 1, 0), (4, 2, 1, 1)),
-  (), ((4, 0, 1, 2), (4, 1, 1, 2), (3, 0, 1, 1), (3, 1, 1, 1), (4, 0, 2, 0), (4, 2, 1, 2)), (), ((3, 2, 1, 1), (4, 1, 2, 0)),
-  ((4, 0, 1, 3), (2, 0, 2, 0)), ((4, 1, 1, 3), (2, 1, 2, 0), (4, 2, 2, 0)), ((4, 2, 1, 3), (2, 2, 2, 0)),
-  ((4, 0, 2, 1), (3, 0, 2, 0), (4, 0, 3, 0), (4, 1, 2, 1), (3, 1, 2, 0)), ((3, 2, 2, 0), (4, 2, 2, 1)),
-  ((4, 0, 2, 2), (4, 1, 2, 2), (3, 0, 2, 1), (3, 1, 2, 1), (4, 1, 3, 0), (4, 2, 2, 2), (3, 2, 2, 1), (4, 0, 2, 3), (3, 0, 3, 0), (4, 0, 3, 1),
-   (4, 1, 2, 3), (3, 1, 3, 0), (4, 2, 2, 3), (3, 0, 3, 1), (4, 1, 3, 1), (4, 0, 3, 2)),
-  (), ((3, 1, 3, 1),), ((4, 1, 3, 2),), (), ((4, 0, 3, 3),), ((4, 1, 3, 3),), (), ()),
- (((0, 0, 1, 0), (2, 0, 1, 0), (2, 1, 1, 0), (1, 0, 1, 0)),
-  ((0, 1, 1, 0), (4, 0, 0, 0), (3, 0, 0, 0), (2, 2, 1, 0), (4, 0, 1, 1), (1, 1, 1, 0), (0, 0, 0, 0), (4, 1, 0, 0), (3, 1, 0, 0), (4, 1, 1, 1),
-   (3, 0, 1, 0), (1, 2, 1, 0), (0, 1, 0, 0), (4, 0, 0, 2), (4, 2, 0, 0), (4, 0, 2, 0), (3, 2, 0, 0), (0, 2, 0, 0), (4, 2, 1, 1), (2, 3, 0, 0),
-   (4, 3, 0, 0), (4, 1, 0, 2), (3, 3, 0, 0), (0, 3, 0, 0), (3, 1, 1, 0), (4, 4, 0, 0), (1, 0, 1, 1), (4, 0, 1, 2), (4, 1, 2, 0), (0, 4, 0, 0),
-   (2, 4, 0, 0), (4, 2, 0, 2), (3, 4, 0, 0), (4, 5, 0, 0), (4, 3, 0, 1), (0, 5, 0, 0), (2, 5, 0, 0), (4, 3, 0, 2), (1, 1, 1, 1), (4, 0, 0, 1),
-   (3, 5, 0, 0), (4, 2, 2, 0), (4, 1, 1, 2), (0, 0, 0, 1), (3, 3, 0, 1), (4, 1, 0, 1), (4, 4, 0, 1), (3, 0, 0, 1), (4, 4, 0, 2), (0, 1, 0, 1),
-   (3, 1, 0, 1), (4, 2, 0, 1), (4, 5, 0, 1), (3, 4, 0, 1), (1, 0, 2, 0), (0, 2, 0, 1), (4, 5, 0, 2), (3, 2, 0, 1), (4, 0, 3, 0), (4, 3, 0, 3),
-   (3, 5, 0, 1), (0, 2, 1, 0), (4, 0, 0, 3), (3, 2, 1, 0), (1, 1, 2, 0), (4, 1, 0, 3), (4, 4, 0, 3), (3, 0, 1, 1), (4, 2, 0, 3), (1, 2, 2, 0),
-   (4, 1, 3, 0), (0, 0, 1, 1), (4, 5, 0, 3), (3, 1, 1, 1), (3, 2, 1, 1), (4, 2, 1, 2)),
-  ((0, 1, 1, 1), (4, 0, 1, 3), (2, 0, 2, 0), (1, 0, 3, 0), (4, 0, 3, 1)),
-  ((4, 1, 1, 3), (4, 2, 1, 3), (2, 1, 2, 0), (2, 2, 2, 0), (1, 1, 3, 0), (4, 0, 2, 1)), (), ((3, 0, 2, 0), (4, 1, 3, 1)),
-  ((4, 1, 2, 1), (3, 1, 2, 0)), ((4, 2, 2, 1), (3, 2, 2, 0), (1, 0, 3, 1)), ((4, 0, 2, 2), (3, 0, 2, 1)),
-  ((4, 1, 2, 2), (3, 1, 2, 1), (1, 1, 3, 1), (3, 2, 2, 1), (4, 2, 2, 2)), (), ((4, 0, 2, 3), (4, 1, 2, 3), (3, 0, 3, 0), (4, 2, 2, 3), (3, 1, 3, 0)),
-  ((3, 0, 3, 1),), ((4, 0, 3, 2),), ((3, 1, 3, 1),), ((4, 1, 3, 2),), ((4, 0, 3, 3),), ((4, 1, 3, 3),), (), ()),
- (((0, 0, 2, 0), (2, 0, 2, 0), (2, 1, 2, 0), (1, 0, 2, 0)),
-  ((0, 1, 2, 0), (2, 2, 2, 0), (4, 0, 2, 1), (3, 0, 2, 0), (1, 1, 2, 0), (0, 2, 2, 0), (4, 0, 1, 0), (4, 1, 2, 1), (3, 0, 1, 0), (1, 2, 2, 0),
-   (4, 0, 3, 0), (3, 1, 2, 0), (4, 2, 2, 1), (4, 1, 1, 0), (0, 0, 1, 0), (3, 1, 1, 0), (4, 0, 2, 2), (1, 0, 3, 0), (4, 0, 0, 0), (3, 0, 0, 0),
-   (4, 0, 1, 2), (3, 2, 2, 0), (4, 1, 0, 0), (0, 0, 0, 0), (4, 1, 2, 2), (4, 1, 3, 0), (3, 1, 0, 0), (4, 2, 0, 0), (0, 1, 0, 0), (4, 1, 1, 2),
-   (3, 2, 0, 0), (1, 1, 3, 0), (2, 3, 0, 0), (0, 2, 0, 0), (4, 0, 0, 2), (4, 3, 0, 0), (3, 3, 0, 0), (3, 0, 2, 1), (4, 4, 0, 0), (0, 3, 0, 0),
-   (4, 2, 2, 2), (4, 1, 0, 2), (4, 0, 3, 1), (2, 4, 0, 0), (4, 2, 0, 2), (0, 4, 0, 0), (4, 5, 0, 0), (2, 5, 0, 0), (4, 3, 0, 1), (4, 3, 0, 2),
-   (0, 5, 0, 0), (4, 0, 0, 1), (3, 4, 0, 0), (3, 5, 0, 0), (1, 0, 3, 1), (4, 0, 2, 3), (4, 1, 0, 1), (3, 3, 0, 1), (0, 0, 0, 1), (4, 4, 0, 1),
-   (3, 0, 0, 1), (4, 1, 3, 1), (4, 5, 0, 1), (4, 2, 0, 1), (0, 1, 0, 1), (4, 4, 0, 2), (3, 1, 0, 1), (3, 4, 0, 1), (1, 1, 3, 1), (4, 5, 0, 2),
-   (0, 2, 0, 1), (3, 5, 0, 1), (4, 3, 0, 3), (3, 2, 0, 1), (4, 0, 0, 3), (0, 1, 1, 0), (2, 2, 1, 0), (4, 2, 1, 0), (4, 1, 0, 3), (4, 4, 0, 3),
-   (3, 2, 1, 0), (4, 5, 0, 3), (0, 2, 1, 0), (4, 2, 0, 3), (4, 0, 1, 1), (3, 0, 1, 1), (4, 2, 1, 1), (3, 2, 1, 1)),
-  (), ((0, 0, 1, 1), (4, 1, 1, 1), (4, 2, 1, 2), (4, 0, 1, 3), (3, 1, 1, 1), (3, 1, 2, 1), (4, 2, 1, 3), (0, 1, 1, 1)), (), ((3, 2, 2, 1),),
-  ((4, 1, 1, 3), (3, 0, 3, 0)), ((4, 1, 2, 3),), ((4, 2, 2, 3), (3, 1, 3, 0)), ((3, 0, 3, 1),), ((4, 0, 3, 2),), ((4, 1, 3, 2), (3, 1, 3, 1)),
-  ((4, 0, 3, 3),), (), (), ((4, 1, 3, 3),), (), (), (), ()),
+SENDS_OUT = ((((0, 0, 0, 0), (0, 1, 0, 0), (3, 0, 0, 0), (3, 1, 0, 0), (3, 2, 0, 0)),
+  ((0, 2, 0, 0), (0, 3, 0, 0), (4, 0, 0, 2), (3, 3, 0, 0), (3, 4, 0, 0), (4, 1, 0, 2), (0, 4, 0, 0), (3, 5, 0, 0), (4, 2, 0, 2), (3, 6, 0, 0),
+   (0, 5, 0, 0), (4, 0, 1, 0), (2, 0, 0, 0), (2, 1, 0, 0), (0, 6, 0, 0), (2, 2, 0, 0), (4, 3, 0, 2), (2, 3, 0, 0), (4, 4, 0, 2), (2, 4, 0, 0),
+   (4, 5, 0, 2), (4, 1, 1, 0), (2, 5, 0, 0), (4, 6, 0, 2), (2, 6, 0, 0), (3, 0, 1, 0), (0, 0, 0, 1), (4, 0, 0, 1), (0, 1, 0, 1), (4, 1, 0, 1),
+   (3, 0, 0, 1), (0, 2, 0, 1), (4, 2, 0, 1), (4, 3, 0, 1), (3, 1, 0, 1), (4, 4, 0, 1), (3, 2, 0, 1), (4, 5, 0, 1), (4, 2, 1, 0), (3, 3, 0, 1),
+   (4, 6, 0, 1), (3, 4, 0, 1), (3, 5, 0, 1), (3, 6, 0, 1), (4, 0, 1, 2), (3, 1, 1, 0), (4, 0, 0, 3), (4, 0, 2, 0), (4, 1, 0, 3), (3, 0, 2, 0),
+   (4, 2, 0, 3), (4, 3, 0, 3), (4, 4, 0, 3), (4, 5, 0, 3), (2, 0, 2, 0), (4, 6, 0, 3), (4, 1, 2, 0), (4, 1, 1, 2), (3, 1, 2, 0)),
+  (), ((3, 0, 2, 1), (4, 0, 1, 1), (4, 0, 2, 2), (4, 0, 2, 1), (4, 1, 1, 1), (2, 1, 2, 0)), (), ((3, 2, 1, 0), (4, 1, 2, 2)),
+  ((4, 2, 1, 1), (3, 0, 1, 1), (3, 1, 1, 1), (4, 0, 2, 3), (4, 1, 2, 1)),
+  ((3, 1, 2, 1), (4, 2, 1, 2), (4, 0, 3, 0), (4, 0, 1, 3), (3, 2, 1, 1), (4, 1, 1, 3), (3, 0, 3, 0), (4, 1, 3, 0), (4, 1, 2, 3), (2, 1, 3, 0),
+   (4, 2, 1, 3), (3, 1, 3, 0), (4, 0, 3, 2), (4, 0, 3, 1), (3, 0, 3, 1)),
+  ((4, 1, 3, 1), (3, 1, 3, 1)), ((4, 1, 3, 2),), (), (), (), ((4, 0, 3, 3),), ((4, 1, 3, 3),), (), ()),
+ (((1, 0, 1, 0), (2, 0, 1, 0), (2, 1, 1, 0), (0, 0, 1, 0)),
+  ((1, 1, 1, 0), (2, 2, 1, 0), (0, 1, 1, 0), (3, 0, 1, 0), (4, 0, 0, 0), (4, 0, 1, 1), (1, 2, 1, 0), (0, 0, 0, 0), (3, 0, 0, 0), (4, 1, 0, 0),
+   (4, 1, 1, 1), (3, 1, 0, 0), (0, 1, 0, 0), (3, 1, 1, 0), (4, 0, 2, 0), (4, 2, 0, 0), (4, 2, 1, 1), (1, 0, 2, 0), (0, 2, 0, 0), (3, 2, 0, 0),
+   (4, 3, 0, 0), (2, 3, 0, 0), (4, 0, 1, 2), (0, 3, 0, 0), (4, 4, 0, 0), (4, 0, 0, 2), (2, 4, 0, 0), (3, 3, 0, 0), (4, 1, 0, 2), (0, 4, 0, 0),
+   (4, 5, 0, 0), (2, 5, 0, 0), (3, 4, 0, 0), (0, 5, 0, 0), (1, 1, 2, 0), (4, 6, 0, 0), (0, 6, 0, 0), (4, 2, 0, 2), (4, 1, 1, 2), (4, 3, 0, 1),
+   (2, 6, 0, 0), (4, 4, 0, 1), (0, 0, 0, 1), (4, 0, 0, 1), (4, 3, 0, 2), (3, 5, 0, 0), (4, 5, 0, 1), (4, 1, 0, 1), (0, 1, 0, 1), (4, 4, 0, 2),
+   (3, 6, 0, 0), (3, 3, 0, 1), (3, 4, 0, 1), (1, 0, 1, 1), (0, 2, 0, 1), (4, 2, 0, 1), (4, 0, 3, 0), (4, 6, 0, 1), (4, 5, 0, 2), (3, 0, 0, 1),
+   (3, 5, 0, 1), (3, 1, 0, 1), (3, 2, 0, 1), (4, 6, 0, 2), (0, 2, 1, 0), (1, 1, 1, 1), (4, 3, 0, 3), (3, 6, 0, 1), (4, 4, 0, 3), (2, 1, 3, 0),
+   (4, 1, 3, 0), (4, 1, 2, 0), (4, 0, 0, 3), (0, 0, 1, 1), (4, 5, 0, 3), (2, 0, 2, 0), (1, 2, 1, 1), (4, 1, 0, 3), (4, 2, 0, 3), (2, 1, 2, 0),
+   (4, 6, 0, 3), (0, 1, 1, 1), (1, 0, 3, 0), (4, 1, 3, 1), (3, 0, 2, 0)),
+  ((4, 0, 3, 1), (0, 2, 1, 1), (4, 0, 2, 1)), ((3, 1, 2, 0), (4, 1, 2, 1), (1, 1, 3, 0)), (), ((3, 0, 2, 1), (4, 0, 2, 2)),
+  ((1, 0, 3, 1), (3, 1, 2, 1), (4, 1, 2, 2)),
+  ((3, 2, 1, 0), (4, 0, 2, 3), (3, 0, 1, 1), (3, 1, 1, 1), (4, 1, 2, 3), (3, 2, 1, 1), (4, 2, 1, 2), (3, 0, 3, 0), (4, 0, 1, 3), (4, 1, 1, 3),
+   (3, 1, 3, 0), (4, 2, 1, 3), (3, 1, 3, 1), (3, 0, 3, 1), (4, 0, 3, 2)),
+  ((4, 1, 3, 2),), (), ((4, 1, 3, 3),), (), (), (), ((4, 0, 3, 3),), (), ()),
+ (((0, 0, 2, 0), (1, 0, 2, 0), (3, 0, 2, 0)),
+  ((3, 1, 2, 0), (0, 1, 2, 0), (1, 1, 2, 0), (2, 0, 2, 0), (4, 0, 2, 2), (2, 1, 2, 0), (4, 0, 1, 0), (0, 0, 1, 0), (4, 1, 2, 2), (4, 0, 3, 0),
+   (3, 0, 3, 0), (4, 1, 1, 0), (1, 0, 3, 0), (4, 0, 2, 1), (4, 0, 0, 0), (0, 0, 0, 0), (3, 0, 0, 0), (4, 1, 3, 0), (0, 1, 0, 0), (3, 1, 0, 0),
+   (4, 1, 2, 1), (4, 1, 0, 0), (3, 1, 3, 0), (4, 2, 0, 0), (0, 2, 0, 0), (1, 1, 3, 0), (3, 2, 0, 0), (0, 3, 0, 0), (4, 3, 0, 0), (3, 3, 0, 0),
+   (4, 0, 3, 2), (4, 4, 0, 0), (3, 4, 0, 0), (0, 4, 0, 0), (4, 0, 0, 2), (3, 5, 0, 0), (4, 5, 0, 0), (0, 5, 0, 0), (3, 0, 3, 1), (4, 0, 3, 1),
+   (4, 1, 0, 2), (0, 6, 0, 0), (4, 1, 3, 2), (4, 6, 0, 0), (1, 0, 3, 1), (4, 2, 0, 2), (0, 0, 0, 1), (4, 0, 0, 1), (3, 6, 0, 0), (4, 3, 0, 2),
+   (4, 4, 0, 2), (3, 0, 0, 1), (0, 1, 0, 1), (4, 1, 0, 1), (3, 1, 0, 1), (4, 5, 0, 2), (2, 3, 0, 0), (4, 2, 0, 1), (0, 2, 0, 1), (3, 2, 0, 1),
+   (2, 4, 0, 0), (0, 1, 1, 0), (4, 0, 3, 3), (2, 5, 0, 0), (4, 6, 0, 2), (2, 6, 0, 0), (3, 0, 2, 1), (4, 0, 0, 3), (4, 2, 1, 0), (4, 1, 0, 3),
+   (0, 2, 1, 0), (4, 3, 0, 1), (3, 3, 0, 1), (4, 2, 0, 3), (4, 4, 0, 1), (3, 4, 0, 1), (4, 5, 0, 1), (3, 5, 0, 1), (4, 0, 1, 1), (3, 6, 0, 1),
+   (4, 6, 0, 1), (3, 1, 2, 1), (0, 0, 1, 1), (4, 1, 1, 1), (4, 0, 2, 3), (4, 3, 0, 3), (3, 0, 1, 0), (4, 4, 0, 3), (0, 1, 1, 1), (4, 5, 0, 3),
+   (3, 1, 1, 0), (4, 6, 0, 3), (4, 2, 1, 1), (3, 2, 1, 0), (0, 2, 1, 1), (4, 1, 2, 3)),
+  ((3, 0, 1, 1),), ((4, 0, 1, 2), (4, 1, 1, 2), (3, 1, 1, 1), (4, 2, 1, 2), (3, 2, 1, 1)), (), ((4, 0, 1, 3), (2, 1, 3, 0)),
+  ((4, 1, 1, 3), (4, 2, 1, 3)), ((3, 1, 3, 1), (4, 1, 3, 1)), (), (), (), ((4, 1, 3, 3),), (), (), (), (), ()),
  (((2, 0, 3, 0), (1, 0, 3, 0)),
-  ((2, 1, 3, 0), (1, 1, 3, 0), (3, 0, 3, 0), (4, 0, 3, 1), (4, 0, 2, 0), (2, 0, 2, 0), (4, 1, 3, 1), (3, 0, 2, 0), (4, 1, 2, 0), (1, 0, 3, 1),
-   (2, 1, 2, 0), (4, 0, 3, 2), (3, 1, 2, 0), (4, 0, 2, 1), (4, 2, 2, 0), (2, 2, 2, 0), (4, 0, 2, 2), (1, 1, 3, 1), (4, 1, 2, 1), (3, 0, 2, 1),
-   (4, 0, 1, 0), (4, 1, 2, 2), (3, 0, 1, 0), (4, 0, 0, 0), (3, 0, 0, 0), (4, 2, 2, 1), (4, 1, 0, 0), (3, 1, 0, 0), (3, 2, 2, 0), (4, 0, 2, 3),
-   (4, 2, 0, 0), (4, 0, 1, 2), (3, 2, 0, 0), (4, 3, 0, 0), (4, 0, 0, 2), (2, 3, 0, 0), (4, 1, 0, 2), (3, 3, 0, 0), (4, 4, 0, 0), (2, 4, 0, 0),
-   (3, 4, 0, 0), (4, 2, 2, 2), (4, 5, 0, 0), (2, 5, 0, 0), (4, 2, 0, 2), (4, 3, 0, 1), (3, 5, 0, 0), (4, 0, 0, 1), (4, 3, 0, 2), (3, 3, 0, 1),
-   (4, 4, 0, 1), (3, 0, 0, 1), (4, 1, 0, 1), (4, 4, 0, 2), (3, 4, 0, 1), (4, 5, 0, 1), (4, 2, 0, 1), (3, 1, 0, 1), (3, 5, 0, 1), (4, 5, 0, 2),
-   (4, 3, 0, 3), (3, 2, 0, 1), (4, 0, 0, 3), (3, 1, 2, 1), (4, 1, 1, 0), (4, 4, 0, 3), (4, 1, 0, 3), (3, 1, 1, 0), (4, 5, 0, 3), (3, 2, 2, 1),
-   (4, 2, 0, 3), (4, 2, 1, 0), (4, 1, 2, 3), (2, 2, 1, 0)),
-  (), ((4, 1, 1, 2), (4, 0, 1, 1), (3, 2, 1, 0), (4, 2, 2, 3), (3, 0, 1, 1), (4, 2, 1, 1)), (), ((4, 1, 1, 1), (3, 2, 1, 1)),
-  ((4, 2, 1, 2), (3, 1, 1, 1)), ((4, 0, 1, 3), (3, 1, 3, 0)), ((4, 2, 1, 3),), ((4, 1, 1, 3), (3, 0, 3, 1)), ((3, 1, 3, 1),),
-  ((4, 1, 3, 2), (4, 0, 3, 3)), (), ((4, 1, 3, 3),), (), (), (), (), (), ()))
-SENDS_BACK = (((), ((0, 0, 3, 0),), (), ((1, 0, 3, 2), (1, 1, 3, 2)), ((1, 2, 3, 2),), ((1, 0, 3, 3),), ((0, 0, 2, 0), (3, 0, 3, 0)), ((1, 1, 3, 3), (3, 1, 3, 0)),
-  ((1, 2, 3, 3), (3, 2, 3, 0), (1, 0, 2, 2)), ((0, 0, 1, 0), (1, 1, 2, 2)), ((1, 2, 2, 2), (1, 3, 2, 2)), ((3, 0, 3, 1), (1, 4, 2, 2), (1, 0, 2, 3)),
-  ((3, 1, 3, 1), (1, 0, 1, 2)), ((1, 1, 1, 2),), ((3, 2, 3, 1), (1, 2, 1, 2), (1, 3, 1, 2), (1, 4, 1, 2)), ((1, 0, 1, 3),),
-  ((1, 1, 1, 3), (3, 0, 1, 0)), ((1, 2, 1, 3), (1, 3, 1, 3)), ((1, 4, 1, 3), (3, 1, 1, 0), (1, 1, 2, 3)), ((0, 0, 0, 0),), (),
-  ((5, 0, 0, 0), (1, 2, 2, 3)),
-  ((2, 2, 1, 1), (2, 3, 1, 1), (3, 0, 1, 1), (1, 0, 0, 2), (3, 1, 1, 1), (1, 1, 0, 2), (1, 2, 0, 2), (3, 0, 2, 0), (1, 3, 0, 2), (1, 4, 0, 2),
-   (1, 0, 0, 3), (3, 2, 1, 0), (1, 1, 0, 3), (5, 1, 0, 0), (3, 3, 1, 0), (1, 2, 0, 3), (1, 3, 0, 3), (3, 1, 2, 0), (1, 4, 0, 3), (2, 4, 1, 1),
-   (3, 0, 2, 1), (1, 3, 2, 3), (1, 4, 2, 3), (2, 2, 0, 1), (3, 1, 2, 1), (2, 3, 0, 1), (2, 4, 0, 1), (3, 4, 1, 0), (5, 2, 0, 0), (2, 2, 2, 1),
-   (2, 3, 2, 1), (2, 4, 2, 1), (3, 2, 2, 0), (3, 3, 2, 0), (3, 4, 2, 0), (2, 0, 0, 1), (2, 1, 0, 1), (4, 0, 0, 0), (4, 2, 0, 0), (4, 1, 0, 0),
-   (4, 3, 0, 0), (4, 4, 0, 0))),
- ((), ((0, 0, 3, 0),), (), ((1, 0, 3, 2), (1, 1, 3, 2)), ((1, 2, 3, 2),), ((1, 0, 3, 3),), ((0, 0, 2, 0),), ((1, 1, 3, 3),),
-  ((1, 2, 3, 3), (1, 0, 2, 2)), ((0, 0, 1, 0), (3, 0, 3, 0)), ((1, 1, 2, 2), (1, 2, 2, 2)), ((3, 1, 3, 0), (1, 3, 2, 2), (1, 4, 2, 2)),
-  ((1, 0, 1, 2), (1, 1, 1, 2)), ((3, 2, 3, 0), (1, 2, 1, 2), (1, 3, 1, 2)), ((1, 4, 1, 2),), ((3, 0, 3, 1), (1, 0, 1, 3), (1, 1, 1, 3)),
-  ((1, 2, 1, 3),), ((3, 1, 3, 1), (1, 3, 1, 3), (1, 4, 1, 3)), ((1, 0, 2, 3),), ((0, 0, 0, 0),), ((1, 1, 2, 3),), ((5, 0, 0, 0),),
-  ((3, 2, 3, 1), (2, 2, 1, 1), (1, 0, 0, 2), (1, 1, 0, 2), (1, 2, 0, 2), (1, 3, 0, 2), (1, 4, 0, 2), (1, 0, 0, 3), (1, 1, 0, 3), (1, 2, 0, 3),
-   (1, 3, 0, 3), (1, 4, 0, 3), (2, 3, 1, 1), (2, 4, 1, 1), (5, 1, 0, 0), (3, 0, 2, 0), (2, 0, 1, 1), (2, 2, 0, 1), (4, 2, 1, 0), (2, 3, 0, 1),
-   (2, 4, 0, 1), (2, 1, 1, 1), (3, 1, 2, 0), (1, 2, 2, 3), (4, 0, 1, 0), (3, 0, 0, 0), (1, 3, 2, 3), (1, 4, 2, 3), (3, 0, 2, 1), (3, 1, 0, 0),
-   (4, 1, 1, 0), (5, 2, 0, 0), (3, 1, 2, 1), (2, 2, 2, 1), (3, 0, 0, 1), (2, 3, 2, 1), (2, 4, 2, 1), (3, 1, 0, 1), (3, 2, 2, 0), (3, 2, 0, 0),
-   (3, 3, 2, 0), (3, 3, 0, 0), (3, 4, 2, 0), (3, 4, 0, 0), (4, 3, 1, 0), (4, 4, 1, 0))),
- ((), ((0, 0, 3, 0),), (), ((1, 0, 3, 2), (1, 1, 3, 2)), ((1, 2, 3, 2),), ((1, 0, 3, 3),), ((0, 0, 2, 0),), ((1, 1, 3, 3),),
-  ((1, 2, 3, 3), (1, 0, 2, 2)), ((0, 0, 1, 0),), ((1, 1, 2, 2), (1, 2, 2, 2)), ((1, 3, 2, 2), (1, 4, 2, 2)), ((1, 0, 2, 3), (3, 0, 3, 0)),
-  ((1, 0, 1, 2), (1, 1, 1, 2)), ((3, 1, 3, 0), (1, 2, 1, 2), (1, 3, 1, 2)), ((1, 4, 1, 2),), ((1, 0, 1, 3),),
-  ((3, 2, 3, 0), (1, 1, 1, 3), (1, 2, 1, 3)), ((1, 3, 1, 3),), ((0, 0, 0, 0), (1, 4, 1, 3)), (), ((5, 0, 0, 0), (3, 0, 3, 1), (1, 1, 2, 3)),
-  ((2, 2, 1, 1), (1, 0, 0, 2), (3, 0, 1, 0), (1, 1, 0, 2), (3, 1, 3, 1), (3, 1, 1, 0), (1, 2, 0, 2), (1, 3, 0, 2), (1, 4, 0, 2), (3, 0, 1, 1),
-   (1, 0, 0, 3), (3, 2, 3, 1), (1, 1, 0, 3), (3, 1, 1, 1), (1, 2, 0, 3), (5, 1, 0, 0), (1, 3, 0, 3), (1, 4, 0, 3), (2, 3, 1, 1), (3, 2, 1, 0),
-   (2, 4, 1, 1), (1, 2, 2, 3), (2, 2, 0, 1), (3, 0, 0, 0), (2, 3, 0, 1), (2, 4, 0, 1), (3, 1, 0, 0), (1, 3, 2, 3), (1, 4, 2, 3), (2, 2, 2, 1),
-   (3, 0, 0, 1), (5, 2, 0, 0), (3, 1, 0, 1), (2, 3, 2, 1), (2, 4, 2, 1), (3, 2, 0, 0), (3, 3, 0, 0), (2, 0, 2, 1), (3, 4, 0, 0), (2, 1, 2, 1),
-   (3, 3, 1, 0), (4, 0, 2, 0), (4, 1, 2, 0), (3, 4, 1, 0), (4, 2, 2, 0), (4, 3, 2, 0), (4, 4, 2, 0))),
- ((), ((0, 0, 3, 0),), (), ((1, 0, 3, 2), (1, 1, 3, 2)), ((1, 2, 3, 2),), ((1, 0, 3, 3),), ((0, 0, 2, 0),), ((1, 1, 3, 3),),
-  ((1, 2, 3, 3), (1, 0, 2, 2)), ((0, 0, 1, 0),), ((1, 1, 2, 2), (1, 2, 2, 2)), ((1, 3, 2, 2), (1, 4, 2, 2)), ((1, 0, 2, 3), (3, 0, 2, 0)),
-  ((1, 0, 1, 2), (1, 1, 1, 2), (3, 1, 2, 0)), ((1, 2, 1, 2), (1, 3, 1, 2)), ((1, 4, 1, 2), (3, 0, 2, 1), (1, 0, 1, 3)), ((3, 0, 1, 0), (1, 1, 1, 3)),
-  ((1, 2, 1, 3), (3, 1, 1, 0)), ((1, 3, 1, 3), (1, 4, 1, 3)), ((0, 0, 0, 0),), ((1, 1, 2, 3),), ((5, 0, 0, 0), (3, 0, 1, 1)),
-  ((2, 2, 1, 1), (3, 1, 1, 1), (1, 0, 0, 2), (1, 1, 0, 2), (1, 2, 0, 2), (1, 3, 0, 2), (3, 1, 2, 1), (1, 4, 0, 2), (3, 2, 1, 0), (1, 0, 0, 3),
-   (3, 0, 0, 0), (1, 1, 0, 3), (1, 2, 0, 3), (1, 3, 0, 3), (5, 1, 0, 0), (3, 1, 0, 0), (1, 4, 0, 3), (2, 0, 3, 1), (3, 0, 0, 1), (2, 1, 3, 1),
-   (2, 2, 0, 1), (3, 1, 0, 1), (2, 3, 0, 1), (2, 4, 0, 1), (4, 0, 3, 0), (2, 2, 3, 1), (4, 1, 3, 0), (2, 3, 1, 1), (3, 2, 0, 0), (2, 4, 1, 1),
-   (5, 2, 0, 0), (3, 3, 0, 0), (1, 2, 2, 3), (3, 4, 0, 0), (1, 3, 2, 3), (1, 4, 2, 3), (4, 2, 3, 0), (3, 3, 1, 0), (3, 4, 1, 0), (2, 2, 2, 1),
-   (2, 3, 2, 1), (2, 4, 2, 1), (3, 2, 2, 0), (3, 3, 2, 0), (3, 4, 2, 0))))
+  ((2, 1, 3, 0), (3, 0, 3, 0), (1, 1, 3, 0), (4, 0, 3, 1), (3, 1, 3, 0), (4, 0, 2, 0), (4, 1, 3, 1), (3, 0, 2, 0), (1, 0, 3, 1), (2, 0, 2, 0),
+   (4, 0, 3, 2), (4, 1, 2, 0), (4, 1, 3, 2), (3, 1, 2, 0), (4, 0, 2, 2), (4, 0, 1, 0), (3, 0, 1, 0), (4, 0, 0, 0), (3, 0, 0, 0), (4, 0, 2, 1),
+   (3, 0, 2, 1), (4, 1, 0, 0), (4, 1, 2, 2), (4, 2, 0, 0), (3, 1, 0, 0), (3, 2, 0, 0), (4, 0, 1, 2), (4, 3, 0, 0), (2, 3, 0, 0), (4, 0, 0, 2),
+   (4, 4, 0, 0), (2, 4, 0, 0), (3, 3, 0, 0), (4, 5, 0, 0), (2, 5, 0, 0), (3, 4, 0, 0), (4, 0, 2, 3), (4, 6, 0, 0), (4, 1, 0, 2), (2, 6, 0, 0),
+   (3, 5, 0, 0), (4, 2, 0, 2), (3, 6, 0, 0), (4, 0, 0, 1), (4, 3, 0, 1), (3, 0, 0, 1), (4, 4, 0, 1), (3, 3, 0, 1), (4, 1, 0, 1), (4, 3, 0, 2),
+   (4, 5, 0, 1), (3, 4, 0, 1), (4, 4, 0, 2), (3, 1, 0, 1), (4, 2, 0, 1), (4, 6, 0, 1), (3, 5, 0, 1), (4, 5, 0, 2), (3, 2, 0, 1), (3, 6, 0, 1),
+   (4, 6, 0, 2), (2, 1, 2, 0), (4, 0, 0, 3), (4, 1, 1, 0), (4, 3, 0, 3), (4, 4, 0, 3), (4, 1, 0, 3), (3, 1, 1, 0), (4, 5, 0, 3), (4, 2, 0, 3),
+   (4, 2, 1, 0), (3, 2, 1, 0), (4, 6, 0, 3), (3, 0, 3, 1), (4, 1, 2, 1), (4, 0, 1, 1)),
+  (), ((3, 0, 1, 1), (3, 1, 1, 1), (4, 1, 1, 2), (4, 2, 1, 2), (4, 1, 1, 1)), (),
+  ((3, 2, 1, 1), (4, 2, 1, 1), (4, 0, 3, 3), (4, 0, 1, 3), (3, 1, 2, 1)), ((4, 1, 1, 3), (3, 1, 3, 1)), ((4, 2, 1, 3), (4, 1, 2, 3), (4, 1, 3, 3)),
+  (), (), (), (), (), (), (), (), ()))
+SENDS_BACK = (((), (), (), ((1, 0, 3, 2),), ((1, 0, 3, 3),), ((1, 1, 3, 2),), (), (), ((3, 0, 3, 0), (1, 1, 3, 3)), (), ((1, 0, 1, 2), (3, 0, 3, 1)),
+  ((1, 0, 1, 3),), ((1, 1, 1, 2), (1, 1, 1, 3), (1, 2, 1, 2), (3, 1, 3, 0), (1, 2, 1, 3)), ((1, 0, 2, 2),), ((1, 0, 2, 3),),
+  ((3, 1, 3, 1), (1, 1, 2, 2)), (), (), ((5, 0, 0, 0), (1, 1, 2, 3)),
+  ((1, 2, 2, 2), (3, 0, 1, 0), (2, 0, 2, 1), (1, 2, 2, 3), (2, 1, 2, 1), (1, 0, 0, 2), (3, 0, 1, 1), (1, 0, 0, 3), (1, 1, 0, 2), (1, 1, 0, 3),
+   (2, 2, 2, 1), (1, 2, 0, 2), (1, 2, 0, 3), (1, 3, 0, 2), (5, 1, 0, 0), (3, 0, 2, 0), (1, 3, 0, 3), (1, 4, 0, 2), (1, 4, 0, 3), (1, 5, 0, 2),
+   (1, 5, 0, 3), (3, 1, 2, 0), (1, 6, 0, 2), (1, 6, 0, 3), (2, 1, 1, 1), (2, 3, 0, 1), (3, 2, 2, 0), (2, 2, 1, 1), (2, 4, 0, 1), (5, 2, 0, 0),
+   (2, 5, 0, 1), (2, 0, 0, 1), (2, 6, 0, 1), (3, 1, 1, 0), (3, 2, 1, 0), (2, 1, 0, 1), (4, 0, 0, 0), (2, 2, 0, 1), (4, 1, 0, 0), (4, 3, 0, 0),
+   (4, 4, 0, 0), (4, 2, 0, 0), (4, 5, 0, 0), (4, 6, 0, 0))),
+ ((), (), (), ((1, 0, 3, 2),), ((1, 0, 3, 3),), ((1, 1, 3, 2),), (), (), ((1, 1, 3, 3),), (), ((1, 0, 2, 2), (1, 0, 2, 3)),
+  ((1, 1, 2, 2), (1, 1, 2, 3)), ((3, 0, 3, 0), (2, 0, 2, 1), (1, 2, 2, 2)), (), ((3, 0, 3, 1), (2, 1, 2, 1), (1, 2, 2, 3)), (), (), ((1, 0, 1, 2),),
+  ((5, 0, 0, 0),),
+  ((1, 0, 0, 2), (3, 1, 3, 0), (1, 0, 0, 3), (2, 2, 2, 1), (1, 1, 0, 2), (1, 1, 0, 3), (1, 2, 0, 2), (3, 1, 3, 1), (1, 2, 0, 3), (1, 3, 0, 2),
+   (1, 3, 0, 3), (1, 4, 0, 2), (1, 4, 0, 3), (1, 5, 0, 2), (1, 5, 0, 3), (5, 1, 0, 0), (1, 6, 0, 2), (1, 6, 0, 3), (1, 0, 1, 3), (2, 3, 0, 1),
+   (2, 4, 0, 1), (2, 5, 0, 1), (3, 0, 0, 0), (2, 6, 0, 1), (1, 1, 1, 2), (3, 0, 0, 1), (1, 1, 1, 3), (1, 2, 1, 2), (3, 1, 0, 0), (2, 0, 1, 1),
+   (3, 0, 2, 0), (5, 2, 0, 0), (3, 1, 0, 1), (3, 2, 0, 0), (1, 2, 1, 3), (3, 1, 2, 0), (3, 2, 0, 1), (2, 1, 1, 1), (3, 3, 0, 0), (3, 4, 0, 0),
+   (3, 2, 2, 0), (4, 0, 1, 0), (3, 5, 0, 0), (2, 2, 1, 1), (3, 6, 0, 0), (4, 1, 1, 0), (4, 2, 1, 0))),
+ ((), (), (), ((1, 0, 3, 2),), ((1, 0, 3, 3),), ((1, 1, 3, 2),), (), (), ((1, 1, 3, 3),), (), ((1, 0, 1, 2),), ((1, 0, 1, 3),),
+  ((1, 1, 1, 2), (1, 1, 1, 3), (1, 2, 1, 2)), ((1, 2, 1, 3),), ((1, 0, 2, 2),), ((1, 0, 2, 3),), (), ((1, 1, 2, 2),), ((5, 0, 0, 0),),
+  ((1, 0, 0, 2), (1, 0, 0, 3), (1, 1, 0, 2), (3, 0, 1, 0), (1, 1, 0, 3), (3, 0, 3, 0), (1, 2, 0, 2), (1, 2, 0, 3), (1, 3, 0, 2), (1, 3, 0, 3),
+   (1, 4, 0, 2), (3, 0, 3, 1), (1, 4, 0, 3), (1, 5, 0, 2), (1, 5, 0, 3), (5, 1, 0, 0), (3, 0, 1, 1), (1, 6, 0, 2), (1, 6, 0, 3), (1, 1, 2, 3),
+   (3, 1, 3, 0), (1, 2, 2, 2), (3, 0, 0, 0), (1, 2, 2, 3), (3, 0, 0, 1), (2, 0, 2, 1), (3, 1, 3, 1), (3, 1, 0, 0), (2, 1, 2, 1), (3, 1, 0, 1),
+   (2, 3, 0, 1), (2, 4, 0, 1), (3, 2, 0, 0), (5, 2, 0, 0), (2, 2, 2, 1), (3, 2, 0, 1), (2, 5, 0, 1), (2, 6, 0, 1), (2, 1, 1, 1), (3, 3, 0, 0),
+   (2, 2, 1, 1), (3, 4, 0, 0), (3, 5, 0, 0), (3, 6, 0, 0), (3, 1, 1, 0), (3, 2, 1, 0), (4, 0, 2, 0), (4, 1, 2, 0), (4, 2, 2, 0))),
+ ((), (), (), ((1, 0, 3, 2),), ((1, 0, 3, 3),), ((1, 1, 3, 2),), (), (), ((1, 0, 2, 2), (1, 0, 2, 3)), (), ((1, 0, 1, 2),), ((1, 0, 1, 3),),
+  ((3, 0, 1, 0), (1, 1, 1, 2), (1, 1, 1, 3), (1, 2, 1, 2)), ((1, 2, 1, 3), (1, 1, 2, 2)), ((1, 1, 2, 3),), ((3, 0, 1, 1), (2, 1, 1, 1)),
+  ((1, 2, 2, 2),), (), ((5, 0, 0, 0),),
+  ((1, 0, 0, 2), (1, 0, 0, 3), (1, 1, 0, 2), (1, 1, 0, 3), (3, 1, 1, 0), (1, 2, 0, 2), (1, 2, 0, 3), (1, 3, 0, 2), (3, 0, 0, 0), (1, 3, 0, 3),
+   (3, 0, 0, 1), (1, 4, 0, 2), (1, 4, 0, 3), (3, 1, 0, 0), (5, 1, 0, 0), (1, 5, 0, 2), (1, 5, 0, 3), (1, 6, 0, 2), (3, 1, 0, 1), (1, 6, 0, 3),
+   (2, 2, 1, 1), (3, 2, 0, 0), (2, 3, 0, 1), (3, 2, 0, 1), (2, 4, 0, 1), (1, 2, 2, 3), (2, 5, 0, 1), (2, 6, 0, 1), (3, 2, 1, 0), (2, 0, 2, 1),
+   (5, 2, 0, 0), (3, 3, 0, 0), (2, 1, 2, 1), (3, 4, 0, 0), (2, 2, 2, 1), (3, 5, 0, 0), (3, 6, 0, 0), (1, 1, 3, 3), (3, 0, 2, 0), (2, 0, 3, 1),
+   (3, 1, 2, 0), (3, 2, 2, 0), (2, 1, 3, 1), (4, 0, 3, 0), (4, 1, 3, 0))))
 
 def unpack(flat_values):
     shapes = [(D, 3 * D), (D, D), (D, FF), (FF, D), (D, FINAL), (G * CD, V), (G * CD, FINAL)]

time: 199 us -> 191 us (0.960)
  Pallas kernels: 197 us -> 188 us
    pallas_call x1, Pallas kernels: 88.6 us -> 81.9 us  [forward(): pl.pallas_call(functools.partial(forward_kernel, pieces, events, weight),...]
where the time goes in v4:
time: 191 us
  Pallas kernels  188 us (98%)
  local copies, waits for them, and re-layouts  1.97 us (1%)
    pallas_call x1, Pallas kernels, backward(): pl.pallas_call(functools.partial(backward_kernel, pieces, events), out_sh...  100 us
    pallas_call x1, Pallas kernels, forward(): pl.pallas_call(functools.partial(forward_kernel, pieces, events, weight),...  81.9 us
    pallas_call x1, Pallas kernels, update(): pl.pallas_call(functools.partial(update_kernel, total), grid=(pl.cdiv(n,...  5.58 us

profile of v4, /device:TPU:0, one launch (start us, length us, event | category | flops | bytes accessed | tf_op | source)
XLA Modules:
  0.0 190.6 jit_solution(7881581017396878774)
XLA Ops:
  0.6 81.9 %shard_map.185 = (bf16[9664,768]{1,0:T(8,128)(2,1)}, bf16[768,256]{1,0:T(8,128)(2,1)}, bf16[448,768]{1,0:T(8,128)(2,1)}, bf16[512,256]{1,0:T(8,128)(2,1)}, f32[8...) custom-call(f32[1812,128]{1,0:T(8,128)} %bitcast.17, ...), custom_call_target="tpu_custom_call" | custom-call | tf_op jit(solution)/shard_map/pallas_call | solution.py:597
  82.5 100.5 %shard_map.186 = (f32[1812,128]{1,0:T(8,128)}, f32[78,128]{1,0:T(8,128)}, f32[8,128]{1,0:T(8,128)}, f32[1,472,768]{2,1,0:T(8,128)}) custom-call(f32[76,128]{1,0:T(8,128)} %bitcast.22, bf16[9664,768]{1,0:T(8,128)(2,1)} %get-tuple-element.43.rest_0_, bf16[768,256]{1,0:T(8,128)(2,1)} %get-tuple-element.44.rest_1_, bf16[448,768]{1,0:T(8,128)(2,1)} %get-tuple-element.45.rest_2_, ...), custom_call_target="tpu_custom_call" | custom-call | tf_op jit(solution)/shard_map/pallas_call | solution.py:922
  183.0 0.0 copy-start.1
  183.1 0.0 copy-start
  183.1 5.6 %shard_map.187 = (f32[1812,128]{1,0:T(8,128)}, bf16[1812,128]{1,0:T(8,128)(2,1)}, f32[1812,128]{1,0:T(8,128)}, f32[1812,128]{1,0:T(8,128)}, f32[76,128]{1,0:T(8,...) custom-call(f32[1812,128]{1,0:T(8,128)} %get-tuple-element.61.g, ...), custom_call_target="tpu_custom_call" | custom-call | tf_op jit(solution)/shard_map/pallas_call | solution.py:959
  188.7 0.0 copy-done.1
  188.7 0.9 copy.23
  189.5 0.0 copy-done
  189.5 1.1 copy.24
Async XLA Ops:
  183.0 5.6 %copy-start.1 = (bf16[1,472,768]{2,1,0:T(8,128)(2,1)S(1)}, bf16[1,472,768]{2,1,0:T(8,128)(2,1)}, u32[]{:S(2)}) copy-start(bf16[1,472,768]{2,1,0:T(8,128)(2,1)} %get-tuple-element.88) | copy-start | bytes 2174980
  183.1 6.5 %copy-start = (f32[1,472,768]{2,1,0:T(8,128)S(1)}, f32[1,472,768]{2,1,0:T(8,128)}, u32[]{:S(2)}) copy-start(f32[1,472,768]{2,1,0:T(8,128)} %get-tuple-element.89) | copy-start | bytes 4349956

commit v5 on v4

--- a/solution.py
+++ b/solution.py
@@ -407,48 +407,46 @@
     v = b[0] if len(b) == 1 else jnp.where(row < 12 - 4 * q, b[1], b[0])
     g[NROW + 16 * (4 * p + q):NROW + 16 * (4 * p + q) + 16, :] = v.astype(bf16)
 
+def wait_sent(g, rows, ssem, rsem, dev):
+    if rows:
+        ref = g.at[pl.ds(0, rows)]
+        remote(ref, ref, ssem, rsem, dev).wait_send()
+
 class Gather:
     def __init__(self, at, g, pieces, R, O, S):
         self.at, self.g, self.pieces, self.R, self.O, self.S = at, g, pieces, R, O, S
-        self.index = {}
-        self.made = {z: [] for z in range(PLANES)}
+        self.sent = {z: [0, 0] for z in range(PLANES)}
         self.seen = set()
 
-    def sem(self, key):
-        return self.S.at[self.index.setdefault(key, len(self.index))]
-
-    def copies(self, i, p, r, dev, kind, c):
+    def copies(self, i, p, r, dev, kind):
         _, first, rows, extra = self.pieces[p][i]
-        a, e = self.at.span(p, r, c, first)
+        a, e = self.at.span(p, r, self.at.c, first)
         unit = 4 * p + self.at.roles[r]
-        got = self.O if kind == CORE else self.R
         out = []
         for j, (s, n) in enumerate([(a, rows)] + [(e, EXTRA)] * extra):
             ref = self.g.at[pl.ds(s, n)]
-            out.append(remote(ref, ref, self.sem((HERE, j) if kind == HERE else (kind, i, p, r, j)), got.at[unit, i + j], dev))
+            out.append(remote(ref, ref, self.S.at[int(kind == CORE)], self.O.at[p] if kind == CORE else self.R.at[unit, i + j], dev))
         return out
 
     def op(self, zs, kind, i, p, r):
         at = self.at
         if not (p == zs and r == 0) and (zs, i, p, r) not in self.seen:
             self.seen.add((zs, i, p, r))
-            for q in self.copies(i, p, r, (zs, at.fc), HERE, at.c): q.wait_recv()
+            for q in self.copies(i, p, r, (zs, at.fc), HERE): q.wait_recv()
         dev = ((zs + 1, at.f), (zs - 1, at.f), (zs, at.uf), (zs, at.vf), (zs, at.fc))[kind]
-        for q in self.copies(i, p, r, dev, kind, at.c): q.start()
-        self.made[zs].append((kind, i, p, r))
+        for q in self.copies(i, p, r, dev, kind): q.start()
+        _, _, rows, extra = self.pieces[p][i]
+        self.sent[zs][int(kind == CORE)] += rows + EXTRA * extra
 
     def other_core(self, zs, p):
-        for r in range(4):
-            if p == zs and r == 0: continue
-            for i in range(len(self.pieces[p])):
-                for q in self.copies(i, p, r, (zs, self.at.fc), CORE, 1 - self.at.c): q.wait_recv()
+        ref = self.g.at[pl.ds(0, HALF * (3 if p == zs else 4))]
+        remote(ref, ref, self.S.at[1], self.O.at[p], (zs, self.at.fc)).wait_recv()
 
     def drain(self):
         for zs in range(PLANES):
             @pl.when(self.at.z == zs)
             def _():
-                for kind, i, p, r in self.made[zs]:
-                    for q in self.copies(i, p, r, (zs, self.at.fc), kind, self.at.c): q.wait_send()
+                for i in range(2): wait_sent(self.g, self.sent[zs][i], self.S.at[i], self.O.at[0], (zs, self.at.fc))
 
 def own_rows(at, g, p_ref, raw, sem):
     n = p_ref.shape[0]
@@ -592,7 +590,6 @@
     sds = jax.ShapeDtypeStruct
     n = params.shape[0] // 128
     most = max(len(ps) for ps in pieces) + 1
-    keys = len({e + (j,) for z in events for s in z for e in s for j in range(1 + pieces[e[2]][e[1]][3])})
     here = [VM(*K1_SHAPE[k]) for k in K1_OUT[1:-1]] + [VM((4 * T, T), bf16)]
     outs = pl.pallas_call(functools.partial(forward_kernel, pieces, events, weight),
         out_shape=[sds(*K1_SHAPE[k]) for k in K1_OUT] + [sds((1, LEN, D), bf16)],
@@ -601,29 +598,25 @@
             + [VM((T, D), bf16), VM((T, D), bf16), VM((D, T), bf16), VM((T, FF), bf16), VM((LT, D), f32), VM((LT, D), f32), VM((T, D), bf16), VM((T, D), bf16),
                VM((256, T), bf16), VM((T, 256), bf16), VM((256, 256), f32), VM((2, 256, 384), f32), VM((1152, 128), f32), VM((2, 768, 128), f32), VM((3, 256, 128), f32),
                VM((256, 384), bf16), VM((256, 256), bf16),
-               DMA((3,)), DMA((16, most)), DMA((16, most)), DMA((keys + 2,)), DMA((24,)), DMA((2,))],
+               DMA((3,)), DMA((16, most)), DMA((PLANES,)), DMA((2,)), DMA((24,)), DMA((2,))],
         compiler_params=pltpu.CompilerParams(collective_id=0, has_side_effects=True, vmem_limit_bytes=63 * 2**20),
     )(params.reshape(n, 128), x, mask, jnp.transpose(dis, (2, 0, 1)), jnp.swapaxes(cho, 1, 2), vec.reshape(-1, 128))
     return dict(zip(K1_OUT, outs)), outs[-1]
 TO_CORE, TO_V, TO_U, TO_Z, KEEP, SMALL = range(6)
 
 class Reduce:
-    def __init__(self, at, g, pieces, LD, LV, LZ, LU, total, RD, RV, RZ, RU, S, SD):
+    def __init__(self, at, g, pieces, LD, LV, LZ, LU, total, RD, RV, RZ, RU, S):
         self.at, self.g, self.pieces, self.total = at, g, pieces, total
         self.LD, self.LV, self.LZ, self.LU = LD, LV, LZ, LU
-        self.RD, self.RV, self.RZ, self.RU, self.S, self.SD = RD, RV, RZ, RU, S, SD
-        self.index = {}
-        self.made = {z: [] for z in range(PLANES)}
+        self.RD, self.RV, self.RZ, self.RU, self.S = RD, RV, RZ, RU, S
+        self.sent = {z: 0 for z in range(PLANES)}
         self.seen = set()
 
-    def sem(self, key):
-        return self.S.at[self.index.setdefault(key, len(self.index))]
-
-    def copies(self, key, p, r, c, first, rows, extra, land, got, dev):
+    def copies(self, p, r, c, first, rows, extra, land, got, dev):
         a, e = self.at.span(p, r, c, first)
         out = []
         for j, (s, n, to) in enumerate([(a, rows, first)] + [(e, EXTRA, MAIN)] * extra):
-            out.append(remote(self.g.at[pl.ds(s, n)], land.at[pl.ds(to, n)], self.sem(key + (j,)), got.at[j], dev))
+            out.append(remote(self.g.at[pl.ds(s, n)], land.at[pl.ds(to, n)], self.S.at[0], got.at[j], dev))
         return out
 
     def build(self, zs, op):
@@ -633,13 +626,13 @@
         _, first, rows, extra = self.pieces[p][i]
         if kind == TO_V:
             n = 2 * p + r - 2
-            return self.copies(op, p, r, at.c, first, rows, extra, self.LV.at[n], self.RV.at[n, i], (zs, at.vf))
+            return self.copies(p, r, at.c, first, rows, extra, self.LV.at[n], self.RV.at[n, i], (zs, at.vf))
         if kind == TO_U:
-            return self.copies(op, p, r, at.c, first, rows, extra, self.LU.at[p], self.RU.at[p, i], (zs, at.uf))
+            return self.copies(p, r, at.c, first, rows, extra, self.LU.at[p], self.RU.at[p, i], (zs, at.uf))
         up = p > zs
         to = zs + 1 if up else zs - 1
         n = 8 + r if (not up and to == p) else 2 * p + r
-        return self.copies(op, p, r, at.c, first, rows, extra, self.LZ.at[n], self.RZ.at[n, i], (to, at.f))
+        return self.copies(p, r, at.c, first, rows, extra, self.LZ.at[n], self.RZ.at[n, i], (to, at.f))
 
     def once(self, zs, key, cs):
         if (zs, key) not in self.seen:
@@ -648,7 +641,8 @@
 
     def send(self, zs, op):
         for q in self.build(zs, op): q.start()
-        self.made[zs].append(op)
+        _, _, rows, extra = self.pieces[op[2]][op[1]]
+        self.sent[zs] += rows + EXTRA * extra
 
     def add(self, p, r, first, rows, extra, lands, final):
         a, e = self.at.span(p, r, self.at.c, first)
@@ -671,17 +665,17 @@
         at = self.at
         kind, i, p, r = op
         unit = 4 * p + at.roles[r]
-        self.once(zs, (TO_CORE, p, r), self.copies((HERE,), p, r, at.c, 0, MAIN, True, self.LD.at[unit], self.RD.at[unit], (zs, at.fc)))
+        self.once(zs, (TO_CORE, p, r), self.copies(p, r, at.c, 0, MAIN, True, self.LD.at[unit], self.RD.at[unit], (zs, at.fc)))
         path, first, rows, extra = self.pieces[p][i]
         if kind == TO_V:
             self.add(p, r, first, rows, extra, [self.LD.at[unit]], False)
             self.send(zs, op)
             return
         n = 2 * p + r
-        self.once(zs, ("v", i, p, r), self.copies((HERE,), p, r, at.c, first, rows, extra, self.LV.at[n], self.RV.at[n, i], (zs, at.fc)))
+        self.once(zs, ("v", i, p, r), self.copies(p, r, at.c, first, rows, extra, self.LV.at[n], self.RV.at[n, i], (zs, at.fc)))
         lands = [self.LD.at[unit], self.LV.at[n]]
         def arrived(land, got, key):
-            self.once(zs, key, self.copies((HERE,), p, r, at.c, first, rows, extra, land, got, (zs, at.fc)))
+            self.once(zs, key, self.copies(p, r, at.c, first, rows, extra, land, got, (zs, at.fc)))
             lands.append(land)
         if path == 0 or r == 0:
             if p >= zs and zs > 0: arrived(self.LZ.at[n], self.RZ.at[n, i], (UP, i, p, r))
@@ -697,7 +691,7 @@
         a, e = self.at.span_of(p, kk, 1 - self.at.c, 0)
         land = self.LD.at[4 * p + kk]
         dev = (self.at.z, self.at.fc)
-        return [remote(self.g.at[pl.ds(s, n)], land.at[pl.ds(to, n)], self.SD.at[4 * p + kk, j], self.RD.at[4 * p + kk, j], dev)
+        return [remote(self.g.at[pl.ds(s, n)], land.at[pl.ds(to, n)], self.S.at[1], self.RD.at[4 * p + kk, j], dev)
                 for j, (s, n, to) in enumerate(((a, MAIN, 0), (e, EXTRA, MAIN)))]
 
     def to_core(self, p, kk):
@@ -707,12 +701,8 @@
     def drain(self):
         for zs in range(PLANES):
             @pl.when(self.at.z == zs)
-            def _():
-                for op in self.made[zs]:
-                    for q in self.build(zs, op): q.wait_send()
-        for p in range(PLANES):
-            for kk in range(4):
-                for q in self.core_copies(p, kk): q.wait_send()
+            def _(): wait_sent(self.g, self.sent[zs], self.S.at[0], self.RD.at[0, 0], (zs, self.at.fc))
+        wait_sent(self.g, 4 * PLANES * HALF, self.S.at[1], self.RD.at[0, 0], (self.at.z, self.at.fc))
 
 class Spread:
     def __init__(self, at, own, land, zland, S, count):
@@ -753,7 +743,7 @@
     hbm = dict(zip(K2_IN, rest[:n_in]))
     (grad, vsum, sq, ig_out, ig, g, vec, wproj, dctx, small, hat1, r1, hat2, r2, gp, ring, normT, attT, q, kT, vv, xT, wq,
      low1, low2, acc, tmp, dp, LD, LV, LZ, LU, total, flat, vg, vland, vzland, sqv, sland, szland,
-     IS, RD, RV, RZ, RU, S, SD, TS, TL, VS, SS) = rest[n_in:]
+     IS, RD, RV, RZ, RU, S, TS, TL, VS, SS) = rest[n_in:]
     here = dict(wproj=wproj, dctx=dctx, small=small, hat1=hat1, r1=r1, hat2=hat2, r2=r2, gp=gp, normT=normT, attT=attT, q=q, kT=kT, vv=vv, xT=xT)
     loads = {}
     def load(name, src=None, dst=None):
@@ -779,7 +769,7 @@
         for cp in cs: cp.wait()
     at = Place()
     at.greet_all(vland.shape[0])
-    re = Reduce(at, g, pieces, LD, LV, LZ, LU, total, RD, RV, RZ, RU, S, SD)
+    re = Reduce(at, g, pieces, LD, LV, LZ, LU, total, RD, RV, RZ, RU, S)
     vs = Spread(at, vg, vland, vzland, VS, vland.shape[0])
     ss = Spread(at, sqv, sland, szland, SS, vland.shape[0])
     def slot(i, cond=None):
@@ -904,10 +894,10 @@
     ss.second()
     for j in range(6):
         grad[pl.ds(j, n, stride=6), :] = flat[pl.ds(6 * (16 - 2 * c - 4 * k) + j, n, stride=6), :]
+    re.drain()
     ss.last()
     sq[...] = sqv[...]
     put_ig.wait()
-    re.drain()
 
 def backward(pieces, events, vec, hbm, count, n):
     V_ = pl.BlockSpec(memory_space=pltpu.VMEM)
@@ -916,7 +906,6 @@
     DMA = pltpu.SemaphoreType.DMA
     sds = jax.ShapeDtypeStruct
     most = max(len(ps) for ps in pieces)
-    keys = len({e + (j,) for z in events for s in z for e in s if e[0] in (TO_V, TO_U, TO_Z) for j in range(1 + pieces[e[2]][e[1]][3])})
     nv = vec.shape[0] + 256
     shape = dict(K1_SHAPE, ring=((FF, T), bf16), wq=((3 * D, D), bf16))
     return pl.pallas_call(functools.partial(backward_kernel, pieces, events),
@@ -926,7 +915,7 @@
             + [VM((T, D), bf16), VM((T, D), bf16), VM((24, D), f32), VM((2, 1024, 128), f32), VM((3, T, D), bf16),
                VM((16, HALF, D), bf16), VM((8, HALF, D), bf16), VM((10, HALF, D), bf16), VM((4, HALF, D), bf16), VM((HALF + 16, D), f32), VM((6 * (HALF + 16), 128), f32),
                VM((1, nv), f32), VM((count, 1, nv), f32), VM((PLANES, 1, nv), f32), VM((8, 128), f32), VM((count, 8, 128), f32), VM((PLANES, 8, 128), f32),
-               DMA((24,)), DMA((16, 2)), DMA((8, most, 2)), DMA((10, most, 2)), DMA((4, most, 2)), DMA((keys + 2,)), DMA((16, 2)), DMA((8,)), DMA((12,)), DMA((2, count + PLANES)), DMA((2, count + PLANES))],
+               DMA((24,)), DMA((16, 2)), DMA((8, most, 2)), DMA((10, most, 2)), DMA((4, most, 2)), DMA((2,)), DMA((8,)), DMA((12,)), DMA((2, count + PLANES)), DMA((2, count + PLANES))],
         compiler_params=pltpu.CompilerParams(collective_id=1, has_side_effects=True, vmem_limit_bytes=63 * 2**20),
     )(vec.reshape(-1, 128), *[hbm[k] for k in K2_IN])
 

time: 191 us -> 187 us (0.979)
  Pallas kernels: 188 us -> 184 us
    pallas_call x1, Pallas kernels: 81.9 us -> 79.1 us  [forward(): pl.pallas_call(functools.partial(forward_kernel, pieces, events, weight),...]
where the time goes in v5:
time: 187 us; the launch traced here: 186 us
  Pallas kernels  184 us (98%)
  local copies, waits for them, and re-layouts  1.97 us (1%)
    pallas_call x1, Pallas kernels, backward(): pl.pallas_call(functools.partial(backward_kernel, pieces, events), out_sh...  98.8 us
    pallas_call x1, Pallas kernels, forward(): pl.pallas_call(functools.partial(forward_kernel, pieces, events, weight),...  79.1 us
    pallas_call x1, Pallas kernels, update(): pl.pallas_call(functools.partial(update_kernel, total), grid=(pl.cdiv(n,...  5.58 us

profile of v5, /device:TPU:0, one launch (start us, length us, event | category | flops | bytes accessed | tf_op | source)
XLA Modules:
  0.0 186.2 jit_solution(14016735920951968230)
XLA Ops:
  0.6 79.1 %shard_map.185 = (bf16[9664,768]{1,0:T(8,128)(2,1)}, bf16[768,256]{1,0:T(8,128)(2,1)}, bf16[448,768]{1,0:T(8,128)(2,1)}, bf16[512,256]{1,0:T(8,128)(2,1)}, f32[8...) custom-call(f32[1812,128]{1,0:T(8,128)} %bitcast.17, ...), custom_call_target="tpu_custom_call" | custom-call | tf_op jit(solution)/shard_map/pallas_call | solution.py:594
  79.8 98.8 %shard_map.186 = (f32[1812,128]{1,0:T(8,128)}, f32[78,128]{1,0:T(8,128)}, f32[8,128]{1,0:T(8,128)}, f32[1,472,768]{2,1,0:T(8,128)}) custom-call(f32[76,128]{1,0:T(8,128)} %bitcast.22, bf16[9664,768]{1,0:T(8,128)(2,1)} %get-tuple-element.43.rest_0_, bf16[768,256]{1,0:T(8,128)(2,1)} %get-tuple-element.44.rest_1_, bf16[448,768]{1,0:T(8,128)(2,1)} %get-tuple-element.45.rest_2_, ...), custom_call_target="tpu_custom_call" | custom-call | tf_op jit(solution)/shard_map/pallas_call | solution.py:911
  178.6 0.0 copy-start.1
  178.6 0.0 copy-start
  178.6 5.6 %shard_map.187 = (f32[1812,128]{1,0:T(8,128)}, bf16[1812,128]{1,0:T(8,128)(2,1)}, f32[1812,128]{1,0:T(8,128)}, f32[1812,128]{1,0:T(8,128)}, f32[76,128]{1,0:T(8,...) custom-call(f32[1812,128]{1,0:T(8,128)} %get-tuple-element.61.g, ...), custom_call_target="tpu_custom_call" | custom-call | tf_op jit(solution)/shard_map/pallas_call | solution.py:948
  184.2 0.0 copy-done.1
  184.2 0.9 copy.23
  185.1 0.0 copy-done
  185.1 1.1 copy.24
Async XLA Ops:
  178.6 5.6 %copy-start.1 = (bf16[1,472,768]{2,1,0:T(8,128)(2,1)S(1)}, bf16[1,472,768]{2,1,0:T(8,128)(2,1)}, u32[]{:S(2)}) copy-start(bf16[1,472,768]{2,1,0:T(8,128)(2,1)} %get-tuple-element.88) | copy-start | bytes 2174980
  178.6 6.5 %copy-start = (f32[1,472,768]{2,1,0:T(8,128)S(1)}, f32[1,472,768]{2,1,0:T(8,128)}, u32[]{:S(2)}) copy-start(f32[1,472,768]{2,1,0:T(8,128)} %get-tuple-element.89) | copy-start | bytes 4349956

commit v6 on v5

--- a/solution.py
+++ b/solution.py
@@ -287,16 +287,18 @@
         v = v + mm_nt(dh[0:LT, c * D:(c + 1) * D], w)
     dr[:, cols] = v
 
+WEAVE = 384
+
 def weave(lhsT, rhs, parts, n, base, gg, tmp, stacked):
     def body(m, _):
         cols = pl.ds(pl.multiple_of(m * 256, 256), 256)
         for t in range(parts):
             r = rhs[t, :, cols] if stacked else rhs[:, pl.ds(pl.multiple_of(t * D + m * 256, 256), 256)]
-            acc = mm(lhsT[pl.ds(pl.multiple_of(n * 256, 256), 256), :], r)
+            acc = mm(lhsT[pl.ds(pl.multiple_of(n * WEAVE, WEAVE), WEAVE), :], r)
             for j in range(2):
-                tmp[j, pl.ds(t, 256, stride=parts), :] = acc[:, 128 * j:128 * j + 128]
+                tmp[j, pl.ds(t, WEAVE, stride=parts), :] = acc[:, 128 * j:128 * j + 128]
         for j in range(2):
-            gg[pl.ds(pl.multiple_of(base + n * 256 * parts, 256), 256 * parts), pl.ds(pl.multiple_of(m * 256 + 128 * j, 128), 128)] = tmp[j, 0:256 * parts, :].astype(bf16)
+            gg[pl.ds(pl.multiple_of(base + n * WEAVE * parts, 128), WEAVE * parts), pl.ds(pl.multiple_of(m * 256 + 128 * j, 128), 128)] = tmp[j, 0:WEAVE * parts, :].astype(bf16)
         return 0
     lax.fori_loop(0, 3, body, 0)
 
@@ -333,14 +335,14 @@
     dp[2, 0:LT, pl.ds(at, 128)] = dv.astype(bf16)
     dp[0, :, pl.ds(at, 128)] = dqT[pl.ds(at, 128), :].T
 
-def input_back(n, dp, wq, dr, out):
+def input_back(n, dp, wq, dr):
     cols = slice(256 * n, 256 * n + 256)
     v = dr[:, cols]
     for t in range(3):
         v = v + mm_nt(dp[t, 0:LT, :], wq[t * D + 256 * n:t * D + 256 * n + 256, :])
-    out[0, :, cols] = v[0:LEN]
+    dr[:, cols] = v
 MESH = pl.DeviceIdType.MESH
-UP, DOWN, U, V_AXIS, CORE, HERE = range(6)
+UP, DOWN, U, V_AXIS, CORE = range(5)
 PLANES = 4
 MAIN = 288
 EXTRA = 16
@@ -423,20 +425,22 @@
         a, e = self.at.span(p, r, self.at.c, first)
         unit = 4 * p + self.at.roles[r]
         out = []
-        for j, (s, n) in enumerate([(a, rows)] + [(e, EXTRA)] * extra):
+        for s, n in [(a, rows)] + [(e, EXTRA)] * extra:
             ref = self.g.at[pl.ds(s, n)]
-            out.append(remote(ref, ref, self.S.at[int(kind == CORE)], self.O.at[p] if kind == CORE else self.R.at[unit, i + j], dev))
+            out.append(remote(ref, ref, self.S.at[int(kind == CORE)], self.O.at[p] if kind == CORE else self.R.at[unit, i], dev))
         return out
 
     def op(self, zs, kind, i, p, r):
         at = self.at
+        _, _, rows, extra = self.pieces[p][i]
+        rows += EXTRA * extra
         if not (p == zs and r == 0) and (zs, i, p, r) not in self.seen:
             self.seen.add((zs, i, p, r))
-            for q in self.copies(i, p, r, (zs, at.fc), HERE): q.wait_recv()
+            ref = self.g.at[pl.ds(0, rows)]
+            remote(ref, ref, self.S.at[0], self.R.at[4 * p + at.roles[r], i], (zs, at.fc)).wait_recv()
         dev = ((zs + 1, at.f), (zs - 1, at.f), (zs, at.uf), (zs, at.vf), (zs, at.fc))[kind]
         for q in self.copies(i, p, r, dev, kind): q.start()
-        _, _, rows, extra = self.pieces[p][i]
-        self.sent[zs][int(kind == CORE)] += rows + EXTRA * extra
+        self.sent[zs][int(kind == CORE)] += rows
 
     def other_core(self, zs, p):
         ref = self.g.at[pl.ds(0, HALF * (3 if p == zs else 4))]
@@ -589,7 +593,7 @@
     DMA = pltpu.SemaphoreType.DMA
     sds = jax.ShapeDtypeStruct
     n = params.shape[0] // 128
-    most = max(len(ps) for ps in pieces) + 1
+    most = max(len(ps) for ps in pieces)
     here = [VM(*K1_SHAPE[k]) for k in K1_OUT[1:-1]] + [VM((4 * T, T), bf16)]
     outs = pl.pallas_call(functools.partial(forward_kernel, pieces, events, weight),
         out_shape=[sds(*K1_SHAPE[k]) for k in K1_OUT] + [sds((1, LEN, D), bf16)],
@@ -615,8 +619,8 @@
     def copies(self, p, r, c, first, rows, extra, land, got, dev):
         a, e = self.at.span(p, r, c, first)
         out = []
-        for j, (s, n, to) in enumerate([(a, rows, first)] + [(e, EXTRA, MAIN)] * extra):
-            out.append(remote(self.g.at[pl.ds(s, n)], land.at[pl.ds(to, n)], self.S.at[0], got.at[j], dev))
+        for s, n, to in [(a, rows, first)] + [(e, EXTRA, MAIN)] * extra:
+            out.append(remote(self.g.at[pl.ds(s, n)], land.at[pl.ds(to, n)], self.S.at[0], got, dev))
         return out
 
     def build(self, zs, op):
@@ -634,10 +638,11 @@
         n = 8 + r if (not up and to == p) else 2 * p + r
         return self.copies(p, r, at.c, first, rows, extra, self.LZ.at[n], self.RZ.at[n, i], (to, at.f))
 
-    def once(self, zs, key, cs):
+    def once(self, zs, key, rows, got):
         if (zs, key) not in self.seen:
             self.seen.add((zs, key))
-            for q in cs: q.wait_recv()
+            ref = self.g.at[pl.ds(0, rows)]
+            remote(ref, ref, self.S.at[0], got, (zs, self.at.fc)).wait_recv()
 
     def send(self, zs, op):
         for q in self.build(zs, op): q.start()
@@ -665,17 +670,17 @@
         at = self.at
         kind, i, p, r = op
         unit = 4 * p + at.roles[r]
-        self.once(zs, (TO_CORE, p, r), self.copies(p, r, at.c, 0, MAIN, True, self.LD.at[unit], self.RD.at[unit], (zs, at.fc)))
+        self.once(zs, (TO_CORE, p, r), HALF, self.RD.at[unit])
         path, first, rows, extra = self.pieces[p][i]
         if kind == TO_V:
             self.add(p, r, first, rows, extra, [self.LD.at[unit]], False)
             self.send(zs, op)
             return
         n = 2 * p + r
-        self.once(zs, ("v", i, p, r), self.copies(p, r, at.c, first, rows, extra, self.LV.at[n], self.RV.at[n, i], (zs, at.fc)))
+        self.once(zs, ("v", i, p, r), rows + EXTRA * extra, self.RV.at[n, i])
         lands = [self.LD.at[unit], self.LV.at[n]]
         def arrived(land, got, key):
-            self.once(zs, key, self.copies(p, r, at.c, first, rows, extra, land, got, (zs, at.fc)))
+            self.once(zs, key, rows + EXTRA * extra, got)
             lands.append(land)
         if path == 0 or r == 0:
             if p >= zs and zs > 0: arrived(self.LZ.at[n], self.RZ.at[n, i], (UP, i, p, r))
@@ -691,8 +696,8 @@
         a, e = self.at.span_of(p, kk, 1 - self.at.c, 0)
         land = self.LD.at[4 * p + kk]
         dev = (self.at.z, self.at.fc)
-        return [remote(self.g.at[pl.ds(s, n)], land.at[pl.ds(to, n)], self.S.at[1], self.RD.at[4 * p + kk, j], dev)
-                for j, (s, n, to) in enumerate(((a, MAIN, 0), (e, EXTRA, MAIN)))]
+        return [remote(self.g.at[pl.ds(s, n)], land.at[pl.ds(to, n)], self.S.at[1], self.RD.at[4 * p + kk], dev)
+                for s, n, to in ((a, MAIN, 0), (e, EXTRA, MAIN))]
 
     def to_core(self, p, kk):
         extra_rows(self.g, p, kk)
@@ -701,8 +706,8 @@
     def drain(self):
         for zs in range(PLANES):
             @pl.when(self.at.z == zs)
-            def _(): wait_sent(self.g, self.sent[zs], self.S.at[0], self.RD.at[0, 0], (zs, self.at.fc))
-        wait_sent(self.g, 4 * PLANES * HALF, self.S.at[1], self.RD.at[0, 0], (self.at.z, self.at.fc))
+            def _(): wait_sent(self.g, self.sent[zs], self.S.at[0], self.RD.at[0], (zs, self.at.fc))
+        wait_sent(self.g, 4 * PLANES * HALF, self.S.at[1], self.RD.at[0], (self.at.z, self.at.fc))
 
 class Spread:
     def __init__(self, at, own, land, zland, S, count):
@@ -741,7 +746,7 @@
 def backward_kernel(pieces, events, vec_ref, *rest):
     n_in = len(K2_IN)
     hbm = dict(zip(K2_IN, rest[:n_in]))
-    (grad, vsum, sq, ig_out, ig, g, vec, wproj, dctx, small, hat1, r1, hat2, r2, gp, ring, normT, attT, q, kT, vv, xT, wq,
+    (grad, vsum, sq, ig_out, g, vec, wproj, dctx, small, hat1, r1, hat2, r2, gp, ring, normT, attT, q, kT, vv, xT, wq,
      low1, low2, acc, tmp, dp, LD, LV, LZ, LU, total, flat, vg, vland, vzland, sqv, sland, szland,
      IS, RD, RV, RZ, RU, S, TS, TL, VS, SS) = rest[n_in:]
     here = dict(wproj=wproj, dctx=dctx, small=small, hat1=hat1, r1=r1, hat2=hat2, r2=r2, gp=gp, normT=normT, attT=attT, q=q, kT=kT, vv=vv, xT=xT)
@@ -812,15 +817,10 @@
     ready(third)
     lax.fori_loop(0, 3, lambda n, _: (up_back_x(n, gp, g, hat2), 0)[1], 0)
     slot(3)
-    def woven(n, _):
-        weave(normT, gp, 4, 2 - n, 3072, g, tmp, False)
-        for kk in range(4):
-            @pl.when(n == int(kk == 0))
-            def _(): re.to_core(2, kk)
-        slot(4, n == 0)
-        slot(5, n == 1)
-        return 0
-    lax.fori_loop(0, 2, woven, 0)
+    weave(normT, gp, 4, 1, 3072, g, tmp, False)
+    for kk in (3, 2, 1, 0): re.to_core(2, kk)
+    slot(4)
+    slot(5)
     slot(6)
     weave(normT, gp, 4, 0, 3072, g, tmp, False)
     re.to_core(1, 2)
@@ -855,11 +855,12 @@
     def wove(n, _):
         weave(xT, dp, 3, n, 0, g, tmp, True)
         for kk in range(4):
-            @pl.when(n == min(kk, 2))
+            @pl.when(n == min(kk, 1))
             def _(): re.to_core(0, kk)
-        for i in range(3): slot(13 + i, n == i)
+        for i in range(2): slot(13 + i, n == i)
         return 0
-    lax.fori_loop(0, 3, wove, 0)
+    lax.fori_loop(0, 2, wove, 0)
+    slot(15)
     slot(16)
     vg[0:1, BQ:BQ + D] = jnp.sum(dp[0].astype(f32), axis=0, keepdims=True)
     vg[0:1, BV:BV + D] = jnp.sum(dp[2].astype(f32), axis=0, keepdims=True)
@@ -869,8 +870,8 @@
     slot(17)
     slot(18)
     for n in range(3):
-        input_back(n, dp, wq, hat1, ig)
-    put_ig = pltpu.make_async_copy(ig, ig_out, IS.at[len(loads)])
+        input_back(n, dp, wq, hat1)
+    put_ig = pltpu.make_async_copy(hat1.at[pl.ds(0, LEN)], ig_out.at[0], IS.at[len(loads)])
     put_ig.start()
     slot(19)
     z, c, k = at.z, at.c, at.k
@@ -911,11 +912,11 @@
     return pl.pallas_call(functools.partial(backward_kernel, pieces, events),
         out_shape=[sds((n, 128), f32), sds((nv // 128, 128), f32), sds((8, 128), f32), sds((1, LEN, D), f32)],
         in_specs=[V_] + [A_] * len(K2_IN), out_specs=[V_] * 3 + [A_],
-        scratch_shapes=[VM((1, LEN, D), f32), VM((GROW, D), bf16), VM((1, vec.shape[0]), f32)] + [VM(*shape[k]) for k in K2_HERE]
-            + [VM((T, D), bf16), VM((T, D), bf16), VM((24, D), f32), VM((2, 1024, 128), f32), VM((3, T, D), bf16),
+        scratch_shapes=[VM((GROW, D), bf16), VM((1, vec.shape[0]), f32)] + [VM(*shape[k]) for k in K2_HERE]
+            + [VM((T, D), bf16), VM((T, D), bf16), VM((24, D), f32), VM((2, 4 * WEAVE, 128), f32), VM((3, T, D), bf16),
                VM((16, HALF, D), bf16), VM((8, HALF, D), bf16), VM((10, HALF, D), bf16), VM((4, HALF, D), bf16), VM((HALF + 16, D), f32), VM((6 * (HALF + 16), 128), f32),
                VM((1, nv), f32), VM((count, 1, nv), f32), VM((PLANES, 1, nv), f32), VM((8, 128), f32), VM((count, 8, 128), f32), VM((PLANES, 8, 128), f32),
-               DMA((24,)), DMA((16, 2)), DMA((8, most, 2)), DMA((10, most, 2)), DMA((4, most, 2)), DMA((2,)), DMA((8,)), DMA((12,)), DMA((2, count + PLANES)), DMA((2, count + PLANES))],
+               DMA((24,)), DMA((16,)), DMA((8, most)), DMA((10, most)), DMA((4, most)), DMA((2,)), DMA((8,)), DMA((12,)), DMA((2, count + PLANES)), DMA((2, count + PLANES))],
         compiler_params=pltpu.CompilerParams(collective_id=1, has_side_effects=True, vmem_limit_bytes=63 * 2**20),
     )(vec.reshape(-1, 128), *[hbm[k] for k in K2_IN])
 
@@ -1010,32 +1011,32 @@
   (), ((3, 0, 1, 1), (3, 1, 1, 1), (4, 1, 1, 2), (4, 2, 1, 2), (4, 1, 1, 1)), (),
   ((3, 2, 1, 1), (4, 2, 1, 1), (4, 0, 3, 3), (4, 0, 1, 3), (3, 1, 2, 1)), ((4, 1, 1, 3), (3, 1, 3, 1)), ((4, 2, 1, 3), (4, 1, 2, 3), (4, 1, 3, 3)),
   (), (), (), (), (), (), (), (), ()))
-SENDS_BACK = (((), (), (), ((1, 0, 3, 2),), ((1, 0, 3, 3),), ((1, 1, 3, 2),), (), (), ((3, 0, 3, 0), (1, 1, 3, 3)), (), ((1, 0, 1, 2), (3, 0, 3, 1)),
-  ((1, 0, 1, 3),), ((1, 1, 1, 2), (1, 1, 1, 3), (1, 2, 1, 2), (3, 1, 3, 0), (1, 2, 1, 3)), ((1, 0, 2, 2),), ((1, 0, 2, 3),),
-  ((3, 1, 3, 1), (1, 1, 2, 2)), (), (), ((5, 0, 0, 0), (1, 1, 2, 3)),
+SENDS_BACK = (((), (), (), ((1, 0, 3, 2),), ((1, 0, 3, 3),), (), (), ((1, 1, 3, 2),), ((3, 0, 3, 0), (1, 1, 3, 3)), (), ((1, 0, 1, 2), (3, 0, 3, 1)),
+  ((1, 0, 1, 3),), ((1, 1, 1, 2), (1, 1, 1, 3), (1, 2, 1, 2), (3, 1, 3, 0), (1, 2, 1, 3)), ((1, 0, 2, 2),),
+  ((3, 1, 3, 1), (1, 0, 2, 3), (1, 1, 2, 2)), (), (), (), ((5, 0, 0, 0), (1, 1, 2, 3)),
   ((1, 2, 2, 2), (3, 0, 1, 0), (2, 0, 2, 1), (1, 2, 2, 3), (2, 1, 2, 1), (1, 0, 0, 2), (3, 0, 1, 1), (1, 0, 0, 3), (1, 1, 0, 2), (1, 1, 0, 3),
    (2, 2, 2, 1), (1, 2, 0, 2), (1, 2, 0, 3), (1, 3, 0, 2), (5, 1, 0, 0), (3, 0, 2, 0), (1, 3, 0, 3), (1, 4, 0, 2), (1, 4, 0, 3), (1, 5, 0, 2),
    (1, 5, 0, 3), (3, 1, 2, 0), (1, 6, 0, 2), (1, 6, 0, 3), (2, 1, 1, 1), (2, 3, 0, 1), (3, 2, 2, 0), (2, 2, 1, 1), (2, 4, 0, 1), (5, 2, 0, 0),
    (2, 5, 0, 1), (2, 0, 0, 1), (2, 6, 0, 1), (3, 1, 1, 0), (3, 2, 1, 0), (2, 1, 0, 1), (4, 0, 0, 0), (2, 2, 0, 1), (4, 1, 0, 0), (4, 3, 0, 0),
    (4, 4, 0, 0), (4, 2, 0, 0), (4, 5, 0, 0), (4, 6, 0, 0))),
- ((), (), (), ((1, 0, 3, 2),), ((1, 0, 3, 3),), ((1, 1, 3, 2),), (), (), ((1, 1, 3, 3),), (), ((1, 0, 2, 2), (1, 0, 2, 3)),
-  ((1, 1, 2, 2), (1, 1, 2, 3)), ((3, 0, 3, 0), (2, 0, 2, 1), (1, 2, 2, 2)), (), ((3, 0, 3, 1), (2, 1, 2, 1), (1, 2, 2, 3)), (), (), ((1, 0, 1, 2),),
-  ((5, 0, 0, 0),),
+ ((), (), (), ((1, 0, 3, 2),), ((1, 0, 3, 3),), (), (), ((1, 1, 3, 2),), ((1, 1, 3, 3),), (), ((1, 0, 2, 2), (1, 0, 2, 3)),
+  ((1, 1, 2, 2), (1, 1, 2, 3)), ((3, 0, 3, 0), (2, 0, 2, 1), (1, 2, 2, 2)), ((2, 1, 2, 1),), ((3, 0, 3, 1), (1, 2, 2, 3)), (), (), (),
+  ((5, 0, 0, 0), (1, 0, 1, 2)),
   ((1, 0, 0, 2), (3, 1, 3, 0), (1, 0, 0, 3), (2, 2, 2, 1), (1, 1, 0, 2), (1, 1, 0, 3), (1, 2, 0, 2), (3, 1, 3, 1), (1, 2, 0, 3), (1, 3, 0, 2),
    (1, 3, 0, 3), (1, 4, 0, 2), (1, 4, 0, 3), (1, 5, 0, 2), (1, 5, 0, 3), (5, 1, 0, 0), (1, 6, 0, 2), (1, 6, 0, 3), (1, 0, 1, 3), (2, 3, 0, 1),
    (2, 4, 0, 1), (2, 5, 0, 1), (3, 0, 0, 0), (2, 6, 0, 1), (1, 1, 1, 2), (3, 0, 0, 1), (1, 1, 1, 3), (1, 2, 1, 2), (3, 1, 0, 0), (2, 0, 1, 1),
    (3, 0, 2, 0), (5, 2, 0, 0), (3, 1, 0, 1), (3, 2, 0, 0), (1, 2, 1, 3), (3, 1, 2, 0), (3, 2, 0, 1), (2, 1, 1, 1), (3, 3, 0, 0), (3, 4, 0, 0),
    (3, 2, 2, 0), (4, 0, 1, 0), (3, 5, 0, 0), (2, 2, 1, 1), (3, 6, 0, 0), (4, 1, 1, 0), (4, 2, 1, 0))),
- ((), (), (), ((1, 0, 3, 2),), ((1, 0, 3, 3),), ((1, 1, 3, 2),), (), (), ((1, 1, 3, 3),), (), ((1, 0, 1, 2),), ((1, 0, 1, 3),),
-  ((1, 1, 1, 2), (1, 1, 1, 3), (1, 2, 1, 2)), ((1, 2, 1, 3),), ((1, 0, 2, 2),), ((1, 0, 2, 3),), (), ((1, 1, 2, 2),), ((5, 0, 0, 0),),
-  ((1, 0, 0, 2), (1, 0, 0, 3), (1, 1, 0, 2), (3, 0, 1, 0), (1, 1, 0, 3), (3, 0, 3, 0), (1, 2, 0, 2), (1, 2, 0, 3), (1, 3, 0, 2), (1, 3, 0, 3),
-   (1, 4, 0, 2), (3, 0, 3, 1), (1, 4, 0, 3), (1, 5, 0, 2), (1, 5, 0, 3), (5, 1, 0, 0), (3, 0, 1, 1), (1, 6, 0, 2), (1, 6, 0, 3), (1, 1, 2, 3),
+ ((), (), (), ((1, 0, 3, 2),), ((1, 0, 3, 3),), (), (), ((1, 1, 3, 2),), ((1, 1, 3, 3),), (), ((1, 0, 1, 2),), ((1, 0, 1, 3),),
+  ((1, 1, 1, 2), (1, 1, 1, 3), (1, 2, 1, 2)), ((1, 2, 1, 3), (1, 0, 2, 2)), ((1, 0, 2, 3),), (), (), (), ((5, 0, 0, 0), (1, 1, 2, 2)),
+  ((1, 0, 0, 2), (1, 0, 0, 3), (3, 0, 3, 0), (1, 1, 0, 2), (3, 0, 1, 0), (1, 1, 0, 3), (1, 2, 0, 2), (1, 2, 0, 3), (1, 3, 0, 2), (3, 0, 3, 1),
+   (1, 3, 0, 3), (1, 4, 0, 2), (1, 4, 0, 3), (1, 5, 0, 2), (1, 5, 0, 3), (5, 1, 0, 0), (3, 0, 1, 1), (1, 6, 0, 2), (1, 6, 0, 3), (1, 1, 2, 3),
    (3, 1, 3, 0), (1, 2, 2, 2), (3, 0, 0, 0), (1, 2, 2, 3), (3, 0, 0, 1), (2, 0, 2, 1), (3, 1, 3, 1), (3, 1, 0, 0), (2, 1, 2, 1), (3, 1, 0, 1),
    (2, 3, 0, 1), (2, 4, 0, 1), (3, 2, 0, 0), (5, 2, 0, 0), (2, 2, 2, 1), (3, 2, 0, 1), (2, 5, 0, 1), (2, 6, 0, 1), (2, 1, 1, 1), (3, 3, 0, 0),
    (2, 2, 1, 1), (3, 4, 0, 0), (3, 5, 0, 0), (3, 6, 0, 0), (3, 1, 1, 0), (3, 2, 1, 0), (4, 0, 2, 0), (4, 1, 2, 0), (4, 2, 2, 0))),
- ((), (), (), ((1, 0, 3, 2),), ((1, 0, 3, 3),), ((1, 1, 3, 2),), (), (), ((1, 0, 2, 2), (1, 0, 2, 3)), (), ((1, 0, 1, 2),), ((1, 0, 1, 3),),
-  ((3, 0, 1, 0), (1, 1, 1, 2), (1, 1, 1, 3), (1, 2, 1, 2)), ((1, 2, 1, 3), (1, 1, 2, 2)), ((1, 1, 2, 3),), ((3, 0, 1, 1), (2, 1, 1, 1)),
-  ((1, 2, 2, 2),), (), ((5, 0, 0, 0),),
+ ((), (), (), ((1, 0, 3, 2),), ((1, 0, 3, 3),), (), (), ((1, 1, 3, 2),), ((1, 0, 2, 2),), ((1, 0, 2, 3),), ((1, 0, 1, 2),), ((1, 0, 1, 3),),
+  ((3, 0, 1, 0), (1, 1, 1, 2), (1, 1, 1, 3), (1, 2, 1, 2)), ((1, 2, 1, 3), (1, 1, 2, 2)), ((3, 0, 1, 1), (2, 1, 1, 1), (1, 1, 2, 3)), (), (),
+  ((1, 2, 2, 2),), ((5, 0, 0, 0),),
   ((1, 0, 0, 2), (1, 0, 0, 3), (1, 1, 0, 2), (1, 1, 0, 3), (3, 1, 1, 0), (1, 2, 0, 2), (1, 2, 0, 3), (1, 3, 0, 2), (3, 0, 0, 0), (1, 3, 0, 3),
    (3, 0, 0, 1), (1, 4, 0, 2), (1, 4, 0, 3), (3, 1, 0, 0), (5, 1, 0, 0), (1, 5, 0, 2), (1, 5, 0, 3), (1, 6, 0, 2), (3, 1, 0, 1), (1, 6, 0, 3),
    (2, 2, 1, 1), (3, 2, 0, 0), (2, 3, 0, 1), (3, 2, 0, 1), (2, 4, 0, 1), (1, 2, 2, 3), (2, 5, 0, 1), (2, 6, 0, 1), (3, 2, 1, 0), (2, 0, 2, 1),

time: 187 us -> 184 us (0.984)
  Pallas kernels: 184 us -> 181 us
    pallas_call x1, Pallas kernels: 98.8 us -> 96.3 us  [backward(): pl.pallas_call(functools.partial(backward_kernel, pieces, events), out_sh...]
where the time goes in v6:
time: 184 us
  Pallas kernels  181 us (98%)
  local copies, waits for them, and re-layouts  1.97 us (1%)
    pallas_call x1, Pallas kernels, backward(): pl.pallas_call(functools.partial(backward_kernel, pieces, events), out_sh...  96.3 us
    pallas_call x1, Pallas kernels, forward(): pl.pallas_call(functools.partial(forward_kernel, pieces, events, weight),...  79 us
    pallas_call x1, Pallas kernels, update(): pl.pallas_call(functools.partial(update_kernel, total), grid=(pl.cdiv(n,...  5.58 us

profile of v6, /device:TPU:0, one launch (start us, length us, event | category | flops | bytes accessed | tf_op | source)
XLA Modules:
  0.0 183.6 jit_solution(2023923448745457166)
XLA Ops:
  0.6 79.0 %shard_map.185 = (bf16[9664,768]{1,0:T(8,128)(2,1)}, bf16[768,256]{1,0:T(8,128)(2,1)}, bf16[448,768]{1,0:T(8,128)(2,1)}, bf16[512,256]{1,0:T(8,128)(2,1)}, f32[8...) custom-call(f32[1812,128]{1,0:T(8,128)} %bitcast.17, ...), custom_call_target="tpu_custom_call" | custom-call | tf_op jit(solution)/shard_map/pallas_call | solution.py:598
  79.6 96.3 %shard_map.186 = (f32[1812,128]{1,0:T(8,128)}, f32[78,128]{1,0:T(8,128)}, f32[8,128]{1,0:T(8,128)}, f32[1,472,768]{2,1,0:T(8,128)}) custom-call(f32[76,128]{1,0:T(8,128)} %bitcast.22, bf16[9664,768]{1,0:T(8,128)(2,1)} %get-tuple-element.43.rest_0_, bf16[768,256]{1,0:T(8,128)(2,1)} %get-tuple-element.44.rest_1_, bf16[448,768]{1,0:T(8,128)(2,1)} %get-tuple-element.45.rest_2_, ...), custom_call_target="tpu_custom_call" | custom-call | tf_op jit(solution)/shard_map/pallas_call | solution.py:912
  176.0 0.0 copy-start.1
  176.0 0.0 copy-start
  176.0 5.6 %shard_map.187 = (f32[1812,128]{1,0:T(8,128)}, bf16[1812,128]{1,0:T(8,128)(2,1)}, f32[1812,128]{1,0:T(8,128)}, f32[1812,128]{1,0:T(8,128)}, f32[76,128]{1,0:T(8,...) custom-call(f32[1812,128]{1,0:T(8,128)} %get-tuple-element.61.g, ...), custom_call_target="tpu_custom_call" | custom-call | tf_op jit(solution)/shard_map/pallas_call | solution.py:949
  181.6 0.0 copy-done.1
  181.6 0.9 copy.23
  182.5 0.0 copy-done
  182.5 1.1 copy.24
Async XLA Ops:
  176.0 5.6 %copy-start.1 = (bf16[1,472,768]{2,1,0:T(8,128)(2,1)S(1)}, bf16[1,472,768]{2,1,0:T(8,128)(2,1)}, u32[]{:S(2)}) copy-start(bf16[1,472,768]{2,1,0:T(8,128)(2,1)} %get-tuple-element.88) | copy-start | bytes 2174980
  176.0 6.5 %copy-start = (f32[1,472,768]{2,1,0:T(8,128)S(1)}, f32[1,472,768]{2,1,0:T(8,128)}, u32[]{:S(2)}) copy-start(f32[1,472,768]{2,1,0:T(8,128)} %get-tuple-element.89) | copy-start | bytes 4349956

commit v7 on v6

--- a/solution.py
+++ b/solution.py
@@ -942,7 +942,7 @@
 def update(total, g, p, m1, m2, vg, v, v1, v2, sq):
     n, nv = g.shape[0], v.shape[0] // 128
     sds = jax.ShapeDtypeStruct
-    rows = 608
+    rows = 464
     part = pl.BlockSpec((rows, 128), lambda i: (i, 0))
     def whole(*shape): return pl.BlockSpec(shape, lambda i: (0, 0))
     flat = lambda a: a.reshape(-1, 128)

time: 184 us -> 184 us (level)
  no operation moved by 1% of the time
where the time goes in v7:
time: 184 us
  Pallas kernels  181 us (98%)
  local copies, waits for them, and re-layouts  1.97 us (1%)
    pallas_call x1, Pallas kernels, backward(): pl.pallas_call(functools.partial(backward_kernel, pieces, events), out_sh...  96.3 us
    pallas_call x1, Pallas kernels, forward(): pl.pallas_call(functools.partial(forward_kernel, pieces, events, weight),...  79 us
    pallas_call x1, Pallas kernels, update(): pl.pallas_call(functools.partial(update_kernel, total), grid=(pl.cdiv(n,...  5.56 us

profile of v7, /device:TPU:0, one launch (start us, length us, event | category | flops | bytes accessed | tf_op | source)
XLA Modules:
  0.0 183.6 jit_solution(9819523153282682343)
XLA Ops:
  0.6 79.0 %shard_map.185 = (bf16[9664,768]{1,0:T(8,128)(2,1)}, bf16[768,256]{1,0:T(8,128)(2,1)}, bf16[448,768]{1,0:T(8,128)(2,1)}, bf16[512,256]{1,0:T(8,128)(2,1)}, f32[8...) custom-call(f32[1812,128]{1,0:T(8,128)} %bitcast.17, ...), custom_call_target="tpu_custom_call" | custom-call | tf_op jit(solution)/shard_map/pallas_call | solution.py:598
  79.6 96.3 %shard_map.186 = (f32[1812,128]{1,0:T(8,128)}, f32[78,128]{1,0:T(8,128)}, f32[8,128]{1,0:T(8,128)}, f32[1,472,768]{2,1,0:T(8,128)}) custom-call(f32[76,128]{1,0:T(8,128)} %bitcast.22, bf16[9664,768]{1,0:T(8,128)(2,1)} %get-tuple-element.43.rest_0_, bf16[768,256]{1,0:T(8,128)(2,1)} %get-tuple-element.44.rest_1_, bf16[448,768]{1,0:T(8,128)(2,1)} %get-tuple-element.45.rest_2_, ...), custom_call_target="tpu_custom_call" | custom-call | tf_op jit(solution)/shard_map/pallas_call | solution.py:912
  176.0 0.0 copy-start.1
  176.0 0.0 copy-start
  176.0 5.6 %shard_map.187 = (f32[1812,128]{1,0:T(8,128)}, bf16[1812,128]{1,0:T(8,128)(2,1)}, f32[1812,128]{1,0:T(8,128)}, f32[1812,128]{1,0:T(8,128)}, f32[76,128]{1,0:T(8,...) custom-call(f32[1812,128]{1,0:T(8,128)} %get-tuple-element.61.g, ...), custom_call_target="tpu_custom_call" | custom-call | tf_op jit(solution)/shard_map/pallas_call | solution.py:949
  181.6 0.0 copy-done.1
  181.6 0.9 copy.23
  182.5 0.0 copy-done
  182.5 1.1 copy.24
Async XLA Ops:
  176.0 5.6 %copy-start.1 = (bf16[1,472,768]{2,1,0:T(8,128)(2,1)S(1)}, bf16[1,472,768]{2,1,0:T(8,128)(2,1)}, u32[]{:S(2)}) copy-start(bf16[1,472,768]{2,1,0:T(8,128)(2,1)} %get-tuple-element.88) | copy-start | bytes 2174980
  176.0 6.5 %copy-start = (f32[1,472,768]{2,1,0:T(8,128)S(1)}, f32[1,472,768]{2,1,0:T(8,128)}, u32[]{:S(2)}) copy-start(f32[1,472,768]{2,1,0:T(8,128)} %get-tuple-element.89) | copy-start | bytes 4349956
